TPU v7x, 128 devices: a whole 4x4x4 slice. The times are simulated.
128 devices in a mesh: row: 4 (over y), col: 8 (over z, core), depth: 4 (over x).
Axes of the slice: x: 4, y: 4, z: 4, core: 2. Of those that a mesh axis runs over, the one named last changes fastest.
Arguments:
- stacked_signals: bfloat16 [1024, 512, 256], P('depth', ('row', 'col')), may hold values from -6 to 6
- presence_indicator: bfloat16 [1024, 512], P('depth', ('row', 'col')), may hold values from 0 to 1, as said below
- normalizer_multiplier: float32 [256], replicated, may hold values from 0.5 to 1.5
- normalizer_shift: float32 [256], replicated, may hold values from -3 to 3
- leading_linear_map: bfloat16 [256, 32], replicated, may hold values from -0.375 to 0.375
- first_projection_offset: float32 [32], replicated, may hold values from -3 to 3
- trailing_linear_map: bfloat16 [256, 32], replicated, may hold values from -0.375 to 0.375
- second_projection_offset: float32 [32], replicated, may hold values from -3 to 3
- final_projection_matrix: bfloat16 [1024, 128], replicated, may hold values from -0.1875 to 0.1875
Outputs:
- pair_update: bfloat16 [512, 512, 128], P(('row', 'depth'), 'col')
Inputs may be any that keep to these rules, and one draw needn't show every extreme that they name: `presence_indicator`: 0 marks a residue absent from a sequence; some residues are absent from every sequence.
All inputs are finite; a program needn't handle non-finite values.
Results may differ from a plain program's by a relative error of at most 0.0036.
Values may be sent and summed in bfloat16 or wider, within the bound.
No kernel may reach another device: no remote copies, remote signals or barrier semaphores. Data moves between devices by JAX's collectives and lax.ppermute only.
A program may use at most 64 MiB of HBM per device.

v0:
```python
import math

import jax
import jax.numpy as jnp
from jax import lax
from jax.sharding import PartitionSpec as P


def panel(normed, weight, bias, mask_floating):
    homolog_lines, residues, feature_depth = normed.shape
    flat = jnp.dot(
        normed.reshape(homolog_lines * residues, feature_depth),
        weight,
        preferred_element_type=jnp.float32,
    )
    flat = flat + bias
    return (flat.reshape(homolog_lines, residues, -1) * mask_floating[:, :, None]).astype(
        jnp.bfloat16
    )


def per_device(
    stacked_signals,
    presence_indicator,
    normalizer_multiplier,
    normalizer_shift,
    leading_linear_map,
    first_projection_offset,
    trailing_linear_map,
    second_projection_offset,
    final_projection_matrix,
):
    homolog_lines, positions_owned, feature_depth = stacked_signals.shape
    chans = leading_linear_map.shape[1]
    pair_chans = final_projection_matrix.shape[1]
    n_row = lax.axis_size("row")
    n_col = lax.axis_size("col")
    tile_i = positions_owned * n_col
    tile_j = positions_owned * n_row
    mask_floating = presence_indicator.astype(jnp.float32)
    element_count = stacked_signals.astype(jnp.float32)
    center = element_count - jnp.mean(element_count, axis=-1, keepdims=True)
    spread = jnp.mean(center * center, axis=-1, keepdims=True)
    normed = (center * lax.rsqrt(spread + 1e-05) * normalizer_multiplier + normalizer_shift).astype(
        jnp.bfloat16
    )
    left = panel(normed, leading_linear_map, first_projection_offset, mask_floating).reshape(
        homolog_lines, positions_owned * chans
    )
    right = panel(normed, trailing_linear_map, second_projection_offset, mask_floating).reshape(
        homolog_lines, positions_owned * chans
    )
    left_tile, mask_rows = (
        lax.all_gather(left, "col", axis=1, tiled=True),
        lax.all_gather(presence_indicator, "col", axis=1, tiled=True),
    )
    right_every, mask_every = (
        lax.all_gather(right, ("row", "col"), axis=1, tiled=True),
        lax.all_gather(presence_indicator, ("row", "col"), axis=1, tiled=True),
    )
    start_j = lax.axis_index("col") * tile_j
    right_tile = lax.dynamic_slice_in_dim(right_every, start_j * chans, tile_j * chans, 1)
    mask_cols = lax.dynamic_slice_in_dim(mask_every, start_j, tile_j, 1)
    weight3 = final_projection_matrix.reshape(chans, chans, pair_chans)
    block = math.gcd(tile_i, 32)
    left_blocks = jnp.moveaxis(
        left_tile.reshape(homolog_lines, tile_i // block, block, chans), 1, 0
    )
    right_cube = right_tile.reshape(homolog_lines, tile_j, chans)

    def one_block(lblock):
        outer = jnp.einsum("sic,sjd->icjd", lblock, right_cube, preferred_element_type=jnp.float32)
        outer = outer.astype(jnp.bfloat16)
        return jnp.einsum("icjd,cde->ije", outer, weight3, preferred_element_type=jnp.float32)

    partial_tile = lax.map(one_block, left_blocks).reshape(tile_i, tile_j, pair_chans)
    count_part = jnp.dot(mask_rows.T, mask_cols, preferred_element_type=jnp.float32)
    slab, count = (
        lax.psum_scatter(partial_tile, "depth", scatter_dimension=0, tiled=True),
        lax.psum_scatter(count_part, "depth", scatter_dimension=0, tiled=True),
    )
    return (slab / jnp.maximum(count, 1.0)[:, :, None]).astype(jnp.bfloat16)


def solution(mesh):
    return jax.shard_map(
        per_device,
        mesh=mesh,
        in_specs=(
            P("depth", ("row", "col"), None),
            P("depth", ("row", "col")),
            P(),
            P(),
            P(),
            P(),
            P(),
            P(),
            P(),
        ),
        out_specs=P(("row", "depth"), "col", None),
        check_vma=False,
    )
```

profile of v0, /device:TPU:1, one launch (start us, length us, event | category | flops | bytes accessed | tf_op | source)
XLA Modules:
  0.0 183.9 jit_solution(12865743325525091595)
XLA Ops:
  7.4 0.0 copy-start
  7.4 0.0 copy-start.1
  7.4 0.0 copy-start.8
  7.4 0.0 copy-start.7
  7.4 0.0 all-gather.3.cloned.1.call-start
  7.4 2.4 %convert_reduce_fusion = f32[256,16]{1,0:T(8,128)S(1)} fusion(bf16[256,16,256]{2,1,0:T(8,128)(2,1)} %param.11), kind=kLoop, calls=%fused_computation.11 | loop fusion | flops 2093056 | bytes 2113536 | tf_op jit(solution)/shard_map/reduce_sum | solution.py:42
  9.8 0.0 copy-start.9
  9.8 2.5 %fusion.21 = f32[256,16]{1,0:T(8,128)S(1)} fusion(bf16[256,16,256]{2,1,0:T(8,128)(2,1)} %param.11, f32[256,16]{1,0:T(8,128)S(1)} %broadcast_multiply_fusion), kind=kLoop, calls=%fused_computation.16 | loop fusion | flops 4190208 | bytes 2129920 | tf_op jit(solution)/shard_map/reduce_sum | solution.py:43
  12.4 0.0 copy-done.1
  12.4 0.0 copy-done.8
  12.4 0.0 copy-done.7
  12.4 1.7 fusion.24
  14.1 0.0 copy-start.2
  14.1 0.0 copy-start.5
  14.1 1.3 copy-done.2
  15.4 0.0 copy-done
  15.4 0.0 copy-done.9
  15.4 0.7 convolution_add_fusion.1
  16.1 0.0 copy-start.3
  16.1 0.0 copy-start.6
  16.1 0.0 copy-start.10
  16.1 1.9 %copy.35 = f32[4096,32]{1,0:T(8,128)} copy(f32[4096,32]{0,1:T(8,128)S(1)} %convolution_add_fusion.1) | data formatting | bytes 1048576 | tf_op jit(solution)/shard_map/add | solution.py:16
  18.1 2.3 %reshape.47 = f32[256,512]{1,0:T(8,128)S(1)} reshape(f32[4096,32]{1,0:T(8,128)} %copy.35) | data formatting | bytes 1048576 | tf_op jit(solution)/shard_map/reshape | solution.py:17
  20.4 0.0 copy-done.5
  20.4 0.8 mul.48
  21.2 1.2 copy.36
  22.5 0.8 multiply_convert_fusion.1
  23.2 0.0 all-gather.3.cloned.1.call-update
  23.3 0.0 all-gather.5.cloned.1.call-start
  23.3 0.0 copy-done.3
  23.3 0.0 copy-done.6
  23.3 0.0 copy-done.10
  23.4 0.7 convolution_add_fusion
  24.1 0.0 copy-start.4
  24.1 0.6 copy.38
  24.7 0.8 reshape.49
  25.5 0.2 copy.39
  25.7 0.8 multiply_convert_fusion
  26.5 0.0 all-gather.5.cloned.1.call-update
  26.5 0.0 reduce-scatter.7.cloned.1.call-start
  26.6 15.3 %all_gather.15 = bf16[256,128]{0,1:T(8,128)(2,1)S(1)} all-gather(bf16[256,16]{0,1:T(8,128)(2,1)S(1)} %copy-done.5), channel_id=1, replica_groups=mesh['row'=4,'col'=8,'depth'=4] {'col'}, dimensions={1}, use_global_device_ids=true | all-gather | bytes 73728 | tf_op jit(solution)/shard_map/all_gather | solution.py:55
  41.8 25.1 %all_gather.14 = bf16[256,512]{0,1:T(8,128)(2,1)S(1)} all-gather(bf16[256,16]{0,1:T(8,128)(2,1)S(1)} %copy-done.5), channel_id=1, replica_groups=mesh['row'=4,'col'=8,'depth'=4] {'row','col'}, dimensions={1}, use_global_device_ids=true | all-gather | bytes 270336 | tf_op jit(solution)/shard_map/all_gather | solution.py:59
  66.9 0.1 convolution_bitcast_fusion
  67.1 0.8 copy.45
  67.8 0.0 reduce-scatter.7.cloned.1.call-update
  67.9 0.2 reduce-scatter.5.cloned.1.call-start
  68.1 0.0 copy-done.4
  68.1 0.1 copy.41
  68.2 0.0 all-gather.3.cloned.1.call-done
  68.2 3.3 %copy.37 = bf16[256,4096]{0,1:T(8,128)(2,1)S(1)} copy(bf16[256,4096]{1,0:T(8,128)(2,1)} %all-gather.3.cloned.1.call-done) | data formatting | bytes 4194304 | tf_op jit(solution)/shard_map/all_gather | solution.py:54
  71.5 37.0 %all-gather.5.cloned.1.call-done = bf16[256,16384]{0,1:T(8,128)(2,1)} async-done(((bf16[256,512]{0,1:T(8,128)(2,1)}), bf16[256,16384]{0,1:T(8,128)(2,1)}) %all-gather.5.cloned.1.call-update) | async-done | bytes 8388624 | tf_op jit(solution)/shard_map/all_gather | solution.py:58
  108.5 1.3 constant_dynamic-slice_fusion
  109.8 0.6 copy.40
  110.4 17.8 %while.10 = (s32[]{:T(128)}, f32[4,32,64,128]{3,2,1,0:T(8,128)}, bf16[4,256,32,32]{1,3,2,0:T(8,128)(2,1)S(1)}, bf16[256,64,32]{0,1,2:T(8,128)(2,1)S(1)}, bf16[32,32,128]{2,0,1:T(8,128)(2,1)S(1)}, /*index=5*/s32[]{:T(128)}) while((s32[]{:T(128)}, f32[4,32,64,128]{3,2,1,0:T(8,128)}, bf16[4,256,32,32]{1,3,2,0:T(8,128)(2,1)S(1)}, ...), condition=%wide.region_3.4_spmd, body=%wide.region_2.3_spmd.sunk | while | flops 1612709888 | bytes 2884677 | solution.py:76
  110.4 4.5 %fusion.41 = f32[4,32,64,128]{3,2,1,0:T(8,128)} fusion(f32[4,32,64,128]{3,2,1,0:T(8,128)} %get-tuple-element.101, s32[]{:T(128)} %get-tuple-element.100, bf16[256,64,32]{0,1,2:T(8,128)(2,1)S(1)} %get-tuple-element.109, bf16[4,256,32,32]{1,3,2,0:T(8,128)(2,1)S(1)} %get-tuple-element.108, bf16[32,32,128]{2,0,1:T(8,128)(2,1)S(1)} %get-tuple-element.110), kind=kOutput, calls=%fused_computation.4.clone.1 | convolution fusion | flops 1612709888 | bytes 2884608 | tf_op jit(solution)/shard_map/while/body/eval_jaxpr/icjd,cde->ije/dot_general | solution.py:74
  114.9 4.4 %fusion.41 = f32[4,32,64,128]{3,2,1,0:T(8,128)} fusion(f32[4,32,64,128]{3,2,1,0:T(8,128)} %get-tuple-element.101, s32[]{:T(128)} %get-tuple-element.100, bf16[256,64,32]{0,1,2:T(8,128)(2,1)S(1)} %get-tuple-element.109, bf16[4,256,32,32]{1,3,2,0:T(8,128)(2,1)S(1)} %get-tuple-element.108, bf16[32,32,128]{2,0,1:T(8,128)(2,1)S(1)} %get-tuple-element.110), kind=kOutput, calls=%fused_computation.4.clone.1 | convolution fusion | flops 1612709888 | bytes 2884608 | tf_op jit(solution)/shard_map/while/body/eval_jaxpr/icjd,cde->ije/dot_general | solution.py:74
  119.4 4.5 %fusion.41 = f32[4,32,64,128]{3,2,1,0:T(8,128)} fusion(f32[4,32,64,128]{3,2,1,0:T(8,128)} %get-tuple-element.101, s32[]{:T(128)} %get-tuple-element.100, bf16[256,64,32]{0,1,2:T(8,128)(2,1)S(1)} %get-tuple-element.109, bf16[4,256,32,32]{1,3,2,0:T(8,128)(2,1)S(1)} %get-tuple-element.108, bf16[32,32,128]{2,0,1:T(8,128)(2,1)S(1)} %get-tuple-element.110), kind=kOutput, calls=%fused_computation.4.clone.1 | convolution fusion | flops 1612709888 | bytes 2884608 | tf_op jit(solution)/shard_map/while/body/eval_jaxpr/icjd,cde->ije/dot_general | solution.py:74
  123.8 4.4 %fusion.41 = f32[4,32,64,128]{3,2,1,0:T(8,128)} fusion(f32[4,32,64,128]{3,2,1,0:T(8,128)} %get-tuple-element.101, s32[]{:T(128)} %get-tuple-element.100, bf16[256,64,32]{0,1,2:T(8,128)(2,1)S(1)} %get-tuple-element.109, bf16[4,256,32,32]{1,3,2,0:T(8,128)(2,1)S(1)} %get-tuple-element.108, bf16[32,32,128]{2,0,1:T(8,128)(2,1)S(1)} %get-tuple-element.110), kind=kOutput, calls=%fused_computation.4.clone.1 | convolution fusion | flops 1612709888 | bytes 2884608 | tf_op jit(solution)/shard_map/while/body/eval_jaxpr/icjd,cde->ije/dot_general | solution.py:74
  128.3 0.0 reduce-scatter.5.cloned.1.call-update
  128.3 0.0 reduce-scatter.7.cloned.1.call-done
  128.3 0.7 broadcast_maximum_fusion
  129.0 45.1 %reduce-scatter.5.cloned.1.call-done = f32[32,64,128]{2,1,0:T(8,128)} async-done(((f32[128,64,128]{2,1,0:T(8,128)}), f32[32,64,128]{2,1,0:T(8,128)}) %reduce-scatter.5.cloned.1.call-update) | async-done | bytes 1048592 | tf_op jit(solution)/shard_map/reduce_scatter | solution.py:79
  174.1 2.4 %divide_convert_fusion = bf16[32,64,128]{2,1,0:T(8,128)(2,1)} fusion(f32[32,64,128]{2,1,0:T(8,128)} %reduce-scatter.5.cloned.1.call-done, f32[32,64]{1,0:T(8,128)S(1)} %broadcast_maximum_fusion), kind=kLoop, calls=%fused_computation.21 | loop fusion | flops 524288 | bytes 1581056 | tf_op jit(solution)/shard_map/convert_element_type | solution.py:82
  (4 shorter events, 0.0 us)
Async XLA Ops:
  7.4 8.0 %copy-start = (bf16[256,32]{0,1:T(8,128)(2,1)S(1)}, bf16[256,32]{0,1:T(8,128)(2,1)}, u32[]{:S(2)}) copy-start(bf16[256,32]{0,1:T(8,128)(2,1)} %param.15) | copy-start | bytes 49156
  7.4 5.0 %copy-start.1 = (bf16[256,16,256]{2,1,0:T(8,128)(2,1)S(1)}, bf16[256,16,256]{2,1,0:T(8,128)(2,1)}, u32[]{:S(2)}) copy-start(bf16[256,16,256]{2,1,0:T(8,128)(2,1)} %param.11) | copy-start | bytes 6291460
  7.4 5.0 %copy-start.8 = (f32[256]{0:T(256)S(1)}, f32[256]{0:T(256)}, u32[]{:S(2)}) copy-start(f32[256]{0:T(256)} %param.13) | copy-start | bytes 3076
  7.4 5.0 %copy-start.7 = (f32[256]{0:T(256)S(1)}, f32[256]{0:T(256)}, u32[]{:S(2)}) copy-start(f32[256]{0:T(256)} %param.14) | copy-start | bytes 3076
  7.4 60.9 %all-gather.3.cloned.1.call-start = ((), (), s32[]{:S(2)}) async-start(), calls=%async_computation.2 | async-start | bytes 2359296 | tf_op jit(solution)/shard_map/all_gather | solution.py:54
  9.8 5.6 %copy-start.9 = (f32[32]{0:T(128)S(1)}, f32[32]{0:T(128)}, u32[]{:S(2)}) copy-start(f32[32]{0:T(128)} %param.16) | copy-start | bytes 388
  14.1 1.3 copy-start.2
  14.1 6.3 %copy-start.5 = (bf16[256,16]{0,1:T(8,128)(2,1)S(1)}, bf16[256,16]{0,1:T(8,128)(2,1)}, u32[]{:S(2)}) copy-start(bf16[256,16]{0,1:T(8,128)(2,1)} %param.12) | copy-start | bytes 24580
  16.1 7.2 %copy-start.3 = (bf16[256,16,256]{2,1,0:T(8,128)(2,1)S(1)}, bf16[256,16,256]{2,1,0:T(8,128)(2,1)}, u32[]{:S(2)}) copy-start(bf16[256,16,256]{2,1,0:T(8,128)(2,1)} %copy-done.2) | copy-start | bytes 6291460
  16.1 7.2 %copy-start.6 = (bf16[256,32]{0,1:T(8,128)(2,1)S(1)}, bf16[256,32]{0,1:T(8,128)(2,1)}, u32[]{:S(2)}) copy-start(bf16[256,32]{0,1:T(8,128)(2,1)} %param.17) | copy-start | bytes 49156
  16.1 7.2 %copy-start.10 = (f32[32]{0:T(128)S(1)}, f32[32]{0:T(128)}, u32[]{:S(2)}) copy-start(f32[32]{0:T(128)} %param.18) | copy-start | bytes 388
  23.3 85.3 %all-gather.5.cloned.1.call-start = ((), (), s32[]{:S(2)}) async-start(), calls=%async_computation.3 | async-start | bytes 8650752 | tf_op jit(solution)/shard_map/all_gather | solution.py:58
  24.1 44.0 %copy-start.4 = (bf16[1024,128]{1,0:T(8,128)(2,1)S(1)}, bf16[1024,128]{1,0:T(8,128)(2,1)}, u32[]{:S(2)}) copy-start(bf16[1024,128]{1,0:T(8,128)(2,1)} %param.19) | copy-start | bytes 786436
  26.5 101.8 %reduce-scatter.7.cloned.1.call-start = ((), (), s32[]{:S(2)}) async-start(), calls=%async_computation.5 | async-start | bytes 81920 | tf_op jit(solution)/shard_map/reduce_scatter | solution.py:80
  67.9 106.3 %reduce-scatter.5.cloned.1.call-start = ((), (), s32[]{:S(2)}) async-start(), calls=%async_computation.4 | async-start | bytes 5242880 | tf_op jit(solution)/shard_map/reduce_scatter | solution.py:79
Sparse Core Ops, SparseCore 0:
  23.4 29.0 all-gather.2
  55.0 53.5 all-gather.4
Sparse Core Ops, SparseCore 1:
  67.9 16.9 reduce-scatter.6
  128.4 45.7 reduce-scatter.4
where the time goes:
time: 184 us
  waiting for transfers between devices  82.2 us (45%)
  blocking collectives  40.4 us (22%)
  matrix products  19.4 us (11%)
  local copies, waits for them, and re-layouts  15.3 us (8%)
  between operations  15.1 us (8%)
  other arithmetic  11.2 us (6%)
    reduce_scatter x1, waiting for transfers between devices, per_device(): lax.psum_scatter(partial_tile, 'depth', scatter_dimension=0, tiled=True)  45.1 us
    all_gather x1, waiting for transfers between devices, per_device(): lax.all_gather(right, ('row', 'col'), axis=1, tiled=True)  37 us
    all_gather x1, blocking collectives, per_device(): lax.all_gather(presence_indicator, ('row', 'col'), axis=1, tiled=True)  25.1 us
    dot_general x4, matrix products, one_block(): jnp.einsum('icjd,cde->ije', outer, weight3, preferred_element_type=jnp.fl...  17.8 us
    all_gather x1, blocking collectives, per_device(): lax.all_gather(presence_indicator, 'col', axis=1, tiled=True)  15.3 us
  transfers between devices with their start and end apart: 4, of which 2 were waited for; matrix products, arithmetic and copies ran while one was open for 15% of the time, Pallas kernels for 0%

commit v1 on v0

v1 whole, which is shorter than its diff:
```python
import functools

import jax
import jax.numpy as jnp
from jax import lax
from jax.experimental import pallas as pl
from jax.experimental.pallas import tpu as pltpu
from jax.sharding import PartitionSpec as P

F32 = jnp.float32
BF16 = jnp.bfloat16
NT = (((1,), (1,)), ((), ()))
NN = (((1,), (0,)), ((), ()))

SEQ = 256
RES = 16
HID = 32
SHARD = RES * HID
ROWS = SHARD + RES


def dot(a, b, dims):
    return lax.dot_general(a, b, dims, preferred_element_type=F32)


def project_kernel(sig, mask, gain, shift, w_left, b_left, w_right, b_right, left, right, wide, cols, turn):
    half = sig.shape[0]

    @pl.when(pl.program_id(0) == 0)
    def _():
        turn[...] = jnp.zeros_like(turn)
        turn[0:256, 0:HID] = w_left[...].astype(F32)
        turn[0:256, HID : 2 * HID] = w_right[...].astype(F32)
        turn[256:384, 0:HID] = jnp.broadcast_to(b_left[...], (128, HID))
        turn[256:384, HID : 2 * HID] = jnp.broadcast_to(b_right[...], (128, HID))

    weights = jnp.transpose(turn[0:256, :])[0 : 2 * HID, :].astype(BF16)
    bias = jnp.transpose(turn[256:384, :])[0 : 2 * HID, :]
    turn[384 : 384 + half, 0:RES] = mask[...].astype(F32)
    presence = jnp.transpose(turn[384 : 384 + half, :])[0:RES, :]

    flat = sig[...].astype(F32).reshape(half * RES, 256)
    wide[0] = flat[:, 0:128]
    wide[1] = flat[:, 128:256]
    for r in range(RES):
        low = wide[0, pl.ds(r, half, stride=RES), :]
        high = wide[1, pl.ds(r, half, stride=RES), :]
        mean = jnp.sum(low + high, axis=1, keepdims=True) * (1.0 / 256)
        low = low - mean
        high = high - mean
        spread = jnp.sum(low * low + high * high, axis=1, keepdims=True) * (1.0 / 256)
        scale = lax.rsqrt(spread + 1e-5)
        low = low * scale * gain[:, 0:128] + shift[:, 0:128]
        high = high * scale * gain[:, 128:256] + shift[:, 128:256]
        normed = jnp.concatenate([low.astype(BF16), high.astype(BF16)], axis=1)
        both = (dot(weights, normed, NT) + bias) * presence[r : r + 1, :]
        left[r * HID : (r + 1) * HID, :] = both[0:HID].astype(BF16)
        cols[r * HID : (r + 1) * HID, :] = both[HID : 2 * HID]
    for d in range(HID):
        right[d * RES : (d + 1) * RES, :] = cols[pl.ds(d, RES, stride=HID), :].astype(BF16)
    left[SHARD:ROWS, :] = presence.astype(BF16)
    right[SHARD:ROWS, :] = presence.astype(BF16)


def project(sig, mask, gain, shift, w_left, b_left, w_right, b_right):
    steps = 2
    half = SEQ // steps
    whole = lambda shape: pl.BlockSpec(shape, lambda s: (0,) * len(shape))
    return pl.pallas_call(
        project_kernel,
        grid=(steps,),
        in_specs=[
            pl.BlockSpec((half, RES, 256), lambda s: (s, 0, 0)),
            pl.BlockSpec((half, RES), lambda s: (s, 0)),
            whole((1, 256)),
            whole((1, 256)),
            whole((256, HID)),
            whole((1, HID)),
            whole((256, HID)),
            whole((1, HID)),
        ],
        out_specs=[pl.BlockSpec((ROWS, half), lambda s: (0, s))] * 2,
        out_shape=[jax.ShapeDtypeStruct((ROWS, SEQ), BF16)] * 2,
        scratch_shapes=[
            pltpu.VMEM((2, half * RES, 128), F32),
            pltpu.VMEM((SHARD, half), F32),
            pltpu.VMEM((384 + half, 128), F32),
        ],
        compiler_params=pltpu.CompilerParams(vmem_limit_bytes=40 * 2**20),
        name="project",
    )(sig, mask, gain, shift, w_left, b_left, w_right, b_right)


def pair_kernel(own, place, *refs):
    lefts, rights, mix = refs[0:4], refs[4:12], refs[12]
    if own:
        out, count, outer, chosen = refs[13:]
    else:
        out, outer, chosen = refs[13:]
    which = place[0]
    for t in range(4):

        @pl.when(which == t)
        def _():
            chosen[...] = lefts[t][...]

    @pl.loop(0, HID // 2)
    def _(step):
        parts = []
        for dd in range(2):
            start = pl.multiple_of(step * 2 * RES + dd * RES, RES)
            for ref in rights:
                parts.append(ref[pl.ds(start, RES), :])
        block = jnp.concatenate(parts, axis=0)
        prod = dot(chosen[0:SHARD, :], block, NT).astype(BF16)
        for dd in range(2):
            at = pl.multiple_of(step * 2 * HID + dd * HID, HID)
            for i in range(RES):
                outer[i // 2, pl.ds(at, HID), (i % 2) * 128 : (i % 2) * 128 + 128] = prod[
                    i * HID : (i + 1) * HID, dd * 128 : (dd + 1) * 128
                ]

    @pl.loop(0, RES // 2)
    def _(pair):
        mixed = dot(mix[...], outer[pair], NN)
        for ii in range(2):
            out[pair * 2 + ii] = jnp.transpose(mixed[:, ii * 128 : (ii + 1) * 128]).astype(out.dtype)

    weights = jnp.concatenate([ref[SHARD:ROWS, :] for ref in rights], axis=0)
    tally = jnp.concatenate([chosen[SHARD:ROWS, :], jnp.zeros((128 - RES, SEQ), BF16)], axis=0)
    tally = dot(weights, tally, NT)
    if own:
        count[...] = tally
    else:
        high = tally.astype(BF16)
        out[RES] = high
        out[RES + 1] = (tally - high.astype(F32)).astype(BF16)


def pair(own, place, lefts, rights, mix):
    vmem = pl.BlockSpec(memory_space=pltpu.VMEM)
    if own:
        out_shape = [
            jax.ShapeDtypeStruct((RES, 128, 128), F32),
            jax.ShapeDtypeStruct((128, 128), F32),
        ]
    else:
        out_shape = [jax.ShapeDtypeStruct((RES + 2, 128, 128), BF16)]
    return pl.pallas_call(
        functools.partial(pair_kernel, own),
        in_specs=[pl.BlockSpec(memory_space=pltpu.SMEM)] + [vmem] * 13,
        out_specs=[vmem] * len(out_shape),
        out_shape=out_shape,
        scratch_shapes=[
            pltpu.VMEM((RES // 2, HID * HID, 256), BF16),
            pltpu.VMEM((ROWS, SEQ), BF16),
        ],
        compiler_params=pltpu.CompilerParams(vmem_limit_bytes=40 * 2**20),
        cost_estimate=pl.CostEstimate(
            flops=2 * SHARD * SHARD * 8 * SEQ + 2 * 128 * 16 * 128 * 1024,
            bytes_accessed=5 * 2**20,
            transcendentals=0,
        ),
        name="pair",
    )(place, *lefts, *rights, mix)


def settle_kernel(place, mine, count, a, b, c, *refs):
    pieces, inverse = refs[0:4], refs[4]
    total = count[...]
    for ref in (a, b, c):
        total = total + (ref[RES].astype(F32) + ref[RES + 1].astype(F32))
    inverse[...] = 1.0 / jnp.maximum(total, 1.0)
    for u in range(4):
        for h in range(2):
            start = pl.multiple_of(place[u * 2 + h], RES)
            rows = pl.ds(start, RES)
            factor = inverse[rows, :]
            for i in range(RES):
                value = mine[i, rows, :]
                for ref in (a, b, c):
                    value = value + ref[i, rows, :].astype(F32)
                pieces[u][i, h * RES : (h + 1) * RES, :] = (value * factor[:, i : i + 1]).astype(BF16)


def settle(place, mine, count, a, b, c):
    vmem = pl.BlockSpec(memory_space=pltpu.VMEM)
    return pl.pallas_call(
        settle_kernel,
        in_specs=[pl.BlockSpec(memory_space=pltpu.SMEM)] + [vmem] * 5,
        out_specs=[vmem] * 4,
        out_shape=[jax.ShapeDtypeStruct((RES, 2 * RES, 128), BF16)] * 4,
        scratch_shapes=[pltpu.VMEM((128, 128), F32)],
        compiler_params=pltpu.CompilerParams(vmem_limit_bytes=40 * 2**20),
        name="settle",
    )(place, mine, count, a, b, c)


def lay_kernel(place, *refs):
    out = refs[4]
    for u in range(4):
        at = pl.multiple_of(place[u * 2] * RES, RES)
        start = pl.multiple_of(place[u * 2 + 1] * 2 * RES, 2 * RES)
        out[pl.ds(at, RES), pl.ds(start, 2 * RES), :] = refs[u][...]


def lay(place, pieces):
    vmem = pl.BlockSpec(memory_space=pltpu.VMEM)
    return pl.pallas_call(
        lay_kernel,
        in_specs=[pl.BlockSpec(memory_space=pltpu.SMEM)] + [vmem] * 4,
        out_specs=vmem,
        out_shape=jax.ShapeDtypeStruct((2 * RES, 4 * RES, 128), BF16),
        compiler_params=pltpu.CompilerParams(vmem_limit_bytes=40 * 2**20),
        name="lay",
    )(place, *pieces)


def shift_pairs(n, step):
    return [(s, (s + step) % n) for s in range(n)]


def per_device(sig, mask, gain, shift, w_left, b_left, w_right, b_right, w_out):
    x = lax.axis_index("depth")
    y = lax.axis_index("row")
    col = lax.axis_index("col")
    z, core = col // 2, col % 2

    left, right = project(
        sig,
        mask,
        gain.reshape(1, 256),
        shift.reshape(1, 256),
        w_left,
        b_left.reshape(1, HID),
        w_right,
        b_right.reshape(1, HID),
    )
    mix = w_out.reshape(HID, HID, 128).transpose(2, 1, 0).reshape(128, HID * HID)

    flip = lambda v: lax.ppermute(v, "col", [(s, s ^ 1) for s in range(8)])
    rights = {0: right}
    lefts = {0: left}
    for t in (2, 1, 3):
        rights[t] = lax.ppermute(right, "row", shift_pairs(4, -t))
        lefts[t] = lax.ppermute(left, "col", shift_pairs(8, -2 * t))
    columns = []
    for t in range(4):
        columns += [rights[t], flip(rights[t])]
    rows = [lefts[t] for t in range(4)]

    def quarter(k):
        return ((x + k - z) % 4).astype(jnp.int32).reshape(1)

    got = {}
    for k in (2, 1, 3):
        (part,) = pair(False, quarter(k), rows, columns, mix)
        got[k] = lax.ppermute(part, "depth", shift_pairs(4, k))
    mine, count = pair(True, quarter(0), rows, columns, mix)

    slot = 2 * (z % 2) + core
    spots = []
    for u in range(4):
        t = ((slot + u) % 4 - y) % 4
        for h in range(2):
            spots.append(t * 32 + (h ^ core) * 16)
    pieces = settle(jnp.stack(spots).astype(jnp.int32), mine, count, got[2], got[1], got[3])

    seats, landed = [], []
    for u in range(4):
        pairs = []
        for s in range(8):
            sz, sc = s // 2, s % 2
            pairs.append((s, 2 * ((2 * (sz % 2) + sc + u) % 4) + sz // 2))
        landed.append(lax.ppermute(pieces[u], "col", pairs))
        seat = (z - u) % 4
        seats += [seat % 2, seat // 2]
    return lay(jnp.stack(seats).astype(jnp.int32), landed)


def solution(mesh):
    return jax.shard_map(
        per_device,
        mesh=mesh,
        in_specs=(
            P("depth", ("row", "col"), None),
            P("depth", ("row", "col")),
            P(),
            P(),
            P(),
            P(),
            P(),
            P(),
            P(),
        ),
        out_specs=P(("row", "depth"), "col", None),
        check_vma=False,
    )
```

time: 184 us -> 114 us (0.62)
  waiting for transfers between devices: 82.2 us -> 11.7 us
  blocking collectives: 40.4 us -> 0 us
  Pallas kernels: 0 us -> 39 us
  starting transfers between devices: 0.34 us -> 31.9 us
  matrix products: 19.4 us -> 0 us
  between operations: 15.1 us -> 0.44 us
  local copies, waits for them, and re-layouts: 15.3 us -> 29.9 us
  other arithmetic: 11.2 us -> 0 us
    reduce_scatter x2 -> x0, waiting for transfers between devices: 45.1 us -> none  [the longest x1 45.1 us: per_device(): lax.psum_scatter(partial_tile, 'depth', scatter_dimension=0, tiled=True)]
    all_gather x2 -> x0, blocking collectives: 40.4 us -> none  [the longest x1 25.1 us: per_device(): lax.all_gather(presence_indicator, ('row', 'col'), axis=1, tiled=True)]
    pallas_call x0 -> x7, Pallas kernels: none -> 39 us  [the longest x4 33 us: pair(): pl.pallas_call(functools.partial(pair_kernel, own), in_specs=[pl.BlockSpe...]
    all_gather x2 -> x0, waiting for transfers between devices: 37 us -> none  [the longest x1 37 us: per_device(): lax.all_gather(right, ('row', 'col'), axis=1, tiled=True)]
    ppermute x0 -> x17, starting transfers between devices: none -> 31.9 us  [the longest x4 10.7 us: per_device(): landed.append(lax.ppermute(pieces[u], 'col', pairs))]
    unnamed x23 -> x75, local copies, waits for them, and re-layouts: 2.15 us -> 26.9 us
    dot_general x7 -> x0, matrix products: 19.4 us -> none  [the longest x4 17.8 us: one_block(): jnp.einsum('icjd,cde->ije', outer, weight3, preferred_element_type=jnp.fl...]
    ppermute x0 -> x17, waiting for transfers between devices: none -> 11.7 us  [the longest x3 5.54 us: per_device(): lefts[t] = lax.ppermute(left, 'col', shift_pairs(8, -2 * t))]
  transfers between devices with their start and end apart: 4 -> 17, of which waited for: 2 -> 4; matrix products, arithmetic and copies ran while one was open for 15% -> 3% of each run, Pallas kernels for 0% -> 22%
where the time goes in v1:
time: 114 us; the launch traced here: 113 us
  Pallas kernels  39 us (34%)
  starting transfers between devices  31.9 us (28%)
  local copies, waits for them, and re-layouts  29.9 us (26%)
  waiting for transfers between devices  11.7 us (10%)
    pallas_call x4, Pallas kernels, pair(): pl.pallas_call(functools.partial(pair_kernel, own), in_specs=[pl.BlockSpe...  33 us
    unnamed x75, local copies, waits for them, and re-layouts  26.9 us
    ppermute x4, starting transfers between devices, per_device(): landed.append(lax.ppermute(pieces[u], 'col', pairs))  10.7 us
    ppermute x3, starting transfers between devices, per_device(): lefts[t] = lax.ppermute(left, 'col', shift_pairs(8, -2 * t))  6.98 us
    ppermute x3, waiting for transfers between devices, per_device(): lefts[t] = lax.ppermute(left, 'col', shift_pairs(8, -2 * t))  5.54 us
    ppermute x3, starting transfers between devices, per_device(): got[k] = lax.ppermute(part, 'depth', shift_pairs(4, k))  5.5 us
    ppermute x3, starting transfers between devices, per_device(): rights[t] = lax.ppermute(right, 'row', shift_pairs(4, -t))  4.99 us
    ppermute x4, waiting for transfers between devices, per_device(): landed.append(lax.ppermute(pieces[u], 'col', pairs))  4.5 us
  transfers between devices with their start and end apart: 17, of which 4 were waited for; matrix products, arithmetic and copies ran while one was open for 3% of the time, Pallas kernels for 22%

profile of v1, /device:TPU:1, one launch (start us, length us, event | category | flops | bytes accessed | tf_op | source)
XLA Modules:
  0.0 112.9 jit_solution(6014177867834194597)
XLA Ops:
  0.0 0.8 copy.21.mask
  0.8 0.8 copy.22.w_left
  1.7 0.8 copy.23.w_right
  2.5 1.6 %copy-done = bf16[256,16,256]{2,1,0:T(8,128)(2,1)S(1)} copy-done((bf16[256,16,256]{2,1,0:T(8,128)(2,1)S(1)}, bf16[256,16,256]{2,1,0:T(8,128)(2,1)}, u32[]{:S(2)}) %copy-start) | copy-done | bytes 2097176
  4.1 0.7 copy-done.1
  4.8 0.7 copy-done.2
  5.4 0.7 copy-done.3
  6.1 0.7 copy-done.4
  6.8 3.5 %project.1 = (bf16[528,256]{1,0:T(8,128)(2,1)S(1)}, bf16[528,256]{1,0:T(8,128)(2,1)S(1)}) custom-call(bf16[256,16,256]{2,1,0:T(8,128)(2,1)S(1)} %copy-done, bf16[256,16]{1,0:T(8,128)(2,1)S(1)} %copy.21.mask, f32[1,256]{1,0:T(1,128)S(1)} %bitcast.28, f32[1,256]{1,0:T(1,128)S(1)} %bitcast.29, bf16[256,32]{1,0:T(8,128)(2,1)S(1)} %copy.22.w_left, ...), custom_call_target="tpu_custom_call" | custom-call | tf_op jit(solution)/shard_map/project/pallas_call | solution.py:69
  10.3 2.5 %collective-permute-start.2 = (bf16[528,256]{1,0:T(8,128)(2,1)S(1)}, bf16[528,256]{1,0:T(8,128)(2,1)S(1)}, u32[]{:S(2)}, u32[]{:S(2)}) collective-permute-start(bf16[528,256]{1,0:T(8,128)(2,1)S(1)} %get-tuple-element.13.refs_0_), channel_id=1, source_target_pairs={{0,8},{4,12},{8,16},{12,20},{16,24},{20,28},{24,0},{28,4},{1,9},{5... | collective-permute-start | bytes 811016 | tf_op jit(solution)/shard_map/ppermute | solution.py:246
  12.8 3.3 %collective-permute-start.1 = (bf16[528,256]{1,0:T(8,128)(2,1)S(1)}, bf16[528,256]{1,0:T(8,128)(2,1)S(1)}, u32[]{:S(2)}, u32[]{:S(2)}) collective-permute-start(bf16[528,256]{1,0:T(8,128)(2,1)S(1)} %get-tuple-element.13.refs_0_), channel_id=1, source_target_pairs={{0,16},{4,20},{8,24},{12,28},{16,0},{20,4},{24,8},{28,12},{1,17},{... | collective-permute-start | bytes 811016 | tf_op jit(solution)/shard_map/ppermute | solution.py:246
  16.1 1.3 %collective-permute-start.8 = (bf16[528,256]{1,0:T(8,128)(2,1)S(1)}, bf16[528,256]{1,0:T(8,128)(2,1)S(1)}, u32[]{:S(2)}, u32[]{:S(2)}) collective-permute-start(bf16[528,256]{1,0:T(8,128)(2,1)S(1)} %get-tuple-element.14.refs_4_), channel_id=1, source_target_pairs={{0,32},{32,64},{64,96},{96,0},{1,33},{33,65},{65,97},{97,1},{2,34}... | collective-permute-start | bytes 811016 | tf_op jit(solution)/shard_map/ppermute | solution.py:245
  17.4 2.6 %collective-permute-start.6 = (bf16[528,256]{1,0:T(8,128)(2,1)S(1)}, bf16[528,256]{1,0:T(8,128)(2,1)S(1)}, u32[]{:S(2)}, u32[]{:S(2)}) collective-permute-start(bf16[528,256]{1,0:T(8,128)(2,1)S(1)} %get-tuple-element.14.refs_4_), channel_id=1, source_target_pairs={{0,64},{32,96},{64,0},{96,32},{1,65},{33,97},{65,1},{97,33},{2,66}... | collective-permute-start | bytes 811016 | tf_op jit(solution)/shard_map/ppermute | solution.py:245
  20.0 1.1 collective-permute-start.4
  21.1 0.0 collective-permute-done.2.refs_3_
  21.1 1.1 %collective-permute-start = (bf16[528,256]{1,0:T(8,128)(2,1)S(1)}, bf16[528,256]{1,0:T(8,128)(2,1)S(1)}, u32[]{:S(2)}, u32[]{:S(2)}) collective-permute-start(bf16[528,256]{1,0:T(8,128)(2,1)S(1)} %get-tuple-element.13.refs_0_), channel_id=1, source_target_pairs={{0,24},{4,28},{8,0},{12,4},{16,8},{20,12},{24,16},{28,20},{1,25},{... | collective-permute-start | bytes 811016 | tf_op jit(solution)/shard_map/ppermute | solution.py:246
  22.3 5.5 %collective-permute-done.1.refs_2_ = bf16[528,256]{1,0:T(8,128)(2,1)S(1)} collective-permute-done((bf16[528,256]{1,0:T(8,128)(2,1)S(1)}, bf16[528,256]{1,0:T(8,128)(2,1)S(1)}, u32[]{:S(2)}, u32[]{:S(2)}) %collective-permute-start.1) | collective-permute-done | bytes 270368 | tf_op jit(solution)/shard_map/ppermute | solution.py:246
  27.8 1.5 %collective-permute-start.3 = (bf16[528,256]{1,0:T(8,128)(2,1)S(1)}, bf16[528,256]{1,0:T(8,128)(2,1)S(1)}, u32[]{:S(2)}, u32[]{:S(2)}) collective-permute-start(bf16[528,256]{1,0:T(8,128)(2,1)S(1)} %get-tuple-element.14.refs_4_), channel_id=1, source_target_pairs={{0,4},{4,0},{8,12},{12,8},{16,20},{20,16},{24,28},{28,24},{1,5},{5... | collective-permute-start | bytes 811016 | tf_op jit(solution)/shard_map/ppermute | solution.py:241
  29.3 0.1 collective-permute-start.9
  29.4 1.7 %collective-permute-done.6.refs_8_ = bf16[528,256]{1,0:T(8,128)(2,1)S(1)} collective-permute-done((bf16[528,256]{1,0:T(8,128)(2,1)S(1)}, bf16[528,256]{1,0:T(8,128)(2,1)S(1)}, u32[]{:S(2)}, u32[]{:S(2)}) %collective-permute-start.6) | collective-permute-done | bytes 270368 | tf_op jit(solution)/shard_map/ppermute | solution.py:245
  31.1 2.2 %collective-permute-start.7 = (bf16[528,256]{1,0:T(8,128)(2,1)S(1)}, bf16[528,256]{1,0:T(8,128)(2,1)S(1)}, u32[]{:S(2)}, u32[]{:S(2)}) collective-permute-start(bf16[528,256]{1,0:T(8,128)(2,1)S(1)} %collective-permute-done.6.refs_8_), channel_id=1, source_target_pairs={{0,4},{4,0},{8,12},{12,8},{16,20},{20,16},{24,28},{28,24},{1,5},{5... | collective-permute-start | bytes 811016 | tf_op jit(solution)/shard_map/ppermute | solution.py:241
  33.2 0.0 collective-permute-start.5
  33.2 1.8 %copy.24 = bf16[128,32,32]{0,2,1:T(8,128)(2,1)} copy(bf16[128,32,32]{0,1,2:T(8,128)(2,1)} %bitcast.33) | data formatting | bytes 524288 | tf_op jit(solution)/shard_map/transpose | solution.py:239
  35.0 1.1 copy.25.refs_12_
  36.1 0.0 copy-start.21
  36.2 0.8 copy-done.28
  37.0 0.7 copy-done.32
  37.7 1.0 copy-done.29
  38.7 1.0 copy-done.33
  39.6 8.1 %pair.5 = bf16[18,128,128]{2,1,0:T(8,128)(2,1)S(1)} custom-call(s32[1]{0:T(128)} %bitcast.24.place, bf16[528,256]{1,0:T(8,128)(2,1)S(1)} %get-tuple-element.13.refs_0_, bf16[528,256]{1,0:T(8,128)(2,1)S(1)} %collective-permute-done.refs_1_, bf16[528,256]{1,0:T(8,128)(2,1)S(1)} %collective-permute-done.1.refs_2_, ...), custom_call_target="tpu_custom_call" | custom-call | flops 1610612736 | bytes 5242880 | tf_op jit(solution)/shard_map/pair/pallas_call | solution.py:149
  47.7 0.7 copy-done.15
  48.4 0.7 copy-done.18
  49.1 2.7 %collective-permute-start.10 = (bf16[18,128,128]{2,1,0:T(8,128)(2,1)S(1)}, bf16[18,128,128]{2,1,0:T(8,128)(2,1)S(1)}, u32[]{:S(2)}, u32[]{:S(2)}) collective-permute-start(bf16[18,128,128]{2,1,0:T(8,128)(2,1)S(1)} %pair.5), channel_id=1, source_target_pairs={{0,2},{1,3},{2,0},{3,1},{4,6},{5,7},{6,4},{7,5},{8,10},{9,11},{10,... | collective-permute-start | bytes 1769480 | tf_op jit(solution)/shard_map/ppermute | solution.py:258
  51.9 0.9 copy-done.16
  52.9 1.0 copy-done.19
  53.8 1.0 copy-done.22
  54.8 1.0 copy-done.25
  55.7 8.1 %pair.6 = bf16[18,128,128]{2,1,0:T(8,128)(2,1)S(1)} custom-call(s32[1]{0:T(128)} %bitcast.25.place, bf16[528,256]{1,0:T(8,128)(2,1)S(1)} %get-tuple-element.13.refs_0_, bf16[528,256]{1,0:T(8,128)(2,1)S(1)} %copy-done.22, bf16[528,256]{1,0:T(8,128)(2,1)S(1)} %collective-permute-done.1.refs_2_, bf16[528,256]{1,0:T(8,128)(2,1)S(1)} %collective-permute-done.2.refs_3_, ...), custom_call_target="tpu_custom_call" | custom-call | flops 1610612736 | bytes 5242880 | tf_op jit(solution)/shard_map/pair/pallas_call | solution.py:149
  63.8 0.4 collective-permute-start.11
  64.2 0.9 copy-done.10
  65.1 1.0 copy-done.13
  66.1 9.0 %pair.7 = bf16[18,128,128]{2,1,0:T(8,128)(2,1)} custom-call(s32[1]{0:T(128)} %bitcast.26.place, bf16[528,256]{1,0:T(8,128)(2,1)S(1)} %get-tuple-element.13.refs_0_, bf16[528,256]{1,0:T(8,128)(2,1)S(1)} %copy-done.22, bf16[528,256]{1,0:T(8,128)(2,1)S(1)} %copy-done.10, bf16[528,256]{1,0:T(8,128)(2,1)S(1)} %collective-permute-done.2.refs_3_, ...), custom_call_target="tpu_custom_call" | custom-call | flops 1610612736 | bytes 5242880 | tf_op jit(solution)/shard_map/pair/pallas_call | solution.py:149
  75.1 2.3 %collective-permute-start.12 = (bf16[18,128,128]{2,1,0:T(8,128)(2,1)}, bf16[18,128,128]{2,1,0:T(8,128)(2,1)S(1)}, u32[]{:S(2)}, u32[]{:S(2)}) collective-permute-start(bf16[18,128,128]{2,1,0:T(8,128)(2,1)} %pair.7), channel_id=1, source_target_pairs={{0,3},{1,0},{2,1},{3,2},{4,7},{5,4},{6,5},{7,6},{8,11},{9,8},{10,9... | collective-permute-start | bytes 1769480 | tf_op jit(solution)/shard_map/ppermute | solution.py:258
  77.4 0.1 stack.71.place
  77.5 1.0 copy-done.6
  78.5 1.0 copy-done.8
  79.4 1.0 copy-done.11
  80.4 1.0 copy-done.14
  81.3 1.0 copy-done.17
  82.3 1.0 copy-done.20
  83.2 1.0 copy-done.23
  84.2 1.0 copy-done.27
  85.1 1.0 copy-done.31
  86.1 1.0 copy-done.35
  87.0 7.9 %pair.4 = (f32[16,128,128]{2,1,0:T(8,128)S(1)}, f32[128,128]{1,0:T(8,128)S(1)}) custom-call(s32[1]{0:T(128)} %bitcast.16.place, bf16[528,256]{1,0:T(8,128)(2,1)S(1)} %get-tuple-element.13.refs_0_, bf16[528,256]{1,0:T(8,128)(2,1)S(1)} %copy-done.23, bf16[528,256]{1,0:T(8,128)(2,1)S(1)} %copy-done.11, bf16[528,256]{1,0:T(8,128)(2,1)S(1)} %copy-done.8, ...), custom_call_target="tpu_custom_call" | custom-call | flops 1610612736 | bytes 5242880 | tf_op jit(solution)/shard_map/pair/pallas_call | solution.py:149
  95.0 1.1 settle.1
  96.1 2.6 %collective-permute-start.13 = (bf16[16,32,128]{2,1,0:T(8,128)(2,1)S(1)}, bf16[16,32,128]{2,1,0:T(8,128)(2,1)S(1)}, u32[]{:S(2)}, u32[]{:S(2)}) collective-permute-start(bf16[16,32,128]{2,1,0:T(8,128)(2,1)S(1)} %get-tuple-element.17), channel_id=1, source_target_pairs={{0,0},{4,8},{8,16},{12,24},{16,4},{20,12},{24,20},{28,28},{1,1},{5... | collective-permute-start | bytes 393224 | tf_op jit(solution)/shard_map/ppermute | solution.py:275
  98.7 4.5 %collective-permute-start.14 = (bf16[16,32,128]{2,1,0:T(8,128)(2,1)S(1)}, bf16[16,32,128]{2,1,0:T(8,128)(2,1)S(1)}, u32[]{:S(2)}, u32[]{:S(2)}) collective-permute-start(bf16[16,32,128]{2,1,0:T(8,128)(2,1)S(1)} %get-tuple-element.18), channel_id=1, source_target_pairs={{0,8},{4,16},{8,24},{12,0},{16,12},{20,20},{24,28},{28,4},{1,9},{5... | collective-permute-start | bytes 393224 | tf_op jit(solution)/shard_map/ppermute | solution.py:275
  103.2 0.1 collective-permute-start.15
  103.3 3.5 %collective-permute-start.16 = (bf16[16,32,128]{2,1,0:T(8,128)(2,1)S(1)}, bf16[16,32,128]{2,1,0:T(8,128)(2,1)S(1)}, u32[]{:S(2)}, u32[]{:S(2)}) collective-permute-start(bf16[16,32,128]{2,1,0:T(8,128)(2,1)S(1)} %get-tuple-element.20), channel_id=1, source_target_pairs={{0,24},{4,0},{8,8},{12,16},{16,28},{20,4},{24,12},{28,20},{1,25},{... | collective-permute-start | bytes 393224 | tf_op jit(solution)/shard_map/ppermute | solution.py:275
  106.9 0.1 stack.62.place
  107.0 1.8 %collective-permute-done.15.refs_2_ = bf16[16,32,128]{2,1,0:T(8,128)(2,1)S(1)} collective-permute-done((bf16[16,32,128]{2,1,0:T(8,128)(2,1)S(1)}, bf16[16,32,128]{2,1,0:T(8,128)(2,1)S(1)}, u32[]{:S(2)}, u32[]{:S(2)}) %collective-permute-start.15) | collective-permute-done | bytes 131104 | tf_op jit(solution)/shard_map/ppermute | solution.py:275
  108.8 2.7 %collective-permute-done.16.refs_3_ = bf16[16,32,128]{2,1,0:T(8,128)(2,1)S(1)} collective-permute-done((bf16[16,32,128]{2,1,0:T(8,128)(2,1)S(1)}, bf16[16,32,128]{2,1,0:T(8,128)(2,1)S(1)}, u32[]{:S(2)}, u32[]{:S(2)}) %collective-permute-start.16) | collective-permute-done | bytes 131104 | tf_op jit(solution)/shard_map/ppermute | solution.py:275
  111.5 1.4 %lay.1 = bf16[32,64,128]{2,1,0:T(8,128)(2,1)} custom-call(s32[8]{0:T(128)S(1)} %stack.62.place, bf16[16,32,128]{2,1,0:T(8,128)(2,1)S(1)} %collective-permute-done.13.refs_0_, bf16[16,32,128]{2,1,0:T(8,128)(2,1)S(1)} %collective-permute-done.14.refs_1_, bf16[16,32,128]{2,1,0:T(8,128)(2,1)S(1)} %collective-permute-done.15.refs_2_, ...), custom_call_target="tpu_custom_call" | custom-call | tf_op jit(solution)/shard_map/lay/pallas_call | solution.py:209
  (56 shorter events, 0.1 us)
Async XLA Ops:
  2.5 1.6 %copy-start = (bf16[256,16,256]{2,1,0:T(8,128)(2,1)S(1)}, bf16[256,16,256]{2,1,0:T(8,128)(2,1)}, u32[]{:S(2)}) copy-start(bf16[256,16,256]{2,1,0:T(8,128)(2,1)} %sig.1) | copy-start | bytes 6291460
  4.1 0.7 copy-start.1
  4.8 0.7 copy-start.2
  5.4 0.7 copy-start.3
  6.1 0.7 copy-start.4
  10.2 53.9 %copy-start.5 = (bf16[528,256]{1,0:T(8,128)(2,1)}, bf16[528,256]{1,0:T(8,128)(2,1)S(1)}, u32[]{:S(2)}) copy-start(bf16[528,256]{1,0:T(8,128)(2,1)S(1)} %get-tuple-element.14.refs_4_) | copy-start | bytes 811012
  10.3 10.9 %collective-permute-start.2 = (bf16[528,256]{1,0:T(8,128)(2,1)S(1)}, bf16[528,256]{1,0:T(8,128)(2,1)S(1)}, u32[]{:S(2)}, u32[]{:S(2)}) collective-permute-start(bf16[528,256]{1,0:T(8,128)(2,1)S(1)} %get-tuple-element.13.refs_0_), channel_id=1, source_target_pairs={{0,8},{4,12},{8,16},{12,20},{16,24},{20,28},{24,0},{28,4},{1,9},{5... | collective-permute-start | bytes 811016 | tf_op jit(solution)/shard_map/ppermute | solution.py:246
  12.8 15.0 %collective-permute-start.1 = (bf16[528,256]{1,0:T(8,128)(2,1)S(1)}, bf16[528,256]{1,0:T(8,128)(2,1)S(1)}, u32[]{:S(2)}, u32[]{:S(2)}) collective-permute-start(bf16[528,256]{1,0:T(8,128)(2,1)S(1)} %get-tuple-element.13.refs_0_), channel_id=1, source_target_pairs={{0,16},{4,20},{8,24},{12,28},{16,0},{20,4},{24,8},{28,12},{1,17},{... | collective-permute-start | bytes 811016 | tf_op jit(solution)/shard_map/ppermute | solution.py:246
  16.1 13.2 %collective-permute-start.8 = (bf16[528,256]{1,0:T(8,128)(2,1)S(1)}, bf16[528,256]{1,0:T(8,128)(2,1)S(1)}, u32[]{:S(2)}, u32[]{:S(2)}) collective-permute-start(bf16[528,256]{1,0:T(8,128)(2,1)S(1)} %get-tuple-element.14.refs_4_), channel_id=1, source_target_pairs={{0,32},{32,64},{64,96},{96,0},{1,33},{33,65},{65,97},{97,1},{2,34}... | collective-permute-start | bytes 811016 | tf_op jit(solution)/shard_map/ppermute | solution.py:245
  17.4 13.7 %collective-permute-start.6 = (bf16[528,256]{1,0:T(8,128)(2,1)S(1)}, bf16[528,256]{1,0:T(8,128)(2,1)S(1)}, u32[]{:S(2)}, u32[]{:S(2)}) collective-permute-start(bf16[528,256]{1,0:T(8,128)(2,1)S(1)} %get-tuple-element.14.refs_4_), channel_id=1, source_target_pairs={{0,64},{32,96},{64,0},{96,32},{1,65},{33,97},{65,1},{97,33},{2,66}... | collective-permute-start | bytes 811016 | tf_op jit(solution)/shard_map/ppermute | solution.py:245
  20.0 13.2 %collective-permute-start.4 = (bf16[528,256]{1,0:T(8,128)(2,1)S(1)}, bf16[528,256]{1,0:T(8,128)(2,1)S(1)}, u32[]{:S(2)}, u32[]{:S(2)}) collective-permute-start(bf16[528,256]{1,0:T(8,128)(2,1)S(1)} %get-tuple-element.14.refs_4_), channel_id=1, source_target_pairs={{0,96},{32,0},{64,32},{96,64},{1,97},{33,1},{65,33},{97,65},{2,98}... | collective-permute-start | bytes 811016 | tf_op jit(solution)/shard_map/ppermute | solution.py:245
  21.1 43.1 %copy-start.7 = (bf16[528,256]{1,0:T(8,128)(2,1)}, bf16[528,256]{1,0:T(8,128)(2,1)S(1)}, u32[]{:S(2)}) copy-start(bf16[528,256]{1,0:T(8,128)(2,1)S(1)} %collective-permute-done.2.refs_3_) | copy-start | bytes 811012
  21.1 15.0 %collective-permute-start = (bf16[528,256]{1,0:T(8,128)(2,1)S(1)}, bf16[528,256]{1,0:T(8,128)(2,1)S(1)}, u32[]{:S(2)}, u32[]{:S(2)}) collective-permute-start(bf16[528,256]{1,0:T(8,128)(2,1)S(1)} %get-tuple-element.13.refs_0_), channel_id=1, source_target_pairs={{0,24},{4,28},{8,0},{12,4},{16,8},{20,12},{24,16},{28,20},{1,25},{... | collective-permute-start | bytes 811016 | tf_op jit(solution)/shard_map/ppermute | solution.py:246
  27.8 24.1 %copy-start.9 = (bf16[528,256]{1,0:T(8,128)(2,1)}, bf16[528,256]{1,0:T(8,128)(2,1)S(1)}, u32[]{:S(2)}) copy-start(bf16[528,256]{1,0:T(8,128)(2,1)S(1)} %collective-permute-done.1.refs_2_) | copy-start | bytes 811012
  27.8 8.4 %collective-permute-start.3 = (bf16[528,256]{1,0:T(8,128)(2,1)S(1)}, bf16[528,256]{1,0:T(8,128)(2,1)S(1)}, u32[]{:S(2)}, u32[]{:S(2)}) collective-permute-start(bf16[528,256]{1,0:T(8,128)(2,1)S(1)} %get-tuple-element.14.refs_4_), channel_id=1, source_target_pairs={{0,4},{4,0},{8,12},{12,8},{16,20},{20,16},{24,28},{28,24},{1,5},{5... | collective-permute-start | bytes 811016 | tf_op jit(solution)/shard_map/ppermute | solution.py:241
  29.3 22.6 %copy-start.12 = (bf16[528,256]{1,0:T(8,128)(2,1)}, bf16[528,256]{1,0:T(8,128)(2,1)S(1)}, u32[]{:S(2)}) copy-start(bf16[528,256]{1,0:T(8,128)(2,1)S(1)} %collective-permute-done.8.refs_10_) | copy-start | bytes 811012
  29.3 6.8 %collective-permute-start.9 = (bf16[528,256]{1,0:T(8,128)(2,1)S(1)}, bf16[528,256]{1,0:T(8,128)(2,1)S(1)}, u32[]{:S(2)}, u32[]{:S(2)}) collective-permute-start(bf16[528,256]{1,0:T(8,128)(2,1)S(1)} %collective-permute-done.8.refs_10_), channel_id=1, source_target_pairs={{0,4},{4,0},{8,12},{12,8},{16,20},{20,16},{24,28},{28,24},{1,5},{5... | collective-permute-start | bytes 811016 | tf_op jit(solution)/shard_map/ppermute | solution.py:241
  31.1 5.9 %collective-permute-start.7 = (bf16[528,256]{1,0:T(8,128)(2,1)S(1)}, bf16[528,256]{1,0:T(8,128)(2,1)S(1)}, u32[]{:S(2)}, u32[]{:S(2)}) collective-permute-start(bf16[528,256]{1,0:T(8,128)(2,1)S(1)} %collective-permute-done.6.refs_8_), channel_id=1, source_target_pairs={{0,4},{4,0},{8,12},{12,8},{16,20},{20,16},{24,28},{28,24},{1,5},{5... | collective-permute-start | bytes 811016 | tf_op jit(solution)/shard_map/ppermute | solution.py:241
  33.2 4.5 %collective-permute-start.5 = (bf16[528,256]{1,0:T(8,128)(2,1)S(1)}, bf16[528,256]{1,0:T(8,128)(2,1)}, u32[]{:S(2)}, u32[]{:S(2)}) collective-permute-start(bf16[528,256]{1,0:T(8,128)(2,1)S(1)} %collective-permute-done.4.refs_6_), channel_id=1, source_target_pairs={{0,4},{4,0},{8,12},{12,8},{16,20},{20,16},{24,28},{28,24},{1,5},{5... | collective-permute-start | bytes 811016 | tf_op jit(solution)/shard_map/ppermute | solution.py:241
  36.1 11.6 %copy-start.21 = (bf16[528,256]{1,0:T(8,128)(2,1)}, bf16[528,256]{1,0:T(8,128)(2,1)S(1)}, u32[]{:S(2)}) copy-start(bf16[528,256]{1,0:T(8,128)(2,1)S(1)} %collective-permute-done.refs_1_) | copy-start | bytes 811012
  36.2 11.6 %copy-start.24 = (bf16[528,256]{1,0:T(8,128)(2,1)}, bf16[528,256]{1,0:T(8,128)(2,1)S(1)}, u32[]{:S(2)}) copy-start(bf16[528,256]{1,0:T(8,128)(2,1)S(1)} %collective-permute-done.3.refs_5_) | copy-start | bytes 811012
  36.2 0.9 copy-start.28
  37.0 0.7 copy-start.32
  37.7 1.0 copy-start.29
  38.7 1.0 copy-start.33
  39.6 12.2 %copy-start.30 = (bf16[528,256]{1,0:T(8,128)(2,1)S(1)}, bf16[528,256]{1,0:T(8,128)(2,1)}, u32[]{:S(2)}) copy-start(bf16[528,256]{1,0:T(8,128)(2,1)} %copy-done.28) | copy-start | bytes 811012
  39.6 12.2 %copy-start.34 = (bf16[528,256]{1,0:T(8,128)(2,1)S(1)}, bf16[528,256]{1,0:T(8,128)(2,1)}, u32[]{:S(2)}) copy-start(bf16[528,256]{1,0:T(8,128)(2,1)} %copy-done.32) | copy-start | bytes 811012
  47.7 0.7 copy-start.15
  48.4 0.7 copy-start.18
  49.1 45.8 %collective-permute-start.10 = (bf16[18,128,128]{2,1,0:T(8,128)(2,1)S(1)}, bf16[18,128,128]{2,1,0:T(8,128)(2,1)S(1)}, u32[]{:S(2)}, u32[]{:S(2)}) collective-permute-start(bf16[18,128,128]{2,1,0:T(8,128)(2,1)S(1)} %pair.5), channel_id=1, source_target_pairs={{0,2},{1,3},{2,0},{3,1},{4,6},{5,7},{6,4},{7,5},{8,10},{9,11},{10,... | collective-permute-start | bytes 1769480 | tf_op jit(solution)/shard_map/ppermute | solution.py:258
  51.9 1.0 copy-start.16
  52.9 1.0 copy-start.19
  53.8 1.0 copy-start.22
  54.8 1.0 copy-start.25
  55.7 8.5 %copy-start.26 = (bf16[528,256]{1,0:T(8,128)(2,1)S(1)}, bf16[528,256]{1,0:T(8,128)(2,1)}, u32[]{:S(2)}) copy-start(bf16[528,256]{1,0:T(8,128)(2,1)} %copy-done.24) | copy-start | bytes 811012
  63.8 31.2 %collective-permute-start.11 = (bf16[18,128,128]{2,1,0:T(8,128)(2,1)S(1)}, bf16[18,128,128]{2,1,0:T(8,128)(2,1)S(1)}, u32[]{:S(2)}, u32[]{:S(2)}) collective-permute-start(bf16[18,128,128]{2,1,0:T(8,128)(2,1)S(1)} %pair.6), channel_id=1, source_target_pairs={{0,1},{1,2},{2,3},{3,0},{4,5},{5,6},{6,7},{7,4},{8,9},{9,10},{10,1... | collective-permute-start | bytes 1769480 | tf_op jit(solution)/shard_map/ppermute | solution.py:258
  64.2 1.0 copy-start.10
  65.1 1.0 copy-start.13
  75.1 19.9 %collective-permute-start.12 = (bf16[18,128,128]{2,1,0:T(8,128)(2,1)}, bf16[18,128,128]{2,1,0:T(8,128)(2,1)S(1)}, u32[]{:S(2)}, u32[]{:S(2)}) collective-permute-start(bf16[18,128,128]{2,1,0:T(8,128)(2,1)} %pair.7), channel_id=1, source_target_pairs={{0,3},{1,0},{2,1},{3,2},{4,7},{5,4},{6,5},{7,6},{8,11},{9,8},{10,9... | collective-permute-start | bytes 1769480 | tf_op jit(solution)/shard_map/ppermute | solution.py:258
  77.5 1.0 copy-start.6
  78.5 1.0 copy-start.8
  79.4 1.0 copy-start.11
  80.4 1.0 copy-start.14
  81.3 1.0 copy-start.17
  82.3 1.0 copy-start.20
  83.2 1.0 copy-start.23
  84.2 1.0 copy-start.27
  85.1 1.0 copy-start.31
  86.1 1.0 copy-start.35
  96.1 10.9 %collective-permute-start.13 = (bf16[16,32,128]{2,1,0:T(8,128)(2,1)S(1)}, bf16[16,32,128]{2,1,0:T(8,128)(2,1)S(1)}, u32[]{:S(2)}, u32[]{:S(2)}) collective-permute-start(bf16[16,32,128]{2,1,0:T(8,128)(2,1)S(1)} %get-tuple-element.17), channel_id=1, source_target_pairs={{0,0},{4,8},{8,16},{12,24},{16,4},{20,12},{24,20},{28,28},{1,1},{5... | collective-permute-start | bytes 393224 | tf_op jit(solution)/shard_map/ppermute | solution.py:275
  98.7 8.3 %collective-permute-start.14 = (bf16[16,32,128]{2,1,0:T(8,128)(2,1)S(1)}, bf16[16,32,128]{2,1,0:T(8,128)(2,1)S(1)}, u32[]{:S(2)}, u32[]{:S(2)}) collective-permute-start(bf16[16,32,128]{2,1,0:T(8,128)(2,1)S(1)} %get-tuple-element.18), channel_id=1, source_target_pairs={{0,8},{4,16},{8,24},{12,0},{16,12},{20,20},{24,28},{28,4},{1,9},{5... | collective-permute-start | bytes 393224 | tf_op jit(solution)/shard_map/ppermute | solution.py:275
  103.2 5.7 %collective-permute-start.15 = (bf16[16,32,128]{2,1,0:T(8,128)(2,1)S(1)}, bf16[16,32,128]{2,1,0:T(8,128)(2,1)S(1)}, u32[]{:S(2)}, u32[]{:S(2)}) collective-permute-start(bf16[16,32,128]{2,1,0:T(8,128)(2,1)S(1)} %get-tuple-element.19), channel_id=1, source_target_pairs={{0,16},{4,24},{8,0},{12,8},{16,20},{20,28},{24,4},{28,12},{1,17},{... | collective-permute-start | bytes 393224 | tf_op jit(solution)/shard_map/ppermute | solution.py:275
  103.3 8.3 %collective-permute-start.16 = (bf16[16,32,128]{2,1,0:T(8,128)(2,1)S(1)}, bf16[16,32,128]{2,1,0:T(8,128)(2,1)S(1)}, u32[]{:S(2)}, u32[]{:S(2)}) collective-permute-start(bf16[16,32,128]{2,1,0:T(8,128)(2,1)S(1)} %get-tuple-element.20), channel_id=1, source_target_pairs={{0,24},{4,0},{8,8},{12,16},{16,28},{20,4},{24,12},{28,20},{1,25},{... | collective-permute-start | bytes 393224 | tf_op jit(solution)/shard_map/ppermute | solution.py:275

commit v2 on v1

--- a/solution.py
+++ b/solution.py
@@ -25,19 +25,12 @@
 
 def project_kernel(sig, mask, gain, shift, w_left, b_left, w_right, b_right, left, right, wide, cols, turn):
     half = sig.shape[0]
-
-    @pl.when(pl.program_id(0) == 0)
-    def _():
-        turn[...] = jnp.zeros_like(turn)
-        turn[0:256, 0:HID] = w_left[...].astype(F32)
-        turn[0:256, HID : 2 * HID] = w_right[...].astype(F32)
-        turn[256:384, 0:HID] = jnp.broadcast_to(b_left[...], (128, HID))
-        turn[256:384, HID : 2 * HID] = jnp.broadcast_to(b_right[...], (128, HID))
-
-    weights = jnp.transpose(turn[0:256, :])[0 : 2 * HID, :].astype(BF16)
-    bias = jnp.transpose(turn[256:384, :])[0 : 2 * HID, :]
-    turn[384 : 384 + half, 0:RES] = mask[...].astype(F32)
-    presence = jnp.transpose(turn[384 : 384 + half, :])[0:RES, :]
+    turn[...] = jnp.zeros_like(turn)
+    turn[:, 0:HID] = jnp.broadcast_to(b_left[...], (128, HID))
+    turn[:, HID : 2 * HID] = jnp.broadcast_to(b_right[...], (128, HID))
+    bias = jnp.transpose(turn[...])[0 : 2 * HID, :]
+    weights = jnp.concatenate([w_left[...], w_right[...]], axis=0)
+    presence = mask[...].astype(F32)
 
     flat = sig[...].astype(F32).reshape(half * RES, 256)
     wide[0] = flat[:, 0:128]
@@ -58,8 +51,8 @@
         cols[r * HID : (r + 1) * HID, :] = both[HID : 2 * HID]
     for d in range(HID):
         right[d * RES : (d + 1) * RES, :] = cols[pl.ds(d, RES, stride=HID), :].astype(BF16)
-    left[SHARD:ROWS, :] = presence.astype(BF16)
-    right[SHARD:ROWS, :] = presence.astype(BF16)
+    left[SHARD:ROWS, :] = mask[...]
+    right[SHARD:ROWS, :] = mask[...]
 
 
 def project(sig, mask, gain, shift, w_left, b_left, w_right, b_right):
@@ -71,12 +64,12 @@
         grid=(steps,),
         in_specs=[
             pl.BlockSpec((half, RES, 256), lambda s: (s, 0, 0)),
-            pl.BlockSpec((half, RES), lambda s: (s, 0)),
+            pl.BlockSpec((RES, half), lambda s: (0, s)),
             whole((1, 256)),
             whole((1, 256)),
-            whole((256, HID)),
+            whole((HID, 256)),
             whole((1, HID)),
-            whole((256, HID)),
+            whole((HID, 256)),
             whole((1, HID)),
         ],
         out_specs=[pl.BlockSpec((ROWS, half), lambda s: (0, s))] * 2,
@@ -84,11 +77,32 @@
         scratch_shapes=[
             pltpu.VMEM((2, half * RES, 128), F32),
             pltpu.VMEM((SHARD, half), F32),
-            pltpu.VMEM((384 + half, 128), F32),
+            pltpu.VMEM((128, 128), F32),
         ],
-        compiler_params=pltpu.CompilerParams(vmem_limit_bytes=40 * 2**20),
+        compiler_params=pltpu.CompilerParams(vmem_limit_bytes=56 * 2**20),
         name="project",
     )(sig, mask, gain, shift, w_left, b_left, w_right, b_right)
+
+
+def order_kernel(w_out, mix, rows, sorted_rows):
+    rows[...] = w_out[...].astype(F32)
+    for d in range(HID):
+        sorted_rows[d * HID : (d + 1) * HID, :] = rows[pl.ds(d, HID, stride=HID), :]
+    for b in range(8):
+        mix[:, b * 128 : (b + 1) * 128] = jnp.transpose(sorted_rows[b * 128 : (b + 1) * 128, :]).astype(BF16)
+
+
+def order(w_out):
+    vmem = pl.BlockSpec(memory_space=pltpu.VMEM)
+    return pl.pallas_call(
+        order_kernel,
+        in_specs=[vmem],
+        out_specs=vmem,
+        out_shape=jax.ShapeDtypeStruct((128, HID * HID), BF16),
+        scratch_shapes=[pltpu.VMEM((HID * HID, 128), F32)] * 2,
+        compiler_params=pltpu.CompilerParams(vmem_limit_bytes=8 * 2**20),
+        name="order",
+    )(w_out)
 
 
 def pair_kernel(own, place, *refs):
@@ -104,7 +118,7 @@
         def _():
             chosen[...] = lefts[t][...]
 
-    @pl.loop(0, HID // 2)
+    @pl.loop(0, HID // 2, unroll=True)
     def _(step):
         parts = []
         for dd in range(2):
@@ -120,7 +134,7 @@
                     i * HID : (i + 1) * HID, dd * 128 : (dd + 1) * 128
                 ]
 
-    @pl.loop(0, RES // 2)
+    @pl.loop(0, RES // 2, unroll=True)
     def _(pair):
         mixed = dot(mix[...], outer[pair], NN)
         for ii in range(2):
@@ -155,7 +169,7 @@
             pltpu.VMEM((RES // 2, HID * HID, 256), BF16),
             pltpu.VMEM((ROWS, SEQ), BF16),
         ],
-        compiler_params=pltpu.CompilerParams(vmem_limit_bytes=40 * 2**20),
+        compiler_params=pltpu.CompilerParams(vmem_limit_bytes=16 * 2**20),
         cost_estimate=pl.CostEstimate(
             flops=2 * SHARD * SHARD * 8 * SEQ + 2 * 128 * 16 * 128 * 1024,
             bytes_accessed=5 * 2**20,
@@ -165,22 +179,20 @@
     )(place, *lefts, *rights, mix)
 
 
-def settle_kernel(place, mine, count, a, b, c, *refs):
-    pieces, inverse = refs[0:4], refs[4]
+def settle_kernel(place, mine, count, a, b, c, pieces, inverse):
     total = count[...]
     for ref in (a, b, c):
         total = total + (ref[RES].astype(F32) + ref[RES + 1].astype(F32))
     inverse[...] = 1.0 / jnp.maximum(total, 1.0)
-    for u in range(4):
+    for p in range(4):
         for h in range(2):
-            start = pl.multiple_of(place[u * 2 + h], RES)
-            rows = pl.ds(start, RES)
+            rows = pl.ds(pl.multiple_of(place[p * 2 + h], RES), RES)
             factor = inverse[rows, :]
             for i in range(RES):
                 value = mine[i, rows, :]
                 for ref in (a, b, c):
                     value = value + ref[i, rows, :].astype(F32)
-                pieces[u][i, h * RES : (h + 1) * RES, :] = (value * factor[:, i : i + 1]).astype(BF16)
+                pieces[p, i, h * RES : (h + 1) * RES, :] = (value * factor[:, i : i + 1]).astype(BF16)
 
 
 def settle(place, mine, count, a, b, c):
@@ -188,32 +200,33 @@
     return pl.pallas_call(
         settle_kernel,
         in_specs=[pl.BlockSpec(memory_space=pltpu.SMEM)] + [vmem] * 5,
-        out_specs=[vmem] * 4,
-        out_shape=[jax.ShapeDtypeStruct((RES, 2 * RES, 128), BF16)] * 4,
+        out_specs=vmem,
+        out_shape=jax.ShapeDtypeStruct((4, RES, 2 * RES, 128), BF16),
         scratch_shapes=[pltpu.VMEM((128, 128), F32)],
-        compiler_params=pltpu.CompilerParams(vmem_limit_bytes=40 * 2**20),
+        compiler_params=pltpu.CompilerParams(vmem_limit_bytes=8 * 2**20),
         name="settle",
     )(place, mine, count, a, b, c)
 
 
-def lay_kernel(place, *refs):
-    out = refs[4]
-    for u in range(4):
-        at = pl.multiple_of(place[u * 2] * RES, RES)
-        start = pl.multiple_of(place[u * 2 + 1] * 2 * RES, 2 * RES)
-        out[pl.ds(at, RES), pl.ds(start, 2 * RES), :] = refs[u][...]
-
-
-def lay(place, pieces):
+def lay_kernel(place, kept, given, out):
+    mine = pl.ds(pl.multiple_of(place[0], RES), RES)
+    theirs = pl.ds(pl.multiple_of(RES - place[0], RES), RES)
+    for half in range(2):
+        span = slice(half * 2 * RES, (half + 1) * 2 * RES)
+        out[mine, span, :] = kept[half]
+        out[theirs, span, :] = given[half]
+
+
+def lay(place, kept, given):
     vmem = pl.BlockSpec(memory_space=pltpu.VMEM)
     return pl.pallas_call(
         lay_kernel,
-        in_specs=[pl.BlockSpec(memory_space=pltpu.SMEM)] + [vmem] * 4,
+        in_specs=[pl.BlockSpec(memory_space=pltpu.SMEM)] + [vmem] * 2,
         out_specs=vmem,
         out_shape=jax.ShapeDtypeStruct((2 * RES, 4 * RES, 128), BF16),
-        compiler_params=pltpu.CompilerParams(vmem_limit_bytes=40 * 2**20),
+        compiler_params=pltpu.CompilerParams(vmem_limit_bytes=8 * 2**20),
         name="lay",
-    )(place, *pieces)
+    )(place, kept, given)
 
 
 def shift_pairs(n, step):
@@ -224,19 +237,18 @@
     x = lax.axis_index("depth")
     y = lax.axis_index("row")
     col = lax.axis_index("col")
-    z, core = col // 2, col % 2
+    z, core = col >> 1, col & 1
 
     left, right = project(
         sig,
-        mask,
+        mask.T,
         gain.reshape(1, 256),
         shift.reshape(1, 256),
-        w_left,
+        w_left.T,
         b_left.reshape(1, HID),
-        w_right,
+        w_right.T,
         b_right.reshape(1, HID),
     )
-    mix = w_out.reshape(HID, HID, 128).transpose(2, 1, 0).reshape(128, HID * HID)
 
     flip = lambda v: lax.ppermute(v, "col", [(s, s ^ 1) for s in range(8)])
     rights = {0: right}
@@ -244,13 +256,14 @@
     for t in (2, 1, 3):
         rights[t] = lax.ppermute(right, "row", shift_pairs(4, -t))
         lefts[t] = lax.ppermute(left, "col", shift_pairs(8, -2 * t))
+    mix, rights[2] = lax.optimization_barrier((order(w_out), rights[2]))
     columns = []
     for t in range(4):
         columns += [rights[t], flip(rights[t])]
     rows = [lefts[t] for t in range(4)]
 
     def quarter(k):
-        return ((x + k - z) % 4).astype(jnp.int32).reshape(1)
+        return ((x + k - z) & 3).astype(jnp.int32).reshape(1)
 
     got = {}
     for k in (2, 1, 3):
@@ -258,24 +271,17 @@
         got[k] = lax.ppermute(part, "depth", shift_pairs(4, k))
     mine, count = pair(True, quarter(0), rows, columns, mix)
 
-    slot = 2 * (z % 2) + core
     spots = []
-    for u in range(4):
-        t = ((slot + u) % 4 - y) % 4
+    for p in range(4):
+        t = (p + 2 * core - y) & 3
         for h in range(2):
             spots.append(t * 32 + (h ^ core) * 16)
     pieces = settle(jnp.stack(spots).astype(jnp.int32), mine, count, got[2], got[1], got[3])
-
-    seats, landed = [], []
-    for u in range(4):
-        pairs = []
-        for s in range(8):
-            sz, sc = s // 2, s % 2
-            pairs.append((s, 2 * ((2 * (sz % 2) + sc + u) % 4) + sz // 2))
-        landed.append(lax.ppermute(pieces[u], "col", pairs))
-        seat = (z - u) % 4
-        seats += [seat % 2, seat // 2]
-    return lay(jnp.stack(seats).astype(jnp.int32), landed)
+    landed = lax.all_to_all(
+        pieces, "col", 0, 0, axis_index_groups=[[0, 2, 4, 6], [5, 7, 1, 3]], tiled=True
+    )
+    given = flip(landed[2:4])
+    return lay((core * RES).astype(jnp.int32).reshape(1), landed[0:2], given)
 
 
 def solution(mesh):

time: 114 us -> 81.6 us (0.72)
  Pallas kernels: 39 us -> 16.2 us
  blocking collectives: 0 us -> 10.2 us
  local copies, waits for them, and re-layouts: 29.9 us -> 22.3 us
  starting transfers between devices: 31.9 us -> 25.7 us
  waiting for transfers between devices: 11.7 us -> 6.22 us
    pallas_call x4, Pallas kernels: 33 us -> 8.58 us  [pair(): pl.pallas_call(functools.partial(pair_kernel, own), in_specs=[pl.BlockSpe...]
    ppermute x4 -> x0, starting transfers between devices: 10.7 us -> none  [per_device(): landed.append(lax.ppermute(pieces[u], 'col', pairs))]
    all_to_all x0 -> x1, blocking collectives: none -> 10.2 us  [per_device(): lax.all_to_all(pieces, 'col', 0, 0, axis_index_groups=[[0, 2, 4, 6], [5,...]
    unnamed x75 -> x74, local copies, waits for them, and re-layouts: 26.9 us -> 22.1 us
    ppermute x4 -> x0, waiting for transfers between devices: 4.5 us -> none  [per_device(): landed.append(lax.ppermute(pieces[u], 'col', pairs))]
    ppermute x4 -> x5, starting transfers between devices: 3.8 us -> 6.97 us  [per_device(): flip = lambda v: lax.ppermute(v, 'col', [(s, s ^ 1) for s in range(8)])]
    ppermute x4 -> x5, waiting for transfers between devices: 0.01 us -> 2.58 us  [per_device(): flip = lambda v: lax.ppermute(v, 'col', [(s, s ^ 1) for s in range(8)])]
    ppermute x3, waiting for transfers between devices: 5.54 us -> 3.63 us  [per_device(): lefts[t] = lax.ppermute(left, 'col', shift_pairs(8, -2 * t))]
  transfers between devices with their start and end apart: 17 -> 14, of which waited for: 4 -> 4; matrix products, arithmetic and copies ran while one was open for 3% -> 0% of each run, Pallas kernels for 22% -> 9%
where the time goes in v2:
time: 81.6 us; the launch traced here: 80.8 us
  starting transfers between devices  25.7 us (31%)
  local copies, waits for them, and re-layouts  22.3 us (27%)
  Pallas kernels  16.2 us (20%)
  blocking collectives  10.2 us (12%)
  waiting for transfers between devices  6.22 us (8%)
    unnamed x74, local copies, waits for them, and re-layouts  22.1 us
    all_to_all x1, blocking collectives, per_device(): lax.all_to_all(pieces, 'col', 0, 0, axis_index_groups=[[0, 2, 4, 6], [5,...  10.2 us
    pallas_call x4, Pallas kernels, pair(): pl.pallas_call(functools.partial(pair_kernel, own), in_specs=[pl.BlockSpe...  8.58 us
    ppermute x5, starting transfers between devices, per_device(): flip = lambda v: lax.ppermute(v, 'col', [(s, s ^ 1) for s in range(8)])  6.97 us
    ppermute x3, starting transfers between devices, per_device(): lefts[t] = lax.ppermute(left, 'col', shift_pairs(8, -2 * t))  6.8 us
    ppermute x3, starting transfers between devices, per_device(): rights[t] = lax.ppermute(right, 'row', shift_pairs(4, -t))  6.42 us
    ppermute x3, starting transfers between devices, per_device(): got[k] = lax.ppermute(part, 'depth', shift_pairs(4, k))  5.5 us
    pallas_call x1, Pallas kernels, project(): pl.pallas_call(project_kernel, grid=(steps,), in_specs=[pl.BlockSpec((hal...  5.29 us
  transfers between devices with their start and end apart: 14, of which 4 were waited for; matrix products, arithmetic and copies ran while one was open for 0% of the time, Pallas kernels for 9%

profile of v2, /device:TPU:1, one launch (start us, length us, event | category | flops | bytes accessed | tf_op | source)
XLA Modules:
  0.0 80.8 jit_solution(8920197539773584969)
XLA Ops:
  0.0 5.3 %project.1 = (bf16[528,256]{1,0:T(8,128)(2,1)}, bf16[528,256]{1,0:T(8,128)(2,1)}) custom-call(bf16[256,16,256]{2,1,0:T(8,128)(2,1)} %sig.1, bf16[16,256]{1,0:T(8,128)(2,1)} %bitcast.22, f32[1,256]{1,0:T(1,128)} %bitcast.23, f32[1,256]{1,0:T(1,128)} %bitcast.24, bf16[32,256]{1,0:T(8,128)(2,1)} %bitcast.20, f32[1,32]{1,0:T(1,128)} %bitcast.25, ...), custom_call_target="tpu_custom_call" | custom-call | tf_op jit(solution)/shard_map/project/pallas_call | solution.py:62
  5.3 3.7 %collective-permute-start.6 = (bf16[528,256]{1,0:T(8,128)(2,1)}, bf16[528,256]{1,0:T(8,128)(2,1)S(1)}, u32[]{:S(2)}, u32[]{:S(2)}) collective-permute-start(bf16[528,256]{1,0:T(8,128)(2,1)} %get-tuple-element.12.refs_4_), channel_id=1, source_target_pairs={{0,64},{32,96},{64,0},{96,32},{1,65},{33,97},{65,1},{97,33},{2,66}... | collective-permute-start | bytes 811016 | tf_op jit(solution)/shard_map/ppermute | solution.py:257
  9.0 1.6 %collective-permute-start.2 = (bf16[528,256]{1,0:T(8,128)(2,1)}, bf16[528,256]{1,0:T(8,128)(2,1)S(1)}, u32[]{:S(2)}, u32[]{:S(2)}) collective-permute-start(bf16[528,256]{1,0:T(8,128)(2,1)} %get-tuple-element.11.refs_0_), channel_id=1, source_target_pairs={{0,8},{4,12},{8,16},{12,20},{16,24},{20,28},{24,0},{28,4},{1,9},{5... | collective-permute-start | bytes 811016 | tf_op jit(solution)/shard_map/ppermute | solution.py:258
  10.7 3.3 %collective-permute-start.1 = (bf16[528,256]{1,0:T(8,128)(2,1)}, bf16[528,256]{1,0:T(8,128)(2,1)S(1)}, u32[]{:S(2)}, u32[]{:S(2)}) collective-permute-start(bf16[528,256]{1,0:T(8,128)(2,1)} %get-tuple-element.11.refs_0_), channel_id=1, source_target_pairs={{0,16},{4,20},{8,24},{12,28},{16,0},{20,4},{24,8},{28,12},{1,17},{... | collective-permute-start | bytes 811016 | tf_op jit(solution)/shard_map/ppermute | solution.py:258
  14.0 0.4 collective-permute-start.8
  14.4 2.3 %collective-permute-start.4 = (bf16[528,256]{1,0:T(8,128)(2,1)}, bf16[528,256]{1,0:T(8,128)(2,1)S(1)}, u32[]{:S(2)}, u32[]{:S(2)}) collective-permute-start(bf16[528,256]{1,0:T(8,128)(2,1)} %get-tuple-element.12.refs_4_), channel_id=1, source_target_pairs={{0,96},{32,0},{64,32},{96,64},{1,97},{33,1},{65,33},{97,65},{2,98}... | collective-permute-start | bytes 811016 | tf_op jit(solution)/shard_map/ppermute | solution.py:257
  16.7 0.0 copy-done
  16.7 0.4 order.1.refs_12_
  17.1 0.0 collective-permute-done.6.refs_8_
  17.1 1.9 %collective-permute-start = (bf16[528,256]{1,0:T(8,128)(2,1)}, bf16[528,256]{1,0:T(8,128)(2,1)S(1)}, u32[]{:S(2)}, u32[]{:S(2)}) collective-permute-start(bf16[528,256]{1,0:T(8,128)(2,1)} %get-tuple-element.11.refs_0_), channel_id=1, source_target_pairs={{0,24},{4,28},{8,0},{12,4},{16,8},{20,12},{24,16},{28,20},{1,25},{... | collective-permute-start | bytes 811016 | tf_op jit(solution)/shard_map/ppermute | solution.py:258
  18.9 0.0 collective-permute-done.2.refs_3_
  19.0 3.0 %collective-permute-start.3 = (bf16[528,256]{1,0:T(8,128)(2,1)}, bf16[528,256]{1,0:T(8,128)(2,1)S(1)}, u32[]{:S(2)}, u32[]{:S(2)}) collective-permute-start(bf16[528,256]{1,0:T(8,128)(2,1)} %get-tuple-element.12.refs_4_), channel_id=1, source_target_pairs={{0,4},{4,0},{8,12},{12,8},{16,20},{20,16},{24,28},{28,24},{1,5},{5... | collective-permute-start | bytes 811016 | tf_op jit(solution)/shard_map/ppermute | solution.py:253
  21.9 3.6 %collective-permute-done.1.refs_2_ = bf16[528,256]{1,0:T(8,128)(2,1)S(1)} collective-permute-done((bf16[528,256]{1,0:T(8,128)(2,1)}, bf16[528,256]{1,0:T(8,128)(2,1)S(1)}, u32[]{:S(2)}, u32[]{:S(2)}) %collective-permute-start.1) | collective-permute-done | bytes 270368 | tf_op jit(solution)/shard_map/ppermute | solution.py:258
  25.6 1.9 %collective-permute-start.7 = (bf16[528,256]{1,0:T(8,128)(2,1)S(1)}, bf16[528,256]{1,0:T(8,128)(2,1)S(1)}, u32[]{:S(2)}, u32[]{:S(2)}) collective-permute-start(bf16[528,256]{1,0:T(8,128)(2,1)S(1)} %collective-permute-done.6.refs_8_), channel_id=1, source_target_pairs={{0,4},{4,0},{8,12},{12,8},{16,20},{20,16},{24,28},{28,24},{1,5},{5... | collective-permute-start | bytes 811016 | tf_op jit(solution)/shard_map/ppermute | solution.py:253
  27.4 0.0 collective-permute-done.8.refs_10_
  27.4 0.1 collective-permute-start.9
  27.5 0.0 collective-permute-done.4.refs_6_
  27.5 0.4 collective-permute-start.5
  27.9 0.0 collective-permute-done.refs_1_
  27.9 0.0 collective-permute-done.3.refs_5_
  27.9 1.0 %collective-permute-done.9.refs_11_ = bf16[528,256]{1,0:T(8,128)(2,1)S(1)} collective-permute-done((bf16[528,256]{1,0:T(8,128)(2,1)S(1)}, bf16[528,256]{1,0:T(8,128)(2,1)S(1)}, u32[]{:S(2)}, u32[]{:S(2)}) %collective-permute-start.9) | collective-permute-done | bytes 270368 | tf_op jit(solution)/shard_map/ppermute | solution.py:253
  29.0 0.0 collective-permute-done.7.refs_9_
  29.0 0.4 collective-permute-done.5.refs_7_
  29.4 0.7 copy-done.33
  30.1 1.0 %copy-done.1 = bf16[528,256]{1,0:T(8,128)(2,1)S(1)} copy-done((bf16[528,256]{1,0:T(8,128)(2,1)S(1)}, bf16[528,256]{1,0:T(8,128)(2,1)}, u32[]{:S(2)}) %copy-start.1) | copy-done | bytes 270360
  31.0 1.0 %copy-done.3 = bf16[528,256]{1,0:T(8,128)(2,1)S(1)} copy-done((bf16[528,256]{1,0:T(8,128)(2,1)S(1)}, bf16[528,256]{1,0:T(8,128)(2,1)}, u32[]{:S(2)}) %copy-start.3) | copy-done | bytes 270360
  32.0 1.0 %copy-done.34 = bf16[528,256]{1,0:T(8,128)(2,1)S(1)} copy-done((bf16[528,256]{1,0:T(8,128)(2,1)S(1)}, bf16[528,256]{1,0:T(8,128)(2,1)}, u32[]{:S(2)}) %copy-start.34) | copy-done | bytes 270360
  32.9 1.9 %pair.5 = bf16[18,128,128]{2,1,0:T(8,128)(2,1)S(1)} custom-call(s32[1]{0:T(128)} %bitcast.17.place, bf16[528,256]{1,0:T(8,128)(2,1)S(1)} %copy-done.1, bf16[528,256]{1,0:T(8,128)(2,1)S(1)} %collective-permute-done.refs_1_, bf16[528,256]{1,0:T(8,128)(2,1)S(1)} %collective-permute-done.1.refs_2_, bf16[528,256]{1,0:T(8,128)(2,1)S(1)} %collective-permute-done.2.refs_3_, ...), custom_call_target="tpu_custom_call" | custom-call | flops 1610612736 | bytes 5242880 | tf_op jit(solution)/shard_map/pair/pallas_call | solution.py:163
  34.9 0.7 copy-done.18
  35.6 0.7 copy-done.22
  36.3 2.8 %collective-permute-start.10 = (bf16[18,128,128]{2,1,0:T(8,128)(2,1)S(1)}, bf16[18,128,128]{2,1,0:T(8,128)(2,1)S(1)}, u32[]{:S(2)}, u32[]{:S(2)}) collective-permute-start(bf16[18,128,128]{2,1,0:T(8,128)(2,1)S(1)} %pair.5), channel_id=1, source_target_pairs={{0,2},{1,3},{2,0},{3,1},{4,6},{5,7},{6,4},{7,5},{8,10},{9,11},{10,... | collective-permute-start | bytes 1769480 | tf_op jit(solution)/shard_map/ppermute | solution.py:271
  39.1 0.0 copy-done.9
  39.1 0.9 %copy-done.19 = bf16[528,256]{1,0:T(8,128)(2,1)S(1)} copy-done((bf16[528,256]{1,0:T(8,128)(2,1)S(1)}, bf16[528,256]{1,0:T(8,128)(2,1)}, u32[]{:S(2)}) %copy-start.19) | copy-done | bytes 270360
  40.0 1.0 %copy-done.23 = bf16[528,256]{1,0:T(8,128)(2,1)S(1)} copy-done((bf16[528,256]{1,0:T(8,128)(2,1)S(1)}, bf16[528,256]{1,0:T(8,128)(2,1)}, u32[]{:S(2)}) %copy-start.23) | copy-done | bytes 270360
  41.0 1.0 %copy-done.27 = bf16[528,256]{1,0:T(8,128)(2,1)S(1)} copy-done((bf16[528,256]{1,0:T(8,128)(2,1)S(1)}, bf16[528,256]{1,0:T(8,128)(2,1)}, u32[]{:S(2)}) %copy-start.27) | copy-done | bytes 270360
  41.9 1.0 %copy-done.30 = bf16[528,256]{1,0:T(8,128)(2,1)S(1)} copy-done((bf16[528,256]{1,0:T(8,128)(2,1)S(1)}, bf16[528,256]{1,0:T(8,128)(2,1)}, u32[]{:S(2)}) %copy-start.30) | copy-done | bytes 270360
  42.9 1.9 %pair.6 = bf16[18,128,128]{2,1,0:T(8,128)(2,1)S(1)} custom-call(s32[1]{0:T(128)} %bitcast.18.place, bf16[528,256]{1,0:T(8,128)(2,1)S(1)} %copy-done.1, bf16[528,256]{1,0:T(8,128)(2,1)S(1)} %copy-done.19, bf16[528,256]{1,0:T(8,128)(2,1)S(1)} %collective-permute-done.1.refs_2_, bf16[528,256]{1,0:T(8,128)(2,1)S(1)} %collective-permute-done.2.refs_3_, ...), custom_call_target="tpu_custom_call" | custom-call | flops 1610612736 | bytes 5242880 | tf_op jit(solution)/shard_map/pair/pallas_call | solution.py:163
  44.8 0.4 collective-permute-start.11
  45.2 0.9 %copy-done.10 = bf16[528,256]{1,0:T(8,128)(2,1)S(1)} copy-done((bf16[528,256]{1,0:T(8,128)(2,1)S(1)}, bf16[528,256]{1,0:T(8,128)(2,1)}, u32[]{:S(2)}) %copy-start.10) | copy-done | bytes 270360
  46.2 1.0 %copy-done.13 = bf16[528,256]{1,0:T(8,128)(2,1)S(1)} copy-done((bf16[528,256]{1,0:T(8,128)(2,1)S(1)}, bf16[528,256]{1,0:T(8,128)(2,1)}, u32[]{:S(2)}) %copy-start.13) | copy-done | bytes 270360
  47.1 1.0 %copy-done.16 = bf16[528,256]{1,0:T(8,128)(2,1)S(1)} copy-done((bf16[528,256]{1,0:T(8,128)(2,1)S(1)}, bf16[528,256]{1,0:T(8,128)(2,1)}, u32[]{:S(2)}) %copy-start.16) | copy-done | bytes 270360
  48.1 2.8 %pair.7 = bf16[18,128,128]{2,1,0:T(8,128)(2,1)} custom-call(s32[1]{0:T(128)} %bitcast.19.place, bf16[528,256]{1,0:T(8,128)(2,1)S(1)} %copy-done.1, bf16[528,256]{1,0:T(8,128)(2,1)S(1)} %copy-done.20, bf16[528,256]{1,0:T(8,128)(2,1)S(1)} %copy-done.10, bf16[528,256]{1,0:T(8,128)(2,1)S(1)} %collective-permute-done.2.refs_3_, bf16[528,256]{1,0:T(8,128)(2,1)S(1)} %copy-done.3, ...), custom_call_target="tpu_custom_call" | custom-call | flops 1610612736 | bytes 5242880 | tf_op jit(solution)/shard_map/pair/pallas_call | solution.py:163
  50.8 2.4 %collective-permute-start.12 = (bf16[18,128,128]{2,1,0:T(8,128)(2,1)}, bf16[18,128,128]{2,1,0:T(8,128)(2,1)S(1)}, u32[]{:S(2)}, u32[]{:S(2)}) collective-permute-start(bf16[18,128,128]{2,1,0:T(8,128)(2,1)} %pair.7), channel_id=1, source_target_pairs={{0,3},{1,0},{2,1},{3,2},{4,7},{5,4},{6,5},{7,6},{8,11},{9,8},{10,9... | collective-permute-start | bytes 1769480 | tf_op jit(solution)/shard_map/ppermute | solution.py:271
  53.2 0.1 stack.35.place
  53.3 1.0 %copy-done.4 = bf16[528,256]{1,0:T(8,128)(2,1)S(1)} copy-done((bf16[528,256]{1,0:T(8,128)(2,1)S(1)}, bf16[528,256]{1,0:T(8,128)(2,1)}, u32[]{:S(2)}) %copy-start.4) | copy-done | bytes 270360
  54.3 1.0 %copy-done.6 = bf16[528,256]{1,0:T(8,128)(2,1)S(1)} copy-done((bf16[528,256]{1,0:T(8,128)(2,1)S(1)}, bf16[528,256]{1,0:T(8,128)(2,1)}, u32[]{:S(2)}) %copy-start.6) | copy-done | bytes 270360
  55.2 1.0 %copy-done.8 = bf16[528,256]{1,0:T(8,128)(2,1)S(1)} copy-done((bf16[528,256]{1,0:T(8,128)(2,1)S(1)}, bf16[528,256]{1,0:T(8,128)(2,1)}, u32[]{:S(2)}) %copy-start.8) | copy-done | bytes 270360
  56.2 1.0 %copy-done.11 = bf16[528,256]{1,0:T(8,128)(2,1)S(1)} copy-done((bf16[528,256]{1,0:T(8,128)(2,1)S(1)}, bf16[528,256]{1,0:T(8,128)(2,1)}, u32[]{:S(2)}) %copy-start.11) | copy-done | bytes 270360
  57.1 1.0 %copy-done.14 = bf16[528,256]{1,0:T(8,128)(2,1)S(1)} copy-done((bf16[528,256]{1,0:T(8,128)(2,1)S(1)}, bf16[528,256]{1,0:T(8,128)(2,1)}, u32[]{:S(2)}) %copy-start.14) | copy-done | bytes 270360
  58.1 1.0 %copy-done.17 = bf16[528,256]{1,0:T(8,128)(2,1)S(1)} copy-done((bf16[528,256]{1,0:T(8,128)(2,1)S(1)}, bf16[528,256]{1,0:T(8,128)(2,1)}, u32[]{:S(2)}) %copy-start.17) | copy-done | bytes 270360
  59.0 1.0 %copy-done.21 = bf16[528,256]{1,0:T(8,128)(2,1)S(1)} copy-done((bf16[528,256]{1,0:T(8,128)(2,1)S(1)}, bf16[528,256]{1,0:T(8,128)(2,1)}, u32[]{:S(2)}) %copy-start.21) | copy-done | bytes 270360
  60.0 1.0 %copy-done.25 = bf16[528,256]{1,0:T(8,128)(2,1)S(1)} copy-done((bf16[528,256]{1,0:T(8,128)(2,1)S(1)}, bf16[528,256]{1,0:T(8,128)(2,1)}, u32[]{:S(2)}) %copy-start.25) | copy-done | bytes 270360
  60.9 1.0 %copy-done.28 = bf16[528,256]{1,0:T(8,128)(2,1)S(1)} copy-done((bf16[528,256]{1,0:T(8,128)(2,1)S(1)}, bf16[528,256]{1,0:T(8,128)(2,1)}, u32[]{:S(2)}) %copy-start.28) | copy-done | bytes 270360
  61.9 1.0 %copy-done.32 = bf16[528,256]{1,0:T(8,128)(2,1)S(1)} copy-done((bf16[528,256]{1,0:T(8,128)(2,1)S(1)}, bf16[528,256]{1,0:T(8,128)(2,1)}, u32[]{:S(2)}) %copy-start.32) | copy-done | bytes 270360
  62.8 1.0 %copy-done.36 = bf16[528,256]{1,0:T(8,128)(2,1)S(1)} copy-done((bf16[528,256]{1,0:T(8,128)(2,1)S(1)}, bf16[528,256]{1,0:T(8,128)(2,1)}, u32[]{:S(2)}) %copy-start.36) | copy-done | bytes 270360
  63.8 2.0 %pair.4 = (f32[16,128,128]{2,1,0:T(8,128)S(1)}, f32[128,128]{1,0:T(8,128)S(1)}) custom-call(s32[1]{0:T(128)} %bitcast.9.place, bf16[528,256]{1,0:T(8,128)(2,1)S(1)} %copy-done.2, bf16[528,256]{1,0:T(8,128)(2,1)S(1)} %copy-done.21, bf16[528,256]{1,0:T(8,128)(2,1)S(1)} %copy-done.11, bf16[528,256]{1,0:T(8,128)(2,1)S(1)} %copy-done.8, ...), custom_call_target="tpu_custom_call" | custom-call | flops 1610612736 | bytes 5242880 | tf_op jit(solution)/shard_map/pair/pallas_call | solution.py:163
  65.8 0.0 collective-permute-done.10.a
  65.8 0.0 collective-permute-done.11.b
  65.8 0.0 collective-permute-done.12.c
  65.8 1.1 %settle.1 = bf16[4,16,32,128]{3,2,1,0:T(8,128)(2,1)S(1)} custom-call(s32[8]{0:T(128)S(1)} %stack.35.place, f32[16,128,128]{2,1,0:T(8,128)S(1)} %get-tuple-element.15.mine, f32[128,128]{1,0:T(8,128)S(1)} %get-tuple-element.16.count, bf16[18,128,128]{2,1,0:T(8,128)(2,1)S(1)} %collective-permute-done.10.a, bf16[18,128,128]{2,1,0:T(8,128)(2,1)S(1)} %collective-permute-done.11.b, ...), custom_call_target="tpu_custom_call" | custom-call | tf_op jit(solution)/shard_map/settle/pallas_call | solution.py:200
  66.9 10.2 %all_to_all.5 = bf16[4,16,32,128]{3,2,1,0:T(8,128)(2,1)S(1)} all-to-all(bf16[4,16,32,128]{3,2,1,0:T(8,128)(2,1)S(1)} %settle.1), channel_id=1, replica_groups={{0,8,16,24},{20,28,4,12},{1,9,17,25},{21,29,5,13},{2,10,18,26},{22,30,6..., dimensions={0} | all-to-all | bytes 1048576 | tf_op jit(solution)/shard_map/all_to_all | solution.py:280
  77.2 1.6 %collective-permute-start.13 = (bf16[2,16,32,128]{3,2,1,0:T(8,128)(2,1)S(1)}, bf16[2,16,32,128]{3,2,1,0:T(8,128)(2,1)S(1)}, u32[]{:S(2)}, u32[]{:S(2)}) collective-permute-start(bf16[2,16,32,128]{3,2,1,0:T(8,128)(2,1)S(1)} %get-tuple-element.17), channel_id=1, source_target_pairs={{0,4},{4,0},{8,12},{12,8},{16,20},{20,16},{24,28},{28,24},{1,5},{5... | collective-permute-start | bytes 786440 | tf_op jit(solution)/shard_map/ppermute | solution.py:253
  78.8 1.2 %collective-permute-done.13.given = bf16[2,16,32,128]{3,2,1,0:T(8,128)(2,1)S(1)} collective-permute-done((bf16[2,16,32,128]{3,2,1,0:T(8,128)(2,1)S(1)}, bf16[2,16,32,128]{3,2,1,0:T(8,128)(2,1)S(1)}, u32[]{:S(2)}, u32[]{:S(2)}) %collective-permute-start.13) | collective-permute-done | bytes 262176 | tf_op jit(solution)/shard_map/ppermute | solution.py:253
  80.0 0.8 %lay.1 = bf16[32,64,128]{2,1,0:T(8,128)(2,1)} custom-call(s32[1]{0:T(128)} %bitcast.place, bf16[2,16,32,128]{3,2,1,0:T(8,128)(2,1)S(1)} %get-tuple-element.18.kept, bf16[2,16,32,128]{3,2,1,0:T(8,128)(2,1)S(1)} %collective-permute-done.13.given), custom_call_target="tpu_custom_call" | custom-call | tf_op jit(solution)/shard_map/lay/pallas_call | solution.py:222
  (49 shorter events, 0.1 us)
Async XLA Ops:
  0.0 16.7 %copy-start = (bf16[1024,128]{1,0:T(8,128)(2,1)S(1)}, bf16[1024,128]{1,0:T(8,128)(2,1)}, u32[]{:S(2)}) copy-start(bf16[1024,128]{1,0:T(8,128)(2,1)} %w_out.1) | copy-start | bytes 786436
  5.3 11.8 %collective-permute-start.6 = (bf16[528,256]{1,0:T(8,128)(2,1)}, bf16[528,256]{1,0:T(8,128)(2,1)S(1)}, u32[]{:S(2)}, u32[]{:S(2)}) collective-permute-start(bf16[528,256]{1,0:T(8,128)(2,1)} %get-tuple-element.12.refs_4_), channel_id=1, source_target_pairs={{0,64},{32,96},{64,0},{96,32},{1,65},{33,97},{65,1},{97,33},{2,66}... | collective-permute-start | bytes 811016 | tf_op jit(solution)/shard_map/ppermute | solution.py:257
  9.0 9.9 %collective-permute-start.2 = (bf16[528,256]{1,0:T(8,128)(2,1)}, bf16[528,256]{1,0:T(8,128)(2,1)S(1)}, u32[]{:S(2)}, u32[]{:S(2)}) collective-permute-start(bf16[528,256]{1,0:T(8,128)(2,1)} %get-tuple-element.11.refs_0_), channel_id=1, source_target_pairs={{0,8},{4,12},{8,16},{12,20},{16,24},{20,28},{24,0},{28,4},{1,9},{5... | collective-permute-start | bytes 811016 | tf_op jit(solution)/shard_map/ppermute | solution.py:258
  10.7 14.9 %collective-permute-start.1 = (bf16[528,256]{1,0:T(8,128)(2,1)}, bf16[528,256]{1,0:T(8,128)(2,1)S(1)}, u32[]{:S(2)}, u32[]{:S(2)}) collective-permute-start(bf16[528,256]{1,0:T(8,128)(2,1)} %get-tuple-element.11.refs_0_), channel_id=1, source_target_pairs={{0,16},{4,20},{8,24},{12,28},{16,0},{20,4},{24,8},{28,12},{1,17},{... | collective-permute-start | bytes 811016 | tf_op jit(solution)/shard_map/ppermute | solution.py:258
  14.0 13.4 %collective-permute-start.8 = (bf16[528,256]{1,0:T(8,128)(2,1)}, bf16[528,256]{1,0:T(8,128)(2,1)S(1)}, u32[]{:S(2)}, u32[]{:S(2)}) collective-permute-start(bf16[528,256]{1,0:T(8,128)(2,1)} %get-tuple-element.12.refs_4_), channel_id=1, source_target_pairs={{0,32},{32,64},{64,96},{96,0},{1,33},{33,65},{65,97},{97,1},{2,34}... | collective-permute-start | bytes 811016 | tf_op jit(solution)/shard_map/ppermute | solution.py:257
  14.4 13.1 %collective-permute-start.4 = (bf16[528,256]{1,0:T(8,128)(2,1)}, bf16[528,256]{1,0:T(8,128)(2,1)S(1)}, u32[]{:S(2)}, u32[]{:S(2)}) collective-permute-start(bf16[528,256]{1,0:T(8,128)(2,1)} %get-tuple-element.12.refs_4_), channel_id=1, source_target_pairs={{0,96},{32,0},{64,32},{96,64},{1,97},{33,1},{65,33},{97,65},{2,98}... | collective-permute-start | bytes 811016 | tf_op jit(solution)/shard_map/ppermute | solution.py:257
  17.1 28.1 %copy-start.5 = (bf16[528,256]{1,0:T(8,128)(2,1)}, bf16[528,256]{1,0:T(8,128)(2,1)S(1)}, u32[]{:S(2)}) copy-start(bf16[528,256]{1,0:T(8,128)(2,1)S(1)} %collective-permute-done.6.refs_8_) | copy-start | bytes 811012
  17.1 10.9 %collective-permute-start = (bf16[528,256]{1,0:T(8,128)(2,1)}, bf16[528,256]{1,0:T(8,128)(2,1)S(1)}, u32[]{:S(2)}, u32[]{:S(2)}) collective-permute-start(bf16[528,256]{1,0:T(8,128)(2,1)} %get-tuple-element.11.refs_0_), channel_id=1, source_target_pairs={{0,24},{4,28},{8,0},{12,4},{16,8},{20,12},{24,16},{28,20},{1,25},{... | collective-permute-start | bytes 811016 | tf_op jit(solution)/shard_map/ppermute | solution.py:258
  19.0 26.3 %copy-start.7 = (bf16[528,256]{1,0:T(8,128)(2,1)}, bf16[528,256]{1,0:T(8,128)(2,1)S(1)}, u32[]{:S(2)}) copy-start(bf16[528,256]{1,0:T(8,128)(2,1)S(1)} %collective-permute-done.2.refs_3_) | copy-start | bytes 811012
  19.0 9.0 %collective-permute-start.3 = (bf16[528,256]{1,0:T(8,128)(2,1)}, bf16[528,256]{1,0:T(8,128)(2,1)S(1)}, u32[]{:S(2)}, u32[]{:S(2)}) collective-permute-start(bf16[528,256]{1,0:T(8,128)(2,1)} %get-tuple-element.12.refs_4_), channel_id=1, source_target_pairs={{0,4},{4,0},{8,12},{12,8},{16,20},{20,16},{24,28},{28,24},{1,5},{5... | collective-permute-start | bytes 811016 | tf_op jit(solution)/shard_map/ppermute | solution.py:253
  25.6 13.5 %copy-start.9 = (bf16[528,256]{1,0:T(8,128)(2,1)}, bf16[528,256]{1,0:T(8,128)(2,1)S(1)}, u32[]{:S(2)}) copy-start(bf16[528,256]{1,0:T(8,128)(2,1)S(1)} %collective-permute-done.1.refs_2_) | copy-start | bytes 811012
  25.6 3.4 %collective-permute-start.7 = (bf16[528,256]{1,0:T(8,128)(2,1)S(1)}, bf16[528,256]{1,0:T(8,128)(2,1)S(1)}, u32[]{:S(2)}, u32[]{:S(2)}) collective-permute-start(bf16[528,256]{1,0:T(8,128)(2,1)S(1)} %collective-permute-done.6.refs_8_), channel_id=1, source_target_pairs={{0,4},{4,0},{8,12},{12,8},{16,20},{20,16},{24,28},{28,24},{1,5},{5... | collective-permute-start | bytes 811016 | tf_op jit(solution)/shard_map/ppermute | solution.py:253
  27.4 11.6 %copy-start.12 = (bf16[528,256]{1,0:T(8,128)(2,1)}, bf16[528,256]{1,0:T(8,128)(2,1)S(1)}, u32[]{:S(2)}) copy-start(bf16[528,256]{1,0:T(8,128)(2,1)S(1)} %collective-permute-done.8.refs_10_) | copy-start | bytes 811012
  27.4 1.6 %collective-permute-start.9 = (bf16[528,256]{1,0:T(8,128)(2,1)S(1)}, bf16[528,256]{1,0:T(8,128)(2,1)S(1)}, u32[]{:S(2)}, u32[]{:S(2)}) collective-permute-start(bf16[528,256]{1,0:T(8,128)(2,1)S(1)} %collective-permute-done.8.refs_10_), channel_id=1, source_target_pairs={{0,4},{4,0},{8,12},{12,8},{16,20},{20,16},{24,28},{28,24},{1,5},{5... | collective-permute-start | bytes 811016 | tf_op jit(solution)/shard_map/ppermute | solution.py:253
  27.5 11.5 %copy-start.15 = (bf16[528,256]{1,0:T(8,128)(2,1)}, bf16[528,256]{1,0:T(8,128)(2,1)S(1)}, u32[]{:S(2)}) copy-start(bf16[528,256]{1,0:T(8,128)(2,1)S(1)} %collective-permute-done.4.refs_6_) | copy-start | bytes 811012
  27.5 1.8 %collective-permute-start.5 = (bf16[528,256]{1,0:T(8,128)(2,1)S(1)}, bf16[528,256]{1,0:T(8,128)(2,1)S(1)}, u32[]{:S(2)}, u32[]{:S(2)}) collective-permute-start(bf16[528,256]{1,0:T(8,128)(2,1)S(1)} %collective-permute-done.4.refs_6_), channel_id=1, source_target_pairs={{0,4},{4,0},{8,12},{12,8},{16,20},{20,16},{24,28},{28,24},{1,5},{5... | collective-permute-start | bytes 811016 | tf_op jit(solution)/shard_map/ppermute | solution.py:253
  29.0 5.9 %copy-start.29 = (bf16[528,256]{1,0:T(8,128)(2,1)}, bf16[528,256]{1,0:T(8,128)(2,1)S(1)}, u32[]{:S(2)}) copy-start(bf16[528,256]{1,0:T(8,128)(2,1)S(1)} %collective-permute-done.9.refs_11_) | copy-start | bytes 811012
  29.0 5.9 %copy-start.26 = (bf16[528,256]{1,0:T(8,128)(2,1)}, bf16[528,256]{1,0:T(8,128)(2,1)S(1)}, u32[]{:S(2)}) copy-start(bf16[528,256]{1,0:T(8,128)(2,1)S(1)} %collective-permute-done.7.refs_9_) | copy-start | bytes 811012
  29.4 0.7 copy-start.33
  30.1 1.0 %copy-start.1 = (bf16[528,256]{1,0:T(8,128)(2,1)S(1)}, bf16[528,256]{1,0:T(8,128)(2,1)}, u32[]{:S(2)}) copy-start(bf16[528,256]{1,0:T(8,128)(2,1)} %get-tuple-element.11.refs_0_) | copy-start | bytes 811012
  31.0 1.0 %copy-start.3 = (bf16[528,256]{1,0:T(8,128)(2,1)S(1)}, bf16[528,256]{1,0:T(8,128)(2,1)}, u32[]{:S(2)}) copy-start(bf16[528,256]{1,0:T(8,128)(2,1)} %get-tuple-element.12.refs_4_) | copy-start | bytes 811012
  32.0 1.0 %copy-start.34 = (bf16[528,256]{1,0:T(8,128)(2,1)S(1)}, bf16[528,256]{1,0:T(8,128)(2,1)}, u32[]{:S(2)}) copy-start(bf16[528,256]{1,0:T(8,128)(2,1)} %copy-done.33) | copy-start | bytes 811012
  32.9 6.1 %copy-start.35 = (bf16[528,256]{1,0:T(8,128)(2,1)S(1)}, bf16[528,256]{1,0:T(8,128)(2,1)}, u32[]{:S(2)}) copy-start(bf16[528,256]{1,0:T(8,128)(2,1)} %copy-done.33) | copy-start | bytes 811012
  34.9 0.7 copy-start.18
  35.6 0.7 copy-start.22
  36.3 29.5 %collective-permute-start.10 = (bf16[18,128,128]{2,1,0:T(8,128)(2,1)S(1)}, bf16[18,128,128]{2,1,0:T(8,128)(2,1)S(1)}, u32[]{:S(2)}, u32[]{:S(2)}) collective-permute-start(bf16[18,128,128]{2,1,0:T(8,128)(2,1)S(1)} %pair.5), channel_id=1, source_target_pairs={{0,2},{1,3},{2,0},{3,1},{4,6},{5,7},{6,4},{7,5},{8,10},{9,11},{10,... | collective-permute-start | bytes 1769480 | tf_op jit(solution)/shard_map/ppermute | solution.py:271
  39.1 1.0 %copy-start.19 = (bf16[528,256]{1,0:T(8,128)(2,1)S(1)}, bf16[528,256]{1,0:T(8,128)(2,1)}, u32[]{:S(2)}) copy-start(bf16[528,256]{1,0:T(8,128)(2,1)} %copy-done.18) | copy-start | bytes 811012
  40.0 1.0 %copy-start.23 = (bf16[528,256]{1,0:T(8,128)(2,1)S(1)}, bf16[528,256]{1,0:T(8,128)(2,1)}, u32[]{:S(2)}) copy-start(bf16[528,256]{1,0:T(8,128)(2,1)} %copy-done.22) | copy-start | bytes 811012
  41.0 1.0 %copy-start.27 = (bf16[528,256]{1,0:T(8,128)(2,1)S(1)}, bf16[528,256]{1,0:T(8,128)(2,1)}, u32[]{:S(2)}) copy-start(bf16[528,256]{1,0:T(8,128)(2,1)} %copy-done.26) | copy-start | bytes 811012
  41.9 1.0 %copy-start.30 = (bf16[528,256]{1,0:T(8,128)(2,1)S(1)}, bf16[528,256]{1,0:T(8,128)(2,1)}, u32[]{:S(2)}) copy-start(bf16[528,256]{1,0:T(8,128)(2,1)} %copy-done.29) | copy-start | bytes 811012
  42.9 2.3 %copy-start.20 = (bf16[528,256]{1,0:T(8,128)(2,1)S(1)}, bf16[528,256]{1,0:T(8,128)(2,1)}, u32[]{:S(2)}) copy-start(bf16[528,256]{1,0:T(8,128)(2,1)} %copy-done.18) | copy-start | bytes 811012
  42.9 2.3 %copy-start.24 = (bf16[528,256]{1,0:T(8,128)(2,1)S(1)}, bf16[528,256]{1,0:T(8,128)(2,1)}, u32[]{:S(2)}) copy-start(bf16[528,256]{1,0:T(8,128)(2,1)} %copy-done.22) | copy-start | bytes 811012
  42.9 2.3 %copy-start.31 = (bf16[528,256]{1,0:T(8,128)(2,1)S(1)}, bf16[528,256]{1,0:T(8,128)(2,1)}, u32[]{:S(2)}) copy-start(bf16[528,256]{1,0:T(8,128)(2,1)} %copy-done.29) | copy-start | bytes 811012
  44.8 20.9 %collective-permute-start.11 = (bf16[18,128,128]{2,1,0:T(8,128)(2,1)S(1)}, bf16[18,128,128]{2,1,0:T(8,128)(2,1)S(1)}, u32[]{:S(2)}, u32[]{:S(2)}) collective-permute-start(bf16[18,128,128]{2,1,0:T(8,128)(2,1)S(1)} %pair.6), channel_id=1, source_target_pairs={{0,1},{1,2},{2,3},{3,0},{4,5},{5,6},{6,7},{7,4},{8,9},{9,10},{10,1... | collective-permute-start | bytes 1769480 | tf_op jit(solution)/shard_map/ppermute | solution.py:271
  45.2 1.0 %copy-start.10 = (bf16[528,256]{1,0:T(8,128)(2,1)S(1)}, bf16[528,256]{1,0:T(8,128)(2,1)}, u32[]{:S(2)}) copy-start(bf16[528,256]{1,0:T(8,128)(2,1)} %copy-done.9) | copy-start | bytes 811012
  46.2 1.0 %copy-start.13 = (bf16[528,256]{1,0:T(8,128)(2,1)S(1)}, bf16[528,256]{1,0:T(8,128)(2,1)}, u32[]{:S(2)}) copy-start(bf16[528,256]{1,0:T(8,128)(2,1)} %copy-done.12) | copy-start | bytes 811012
  47.1 1.0 %copy-start.16 = (bf16[528,256]{1,0:T(8,128)(2,1)S(1)}, bf16[528,256]{1,0:T(8,128)(2,1)}, u32[]{:S(2)}) copy-start(bf16[528,256]{1,0:T(8,128)(2,1)} %copy-done.15) | copy-start | bytes 811012
  48.1 5.2 %copy-start.2 = (bf16[528,256]{1,0:T(8,128)(2,1)S(1)}, bf16[528,256]{1,0:T(8,128)(2,1)}, u32[]{:S(2)}) copy-start(bf16[528,256]{1,0:T(8,128)(2,1)} %get-tuple-element.11.refs_0_) | copy-start | bytes 811012
  50.8 14.9 %collective-permute-start.12 = (bf16[18,128,128]{2,1,0:T(8,128)(2,1)}, bf16[18,128,128]{2,1,0:T(8,128)(2,1)S(1)}, u32[]{:S(2)}, u32[]{:S(2)}) collective-permute-start(bf16[18,128,128]{2,1,0:T(8,128)(2,1)} %pair.7), channel_id=1, source_target_pairs={{0,3},{1,0},{2,1},{3,2},{4,7},{5,4},{6,5},{7,6},{8,11},{9,8},{10,9... | collective-permute-start | bytes 1769480 | tf_op jit(solution)/shard_map/ppermute | solution.py:271
  53.3 1.0 %copy-start.4 = (bf16[528,256]{1,0:T(8,128)(2,1)S(1)}, bf16[528,256]{1,0:T(8,128)(2,1)}, u32[]{:S(2)}) copy-start(bf16[528,256]{1,0:T(8,128)(2,1)} %get-tuple-element.12.refs_4_) | copy-start | bytes 811012
  54.3 1.0 %copy-start.6 = (bf16[528,256]{1,0:T(8,128)(2,1)S(1)}, bf16[528,256]{1,0:T(8,128)(2,1)}, u32[]{:S(2)}) copy-start(bf16[528,256]{1,0:T(8,128)(2,1)} %copy-done.5) | copy-start | bytes 811012
  55.2 1.0 %copy-start.8 = (bf16[528,256]{1,0:T(8,128)(2,1)S(1)}, bf16[528,256]{1,0:T(8,128)(2,1)}, u32[]{:S(2)}) copy-start(bf16[528,256]{1,0:T(8,128)(2,1)} %copy-done.7) | copy-start | bytes 811012
  56.2 1.0 %copy-start.11 = (bf16[528,256]{1,0:T(8,128)(2,1)S(1)}, bf16[528,256]{1,0:T(8,128)(2,1)}, u32[]{:S(2)}) copy-start(bf16[528,256]{1,0:T(8,128)(2,1)} %copy-done.9) | copy-start | bytes 811012
  57.1 1.0 %copy-start.14 = (bf16[528,256]{1,0:T(8,128)(2,1)S(1)}, bf16[528,256]{1,0:T(8,128)(2,1)}, u32[]{:S(2)}) copy-start(bf16[528,256]{1,0:T(8,128)(2,1)} %copy-done.12) | copy-start | bytes 811012
  58.1 1.0 %copy-start.17 = (bf16[528,256]{1,0:T(8,128)(2,1)S(1)}, bf16[528,256]{1,0:T(8,128)(2,1)}, u32[]{:S(2)}) copy-start(bf16[528,256]{1,0:T(8,128)(2,1)} %copy-done.15) | copy-start | bytes 811012
  59.0 1.0 %copy-start.21 = (bf16[528,256]{1,0:T(8,128)(2,1)S(1)}, bf16[528,256]{1,0:T(8,128)(2,1)}, u32[]{:S(2)}) copy-start(bf16[528,256]{1,0:T(8,128)(2,1)} %copy-done.18) | copy-start | bytes 811012
  60.0 1.0 %copy-start.25 = (bf16[528,256]{1,0:T(8,128)(2,1)S(1)}, bf16[528,256]{1,0:T(8,128)(2,1)}, u32[]{:S(2)}) copy-start(bf16[528,256]{1,0:T(8,128)(2,1)} %copy-done.22) | copy-start | bytes 811012
  60.9 1.0 %copy-start.28 = (bf16[528,256]{1,0:T(8,128)(2,1)S(1)}, bf16[528,256]{1,0:T(8,128)(2,1)}, u32[]{:S(2)}) copy-start(bf16[528,256]{1,0:T(8,128)(2,1)} %copy-done.26) | copy-start | bytes 811012
  61.9 1.0 %copy-start.32 = (bf16[528,256]{1,0:T(8,128)(2,1)S(1)}, bf16[528,256]{1,0:T(8,128)(2,1)}, u32[]{:S(2)}) copy-start(bf16[528,256]{1,0:T(8,128)(2,1)} %copy-done.29) | copy-start | bytes 811012
  62.8 1.0 %copy-start.36 = (bf16[528,256]{1,0:T(8,128)(2,1)S(1)}, bf16[528,256]{1,0:T(8,128)(2,1)}, u32[]{:S(2)}) copy-start(bf16[528,256]{1,0:T(8,128)(2,1)} %copy-done.33) | copy-start | bytes 811012
  77.2 2.8 %collective-permute-start.13 = (bf16[2,16,32,128]{3,2,1,0:T(8,128)(2,1)S(1)}, bf16[2,16,32,128]{3,2,1,0:T(8,128)(2,1)S(1)}, u32[]{:S(2)}, u32[]{:S(2)}) collective-permute-start(bf16[2,16,32,128]{3,2,1,0:T(8,128)(2,1)S(1)} %get-tuple-element.17), channel_id=1, source_target_pairs={{0,4},{4,0},{8,12},{12,8},{16,20},{20,16},{24,28},{28,24},{1,5},{5... | collective-permute-start | bytes 786440 | tf_op jit(solution)/shard_map/ppermute | solution.py:253

commit v3 on v2

--- a/solution.py
+++ b/solution.py
@@ -17,6 +17,8 @@
 HID = 32
 SHARD = RES * HID
 ROWS = SHARD + RES
+WIDE = 8 * RES
+BIG = 56 * 2**20
 
 
 def dot(a, b, dims):
@@ -79,133 +81,153 @@
             pltpu.VMEM((SHARD, half), F32),
             pltpu.VMEM((128, 128), F32),
         ],
-        compiler_params=pltpu.CompilerParams(vmem_limit_bytes=56 * 2**20),
+        compiler_params=pltpu.CompilerParams(vmem_limit_bytes=BIG),
         name="project",
     )(sig, mask, gain, shift, w_left, b_left, w_right, b_right)
 
 
-def order_kernel(w_out, mix, rows, sorted_rows):
+def order_kernel(w_out, left_in, right_in, mix, left, right, rows, sorted_rows):
     rows[...] = w_out[...].astype(F32)
     for d in range(HID):
         sorted_rows[d * HID : (d + 1) * HID, :] = rows[pl.ds(d, HID, stride=HID), :]
     for b in range(8):
         mix[:, b * 128 : (b + 1) * 128] = jnp.transpose(sorted_rows[b * 128 : (b + 1) * 128, :]).astype(BF16)
-
-
-def order(w_out):
+    left[...] = left_in[...]
+    right[...] = right_in[...]
+
+
+def order(w_out, left, right):
     vmem = pl.BlockSpec(memory_space=pltpu.VMEM)
     return pl.pallas_call(
         order_kernel,
-        in_specs=[vmem],
-        out_specs=vmem,
-        out_shape=jax.ShapeDtypeStruct((128, HID * HID), BF16),
+        in_specs=[vmem] * 3,
+        out_specs=[vmem] * 3,
+        out_shape=[jax.ShapeDtypeStruct((128, HID * HID), BF16)] + [jax.ShapeDtypeStruct((ROWS, SEQ), BF16)] * 2,
         scratch_shapes=[pltpu.VMEM((HID * HID, 128), F32)] * 2,
         compiler_params=pltpu.CompilerParams(vmem_limit_bytes=8 * 2**20),
         name="order",
-    )(w_out)
-
-
-def pair_kernel(own, place, *refs):
-    lefts, rights, mix = refs[0:4], refs[4:12], refs[12]
-    if own:
-        out, count, outer, chosen = refs[13:]
+    )(w_out, left, right)
+
+
+def pair_kernel(first, place, *refs):
+    if first:
+        lefts, rights, mix, out, packed, outer = refs[0:4], refs[4:12], *refs[12:]
+        for t in range(4):
+            packed[t] = lefts[t][...]
+        for v in range(8):
+            packed[4 + v] = rights[v][...]
+        outs = [out]
     else:
-        out, outer, chosen = refs[13:]
-    which = place[0]
-    for t in range(4):
-
-        @pl.when(which == t)
-        def _():
-            chosen[...] = lefts[t][...]
-
-    @pl.loop(0, HID // 2, unroll=True)
-    def _(step):
-        parts = []
-        for dd in range(2):
-            start = pl.multiple_of(step * 2 * RES + dd * RES, RES)
-            for ref in rights:
-                parts.append(ref[pl.ds(start, RES), :])
-        block = jnp.concatenate(parts, axis=0)
-        prod = dot(chosen[0:SHARD, :], block, NT).astype(BF16)
-        for dd in range(2):
-            at = pl.multiple_of(step * 2 * HID + dd * HID, HID)
-            for i in range(RES):
-                outer[i // 2, pl.ds(at, HID), (i % 2) * 128 : (i % 2) * 128 + 128] = prod[
-                    i * HID : (i + 1) * HID, dd * 128 : (dd + 1) * 128
-                ]
-
-    @pl.loop(0, RES // 2, unroll=True)
-    def _(pair):
-        mixed = dot(mix[...], outer[pair], NN)
-        for ii in range(2):
-            out[pair * 2 + ii] = jnp.transpose(mixed[:, ii * 128 : (ii + 1) * 128]).astype(out.dtype)
-
-    weights = jnp.concatenate([ref[SHARD:ROWS, :] for ref in rights], axis=0)
-    tally = jnp.concatenate([chosen[SHARD:ROWS, :], jnp.zeros((128 - RES, SEQ), BF16)], axis=0)
-    tally = dot(weights, tally, NT)
-    if own:
-        count[...] = tally
+        packed, mix, *outs, own, count, outer = refs
+
+    def right(v, rows):
+        return rights[v][rows, :] if first else packed[4 + v, rows, :]
+
+    weights = jnp.concatenate([right(v, slice(SHARD, ROWS)) for v in range(8)], axis=0)
+    for q in range(1 if first else 3):
+        which = place[q]
+        rows = packed[which, 0:SHARD, :]
+        for step in range(HID // 2):
+            parts = []
+            for dd in range(2):
+                start = (step * 2 + dd) * RES
+                parts += [right(v, slice(start, start + RES)) for v in range(8)]
+            prod = dot(rows, jnp.concatenate(parts, axis=0), NT).astype(BF16)
+            for dd in range(2):
+                at = (step * 2 + dd) * HID
+                for i in range(RES):
+                    outer[i // 2, at : at + HID, (i % 2) * 128 : (i % 2) * 128 + 128] = prod[
+                        i * HID : (i + 1) * HID, dd * 128 : (dd + 1) * 128
+                    ]
+        for pair in range(RES // 2):
+            mixed = dot(mix[...], outer[pair], NN)
+            for ii in range(2):
+                at = (pair * 2 + ii) * WIDE
+                turned = jnp.transpose(mixed[:, ii * 128 : (ii + 1) * 128])
+                if q < len(outs):
+                    outs[q][at : at + WIDE, :] = turned.astype(BF16)
+                else:
+                    own[at : at + WIDE, :] = turned
+        tally = dot(packed[which, SHARD:ROWS, :], weights, NT)
+        if q < len(outs):
+            high = tally.astype(BF16)
+            outs[q][RES * WIDE : RES * WIDE + RES, :] = high
+            outs[q][RES * WIDE + RES : RES * WIDE + 2 * RES, :] = (tally - high.astype(F32)).astype(BF16)
+        else:
+            count[...] = tally
+
+
+def pair(first, place, *args):
+    vmem = pl.BlockSpec(memory_space=pltpu.VMEM)
+    part = jax.ShapeDtypeStruct((RES * WIDE + 2 * RES, 128), BF16)
+    if first:
+        out_shape = [part, jax.ShapeDtypeStruct((12, ROWS, SEQ), BF16)]
     else:
-        high = tally.astype(BF16)
-        out[RES] = high
-        out[RES + 1] = (tally - high.astype(F32)).astype(BF16)
-
-
-def pair(own, place, lefts, rights, mix):
-    vmem = pl.BlockSpec(memory_space=pltpu.VMEM)
-    if own:
         out_shape = [
-            jax.ShapeDtypeStruct((RES, 128, 128), F32),
-            jax.ShapeDtypeStruct((128, 128), F32),
+            part,
+            part,
+            jax.ShapeDtypeStruct((RES * WIDE, 128), F32),
+            jax.ShapeDtypeStruct((RES, 128), F32),
         ]
-    else:
-        out_shape = [jax.ShapeDtypeStruct((RES + 2, 128, 128), BF16)]
-    return pl.pallas_call(
-        functools.partial(pair_kernel, own),
-        in_specs=[pl.BlockSpec(memory_space=pltpu.SMEM)] + [vmem] * 13,
+    return pl.pallas_call(
+        functools.partial(pair_kernel, first),
+        in_specs=[pl.BlockSpec(memory_space=pltpu.SMEM)] + [vmem] * len(args),
         out_specs=[vmem] * len(out_shape),
         out_shape=out_shape,
-        scratch_shapes=[
-            pltpu.VMEM((RES // 2, HID * HID, 256), BF16),
-            pltpu.VMEM((ROWS, SEQ), BF16),
-        ],
-        compiler_params=pltpu.CompilerParams(vmem_limit_bytes=16 * 2**20),
-        cost_estimate=pl.CostEstimate(
-            flops=2 * SHARD * SHARD * 8 * SEQ + 2 * 128 * 16 * 128 * 1024,
-            bytes_accessed=5 * 2**20,
-            transcendentals=0,
-        ),
-        name="pair",
-    )(place, *lefts, *rights, mix)
-
-
-def settle_kernel(place, mine, count, a, b, c, pieces, inverse):
+        scratch_shapes=[pltpu.VMEM((RES // 2, HID * HID, 256), BF16)],
+        compiler_params=pltpu.CompilerParams(vmem_limit_bytes=12 * 2**20),
+        cost_estimate=pl.CostEstimate(flops=2**28, bytes_accessed=2**16, transcendentals=0),
+        name="pair_first" if first else "pair_rest",
+    )(place, *args)
+
+
+def fold_kernel(mine, count, part, total, total_count):
+    end = RES * WIDE
+    total[...] = mine[...] + part[0:end, :].astype(F32)
+    high, low = part[end : end + RES, :].astype(F32), part[end + RES : end + 2 * RES, :].astype(F32)
+    total_count[...] = count[...] + (high + low)
+
+
+def fold(mine, count, part):
+    vmem = pl.BlockSpec(memory_space=pltpu.VMEM)
+    return pl.pallas_call(
+        fold_kernel,
+        in_specs=[vmem] * 3,
+        out_specs=[vmem] * 2,
+        out_shape=[jax.ShapeDtypeStruct(mine.shape, F32), jax.ShapeDtypeStruct(count.shape, F32)],
+        compiler_params=pltpu.CompilerParams(vmem_limit_bytes=8 * 2**20),
+        name="fold",
+    )(mine, count, part)
+
+
+def settle_kernel(place, mine, count, a, b, pieces, inverse):
+    end = RES * WIDE
     total = count[...]
-    for ref in (a, b, c):
-        total = total + (ref[RES].astype(F32) + ref[RES + 1].astype(F32))
-    inverse[...] = 1.0 / jnp.maximum(total, 1.0)
+    for ref in (a, b):
+        total = total + (ref[end : end + RES, :].astype(F32) + ref[end + RES : end + 2 * RES, :].astype(F32))
+    inverse[0:RES, :] = 1.0 / jnp.maximum(total, 1.0)
+    inverse[...] = jnp.transpose(inverse[...])
     for p in range(4):
         for h in range(2):
-            rows = pl.ds(pl.multiple_of(place[p * 2 + h], RES), RES)
-            factor = inverse[rows, :]
+            start = pl.multiple_of(place[p * 2 + h], RES)
+            factor = inverse[pl.ds(start, RES), :]
             for i in range(RES):
-                value = mine[i, rows, :]
-                for ref in (a, b, c):
-                    value = value + ref[i, rows, :].astype(F32)
+                rows = pl.ds(pl.multiple_of(start + i * WIDE, RES), RES)
+                value = mine[rows, :] + (a[rows, :].astype(F32) + b[rows, :].astype(F32))
                 pieces[p, i, h * RES : (h + 1) * RES, :] = (value * factor[:, i : i + 1]).astype(BF16)
 
 
-def settle(place, mine, count, a, b, c):
+def settle(place, mine, count, a, b):
     vmem = pl.BlockSpec(memory_space=pltpu.VMEM)
     return pl.pallas_call(
         settle_kernel,
-        in_specs=[pl.BlockSpec(memory_space=pltpu.SMEM)] + [vmem] * 5,
+        in_specs=[pl.BlockSpec(memory_space=pltpu.SMEM)] + [vmem] * 4,
         out_specs=vmem,
         out_shape=jax.ShapeDtypeStruct((4, RES, 2 * RES, 128), BF16),
         scratch_shapes=[pltpu.VMEM((128, 128), F32)],
         compiler_params=pltpu.CompilerParams(vmem_limit_bytes=8 * 2**20),
         name="settle",
-    )(place, mine, count, a, b, c)
+    )(place, mine, count, a, b)
 
 
 def lay_kernel(place, kept, given, out):
@@ -256,27 +278,27 @@
     for t in (2, 1, 3):
         rights[t] = lax.ppermute(right, "row", shift_pairs(4, -t))
         lefts[t] = lax.ppermute(left, "col", shift_pairs(8, -2 * t))
-    mix, rights[2] = lax.optimization_barrier((order(w_out), rights[2]))
+    mix, lefts[0], rights[0], rights[2] = lax.optimization_barrier((*order(w_out, left, right), rights[2]))
     columns = []
     for t in range(4):
         columns += [rights[t], flip(rights[t])]
     rows = [lefts[t] for t in range(4)]
 
-    def quarter(k):
-        return ((x + k - z) & 3).astype(jnp.int32).reshape(1)
-
+    quarter = lambda *ks: jnp.stack([(x + k - z) & 3 for k in ks]).astype(jnp.int32)
     got = {}
-    for k in (2, 1, 3):
-        (part,) = pair(False, quarter(k), rows, columns, mix)
-        got[k] = lax.ppermute(part, "depth", shift_pairs(4, k))
-    mine, count = pair(True, quarter(0), rows, columns, mix)
+    part, packed = pair(True, quarter(2), *rows, *columns, mix)
+    got[2] = lax.ppermute(part, "depth", shift_pairs(4, 2))
+    ahead, behind, mine, count = pair(False, quarter(1, 3, 0), packed, mix)
+    got[1] = lax.ppermute(ahead, "depth", shift_pairs(4, 1))
+    got[3] = lax.ppermute(behind, "depth", shift_pairs(4, 3))
 
     spots = []
     for p in range(4):
         t = (p + 2 * core - y) & 3
         for h in range(2):
             spots.append(t * 32 + (h ^ core) * 16)
-    pieces = settle(jnp.stack(spots).astype(jnp.int32), mine, count, got[2], got[1], got[3])
+    mine, count = fold(mine, count, got[2])
+    pieces = settle(jnp.stack(spots).astype(jnp.int32), mine, count, got[1], got[3])
     landed = lax.all_to_all(
         pieces, "col", 0, 0, axis_index_groups=[[0, 2, 4, 6], [5, 7, 1, 3]], tiled=True
     )

time: 81.6 us -> 73.9 us (0.906)
  local copies, waits for them, and re-layouts: 22.3 us -> 2.02 us
  waiting for transfers between devices: 6.22 us -> 19.7 us
  Pallas kernels: 16.2 us -> 17.6 us
  starting transfers between devices: 25.7 us -> 24.3 us
    unnamed x74 -> x4, local copies, waits for them, and re-layouts: 22.1 us -> 1.9 us
    ppermute x3, waiting for transfers between devices: 0.01 us -> 15.6 us  [the longest x1 12.7 us: per_device(): got[1] = lax.ppermute(ahead, 'depth', shift_pairs(4, 1))]
    ppermute x3, waiting for transfers between devices: 3.63 us -> 1.92 us  [per_device(): lefts[t] = lax.ppermute(left, 'col', shift_pairs(8, -2 * t))]
    pallas_call x5 -> x4, Pallas kernels: 8.98 us -> 10.3 us  [the longest x2 8.82 us: pair(): pl.pallas_call(functools.partial(pair_kernel, first), in_specs=[pl.BlockS...]
    ppermute x3, starting transfers between devices: 6.8 us -> 5.74 us  [per_device(): lefts[t] = lax.ppermute(left, 'col', shift_pairs(8, -2 * t))]
  transfers between devices with their start and end apart: 14 -> 14, of which waited for: 4 -> 5; matrix products, arithmetic and copies ran while one was open for 0% -> 0% of each run, Pallas kernels for 9% -> 10%
where the time goes in v3:
time: 73.9 us; the launch traced here: 73.7 us
  starting transfers between devices  24.3 us (33%)
  waiting for transfers between devices  19.7 us (27%)
  Pallas kernels  17.6 us (24%)
  blocking collectives  9.96 us (13%)
  local copies, waits for them, and re-layouts  2.02 us (3%)
    ppermute x1, waiting for transfers between devices, per_device(): got[1] = lax.ppermute(ahead, 'depth', shift_pairs(4, 1))  12.7 us
    all_to_all x1, blocking collectives, per_device(): lax.all_to_all(pieces, 'col', 0, 0, axis_index_groups=[[0, 2, 4, 6], [5,...  9.96 us
    pallas_call x2, Pallas kernels, pair(): pl.pallas_call(functools.partial(pair_kernel, first), in_specs=[pl.BlockS...  8.82 us
    ppermute x5, starting transfers between devices, per_device(): flip = lambda v: lax.ppermute(v, 'col', [(s, s ^ 1) for s in range(8)])  6.64 us
    ppermute x3, starting transfers between devices, per_device(): rights[t] = lax.ppermute(right, 'row', shift_pairs(4, -t))  6.42 us
    ppermute x3, starting transfers between devices, per_device(): lefts[t] = lax.ppermute(left, 'col', shift_pairs(8, -2 * t))  5.74 us
    pallas_call x1, Pallas kernels, project(): pl.pallas_call(project_kernel, grid=(steps,), in_specs=[pl.BlockSpec((hal...  5.27 us
    ppermute x1, waiting for transfers between devices, per_device(): got[2] = lax.ppermute(part, 'depth', shift_pairs(4, 2))  2.89 us
  transfers between devices with their start and end apart: 14, of which 5 were waited for; matrix products, arithmetic and copies ran while one was open for 0% of the time, Pallas kernels for 10%

profile of v3, /device:TPU:1, one launch (start us, length us, event | category | flops | bytes accessed | tf_op | source)
XLA Modules:
  0.0 73.7 jit_solution(6718678315613467069)
XLA Ops:
  0.0 5.3 %project.1 = (bf16[528,256]{1,0:T(8,128)(2,1)}, bf16[528,256]{1,0:T(8,128)(2,1)}) custom-call(bf16[256,16,256]{2,1,0:T(8,128)(2,1)} %sig.1, bf16[16,256]{1,0:T(8,128)(2,1)} %bitcast.22, f32[1,256]{1,0:T(1,128)} %bitcast.23, f32[1,256]{1,0:T(1,128)} %bitcast.24, bf16[32,256]{1,0:T(8,128)(2,1)} %bitcast.20, f32[1,32]{1,0:T(1,128)} %bitcast.25, ...), custom_call_target="tpu_custom_call" | custom-call | tf_op jit(solution)/shard_map/project/pallas_call | solution.py:64
  5.3 3.7 %collective-permute-start = (bf16[528,256]{1,0:T(8,128)(2,1)}, bf16[528,256]{1,0:T(8,128)(2,1)S(1)}, u32[]{:S(2)}, u32[]{:S(2)}) collective-permute-start(bf16[528,256]{1,0:T(8,128)(2,1)} %get-tuple-element.23.right_in), channel_id=1, source_target_pairs={{0,64},{32,96},{64,0},{96,32},{1,65},{33,97},{65,1},{97,33},{2,66}... | collective-permute-start | bytes 811016 | tf_op jit(solution)/shard_map/ppermute | solution.py:279
  9.0 1.6 %collective-permute-start.3 = (bf16[528,256]{1,0:T(8,128)(2,1)}, bf16[528,256]{1,0:T(8,128)(2,1)S(1)}, u32[]{:S(2)}, u32[]{:S(2)}) collective-permute-start(bf16[528,256]{1,0:T(8,128)(2,1)} %get-tuple-element.22.left_in), channel_id=1, source_target_pairs={{0,8},{4,12},{8,16},{12,20},{16,24},{20,28},{24,0},{28,4},{1,9},{5... | collective-permute-start | bytes 811016 | tf_op jit(solution)/shard_map/ppermute | solution.py:280
  10.7 0.4 collective-permute-start.8
  11.0 2.3 %collective-permute-start.5 = (bf16[528,256]{1,0:T(8,128)(2,1)}, bf16[528,256]{1,0:T(8,128)(2,1)S(1)}, u32[]{:S(2)}, u32[]{:S(2)}) collective-permute-start(bf16[528,256]{1,0:T(8,128)(2,1)} %get-tuple-element.23.right_in), channel_id=1, source_target_pairs={{0,96},{32,0},{64,32},{96,64},{1,97},{33,1},{65,33},{97,65},{2,98}... | collective-permute-start | bytes 811016 | tf_op jit(solution)/shard_map/ppermute | solution.py:279
  13.3 3.3 %collective-permute-start.2 = (bf16[528,256]{1,0:T(8,128)(2,1)}, bf16[528,256]{1,0:T(8,128)(2,1)S(1)}, u32[]{:S(2)}, u32[]{:S(2)}) collective-permute-start(bf16[528,256]{1,0:T(8,128)(2,1)} %get-tuple-element.22.left_in), channel_id=1, source_target_pairs={{0,16},{4,20},{8,24},{12,28},{16,0},{20,4},{24,8},{28,12},{1,17},{... | collective-permute-start | bytes 811016 | tf_op jit(solution)/shard_map/ppermute | solution.py:280
  16.6 0.0 copy-start
  16.6 1.0 %copy-done = bf16[528,256]{1,0:T(8,128)(2,1)S(1)} copy-done((bf16[528,256]{1,0:T(8,128)(2,1)S(1)}, bf16[528,256]{1,0:T(8,128)(2,1)}, u32[]{:S(2)}) %copy-start) | copy-done | bytes 270360
  17.6 0.0 copy-start.1
  17.6 0.9 %copy-done.1 = bf16[1024,128]{1,0:T(8,128)(2,1)S(1)} copy-done((bf16[1024,128]{1,0:T(8,128)(2,1)S(1)}, bf16[1024,128]{1,0:T(8,128)(2,1)}, u32[]{:S(2)}) %copy-start.1) | copy-done | bytes 262168
  18.5 1.4 %order.1 = (bf16[128,1024]{1,0:T(8,128)(2,1)S(1)}, bf16[528,256]{1,0:T(8,128)(2,1)S(1)}, bf16[528,256]{1,0:T(8,128)(2,1)S(1)}) custom-call(bf16[1024,128]{1,0:T(8,128)(2,1)S(1)} %copy-done.1, bf16[528,256]{1,0:T(8,128)(2,1)} %get-tuple-element.22.left_in, bf16[528,256]{1,0:T(8,128)(2,1)S(1)} %copy-done), custom_call_target="tpu_custom_call" | custom-call | tf_op jit(solution)/shard_map/order/pallas_call | solution.py:101
  19.9 0.0 collective-permute-done.refs_8_
  19.9 0.8 %collective-permute-start.1 = (bf16[528,256]{1,0:T(8,128)(2,1)}, bf16[528,256]{1,0:T(8,128)(2,1)S(1)}, u32[]{:S(2)}, u32[]{:S(2)}) collective-permute-start(bf16[528,256]{1,0:T(8,128)(2,1)} %get-tuple-element.22.left_in), channel_id=1, source_target_pairs={{0,24},{4,28},{8,0},{12,4},{16,8},{20,12},{24,16},{28,20},{1,25},{... | collective-permute-start | bytes 811016 | tf_op jit(solution)/shard_map/ppermute | solution.py:280
  20.7 0.0 collective-permute-done.3.refs_3_
  20.7 2.4 %collective-permute-start.4 = (bf16[528,256]{1,0:T(8,128)(2,1)S(1)}, bf16[528,256]{1,0:T(8,128)(2,1)S(1)}, u32[]{:S(2)}, u32[]{:S(2)}) collective-permute-start(bf16[528,256]{1,0:T(8,128)(2,1)S(1)} %get-tuple-element.28.refs_4_), channel_id=1, source_target_pairs={{0,4},{4,0},{8,12},{12,8},{16,20},{20,16},{24,28},{28,24},{1,5},{5... | collective-permute-start | bytes 811016 | tf_op jit(solution)/shard_map/ppermute | solution.py:275
  23.1 0.0 collective-permute-done.8.refs_10_
  23.1 0.1 collective-permute-start.9
  23.2 0.0 collective-permute-done.5.refs_6_
  23.2 0.4 collective-permute-start.6
  23.6 1.9 %collective-permute-done.2.refs_2_ = bf16[528,256]{1,0:T(8,128)(2,1)S(1)} collective-permute-done((bf16[528,256]{1,0:T(8,128)(2,1)}, bf16[528,256]{1,0:T(8,128)(2,1)S(1)}, u32[]{:S(2)}, u32[]{:S(2)}) %collective-permute-start.2) | collective-permute-done | bytes 270368 | tf_op jit(solution)/shard_map/ppermute | solution.py:280
  25.5 1.9 %collective-permute-start.7 = (bf16[528,256]{1,0:T(8,128)(2,1)S(1)}, bf16[528,256]{1,0:T(8,128)(2,1)S(1)}, u32[]{:S(2)}, u32[]{:S(2)}) collective-permute-start(bf16[528,256]{1,0:T(8,128)(2,1)S(1)} %collective-permute-done.refs_8_), channel_id=1, source_target_pairs={{0,4},{4,0},{8,12},{12,8},{16,20},{20,16},{24,28},{28,24},{1,5},{5... | collective-permute-start | bytes 811016 | tf_op jit(solution)/shard_map/ppermute | solution.py:275
  27.4 0.1 pad_add_fusion.place
  27.5 0.0 collective-permute-done.1.refs_1_
  27.5 0.0 collective-permute-done.9.refs_11_
  27.5 0.0 collective-permute-done.6.refs_7_
  27.5 0.0 collective-permute-done.4.refs_5_
  27.5 1.1 %collective-permute-done.7.refs_9_ = bf16[528,256]{1,0:T(8,128)(2,1)S(1)} collective-permute-done((bf16[528,256]{1,0:T(8,128)(2,1)S(1)}, bf16[528,256]{1,0:T(8,128)(2,1)S(1)}, u32[]{:S(2)}, u32[]{:S(2)}) %collective-permute-start.7) | collective-permute-done | bytes 270368 | tf_op jit(solution)/shard_map/ppermute | solution.py:275
  28.6 2.9 %pair_first.1 = (bf16[2080,128]{1,0:T(8,128)(2,1)}, bf16[12,528,256]{2,1,0:T(8,128)(2,1)S(1)}) custom-call(s32[1]{0:T(128)} %bitcast.12.place, bf16[528,256]{1,0:T(8,128)(2,1)S(1)} %get-tuple-element.27.refs_0_, bf16[528,256]{1,0:T(8,128)(2,1)S(1)} %collective-permute-done.1.refs_1_, bf16[528,256]{1,0:T(8,128)(2,1)S(1)} %collective-permute-done.2.refs_2_, ...), custom_call_target="tpu_custom_call" | custom-call | flops 268435456 | bytes 65536 | tf_op jit(solution)/shard_map/pair_first/pallas_call | solution.py:172
  31.5 2.7 %collective-permute-start.10 = (bf16[2080,128]{1,0:T(8,128)(2,1)}, bf16[2080,128]{1,0:T(8,128)(2,1)S(1)}, u32[]{:S(2)}, u32[]{:S(2)}) collective-permute-start(bf16[2080,128]{1,0:T(8,128)(2,1)} %get-tuple-element.34), channel_id=1, source_target_pairs={{0,2},{1,3},{2,0},{3,1},{4,6},{5,7},{6,4},{7,5},{8,10},{9,11},{10,... | collective-permute-start | bytes 1597448 | tf_op jit(solution)/shard_map/ppermute | solution.py:290
  34.2 5.9 %pair_rest.1 = (bf16[2080,128]{1,0:T(8,128)(2,1)}, bf16[2080,128]{1,0:T(8,128)(2,1)S(1)}, f32[2048,128]{1,0:T(8,128)S(1)}, f32[16,128]{1,0:T(8,128)S(1)}) custom-call(s32[3]{0:T(128)S(1)} %pad_add_fusion.place, bf16[12,528,256]{2,1,0:T(8,128)(2,1)S(1)} %get-tuple-element.31.refs_0_, bf16[128,1024]{1,0:T(8,128)(2,1)S(1)} %get-tuple-element.30.refs_12_.refs_1_), custom_call_target="tpu_custom_call" | custom-call | flops 268435456 | bytes 65536 | tf_op jit(solution)/shard_map/pair_rest/pallas_call | solution.py:172
  40.1 0.4 collective-permute-start.11
  40.5 2.4 %collective-permute-start.12 = (bf16[2080,128]{1,0:T(8,128)(2,1)S(1)}, bf16[2080,128]{1,0:T(8,128)(2,1)S(1)}, u32[]{:S(2)}, u32[]{:S(2)}) collective-permute-start(bf16[2080,128]{1,0:T(8,128)(2,1)S(1)} %get-tuple-element.38), channel_id=1, source_target_pairs={{0,3},{1,0},{2,1},{3,2},{4,7},{5,4},{6,5},{7,6},{8,11},{9,8},{10,9... | collective-permute-start | bytes 1597448 | tf_op jit(solution)/shard_map/ppermute | solution.py:293
  42.9 0.1 stack.50.place
  43.0 2.9 %collective-permute-done.10.part = bf16[2080,128]{1,0:T(8,128)(2,1)S(1)} collective-permute-done((bf16[2080,128]{1,0:T(8,128)(2,1)}, bf16[2080,128]{1,0:T(8,128)(2,1)S(1)}, u32[]{:S(2)}, u32[]{:S(2)}) %collective-permute-start.10) | collective-permute-done | bytes 532512 | tf_op jit(solution)/shard_map/ppermute | solution.py:290
  45.9 0.1 fold.1
  45.9 12.7 %collective-permute-done.11.a = bf16[2080,128]{1,0:T(8,128)(2,1)S(1)} collective-permute-done((bf16[2080,128]{1,0:T(8,128)(2,1)}, bf16[2080,128]{1,0:T(8,128)(2,1)S(1)}, u32[]{:S(2)}, u32[]{:S(2)}) %collective-permute-start.11) | collective-permute-done | bytes 532512 | tf_op jit(solution)/shard_map/ppermute | solution.py:292
  58.6 0.0 collective-permute-done.12.b
  58.6 1.2 %settle.1 = bf16[4,16,32,128]{3,2,1,0:T(8,128)(2,1)S(1)} custom-call(s32[8]{0:T(128)S(1)} %stack.50.place, f32[2048,128]{1,0:T(8,128)S(1)} %get-tuple-element.35.mine, f32[16,128]{1,0:T(8,128)S(1)} %get-tuple-element.36.count, bf16[2080,128]{1,0:T(8,128)(2,1)S(1)} %collective-permute-done.11.a, bf16[2080,128]{1,0:T(8,128)(2,1)S(1)} %collective-permute-done.12.b), custom_call_target="tpu_custom_call" | custom-call | tf_op jit(solution)/shard_map/settle/pallas_call | solution.py:222
  59.8 10.0 %all_to_all.5 = bf16[4,16,32,128]{3,2,1,0:T(8,128)(2,1)S(1)} all-to-all(bf16[4,16,32,128]{3,2,1,0:T(8,128)(2,1)S(1)} %settle.1), channel_id=1, replica_groups={{0,8,16,24},{20,28,4,12},{1,9,17,25},{21,29,5,13},{2,10,18,26},{22,30,6..., dimensions={0} | all-to-all | bytes 1048576 | tf_op jit(solution)/shard_map/all_to_all | solution.py:302
  69.8 1.9 %collective-permute-start.13 = (bf16[2,16,32,128]{3,2,1,0:T(8,128)(2,1)S(1)}, bf16[2,16,32,128]{3,2,1,0:T(8,128)(2,1)S(1)}, u32[]{:S(2)}, u32[]{:S(2)}) collective-permute-start(bf16[2,16,32,128]{3,2,1,0:T(8,128)(2,1)S(1)} %get-tuple-element.39), channel_id=1, source_target_pairs={{0,4},{4,0},{8,12},{12,8},{16,20},{20,16},{24,28},{28,24},{1,5},{5... | collective-permute-start | bytes 786440 | tf_op jit(solution)/shard_map/ppermute | solution.py:275
  71.7 1.2 %collective-permute-done.13.given = bf16[2,16,32,128]{3,2,1,0:T(8,128)(2,1)S(1)} collective-permute-done((bf16[2,16,32,128]{3,2,1,0:T(8,128)(2,1)S(1)}, bf16[2,16,32,128]{3,2,1,0:T(8,128)(2,1)S(1)}, u32[]{:S(2)}, u32[]{:S(2)}) %collective-permute-start.13) | collective-permute-done | bytes 262176 | tf_op jit(solution)/shard_map/ppermute | solution.py:275
  72.9 0.8 %lay.1 = bf16[32,64,128]{2,1,0:T(8,128)(2,1)} custom-call(s32[1]{0:T(128)} %bitcast.place, bf16[2,16,32,128]{3,2,1,0:T(8,128)(2,1)S(1)} %get-tuple-element.40.kept, bf16[2,16,32,128]{3,2,1,0:T(8,128)(2,1)S(1)} %collective-permute-done.13.given), custom_call_target="tpu_custom_call" | custom-call | tf_op jit(solution)/shard_map/lay/pallas_call | solution.py:244
  (1 shorter events, 0.0 us)
Async XLA Ops:
  5.3 14.7 %collective-permute-start = (bf16[528,256]{1,0:T(8,128)(2,1)}, bf16[528,256]{1,0:T(8,128)(2,1)S(1)}, u32[]{:S(2)}, u32[]{:S(2)}) collective-permute-start(bf16[528,256]{1,0:T(8,128)(2,1)} %get-tuple-element.23.right_in), channel_id=1, source_target_pairs={{0,64},{32,96},{64,0},{96,32},{1,65},{33,97},{65,1},{97,33},{2,66}... | collective-permute-start | bytes 811016 | tf_op jit(solution)/shard_map/ppermute | solution.py:279
  9.0 11.7 %collective-permute-start.3 = (bf16[528,256]{1,0:T(8,128)(2,1)}, bf16[528,256]{1,0:T(8,128)(2,1)S(1)}, u32[]{:S(2)}, u32[]{:S(2)}) collective-permute-start(bf16[528,256]{1,0:T(8,128)(2,1)} %get-tuple-element.22.left_in), channel_id=1, source_target_pairs={{0,8},{4,12},{8,16},{12,20},{16,24},{20,28},{24,0},{28,4},{1,9},{5... | collective-permute-start | bytes 811016 | tf_op jit(solution)/shard_map/ppermute | solution.py:280
  10.7 12.4 %collective-permute-start.8 = (bf16[528,256]{1,0:T(8,128)(2,1)}, bf16[528,256]{1,0:T(8,128)(2,1)S(1)}, u32[]{:S(2)}, u32[]{:S(2)}) collective-permute-start(bf16[528,256]{1,0:T(8,128)(2,1)} %get-tuple-element.23.right_in), channel_id=1, source_target_pairs={{0,32},{32,64},{64,96},{96,0},{1,33},{33,65},{65,97},{97,1},{2,34}... | collective-permute-start | bytes 811016 | tf_op jit(solution)/shard_map/ppermute | solution.py:279
  11.0 12.1 %collective-permute-start.5 = (bf16[528,256]{1,0:T(8,128)(2,1)}, bf16[528,256]{1,0:T(8,128)(2,1)S(1)}, u32[]{:S(2)}, u32[]{:S(2)}) collective-permute-start(bf16[528,256]{1,0:T(8,128)(2,1)} %get-tuple-element.23.right_in), channel_id=1, source_target_pairs={{0,96},{32,0},{64,32},{96,64},{1,97},{33,1},{65,33},{97,65},{2,98}... | collective-permute-start | bytes 811016 | tf_op jit(solution)/shard_map/ppermute | solution.py:279
  13.3 12.2 %collective-permute-start.2 = (bf16[528,256]{1,0:T(8,128)(2,1)}, bf16[528,256]{1,0:T(8,128)(2,1)S(1)}, u32[]{:S(2)}, u32[]{:S(2)}) collective-permute-start(bf16[528,256]{1,0:T(8,128)(2,1)} %get-tuple-element.22.left_in), channel_id=1, source_target_pairs={{0,16},{4,20},{8,24},{12,28},{16,0},{20,4},{24,8},{28,12},{1,17},{... | collective-permute-start | bytes 811016 | tf_op jit(solution)/shard_map/ppermute | solution.py:280
  16.6 1.0 %copy-start = (bf16[528,256]{1,0:T(8,128)(2,1)S(1)}, bf16[528,256]{1,0:T(8,128)(2,1)}, u32[]{:S(2)}) copy-start(bf16[528,256]{1,0:T(8,128)(2,1)} %get-tuple-element.23.right_in) | copy-start | bytes 811012
  17.6 0.9 %copy-start.1 = (bf16[1024,128]{1,0:T(8,128)(2,1)S(1)}, bf16[1024,128]{1,0:T(8,128)(2,1)}, u32[]{:S(2)}) copy-start(bf16[1024,128]{1,0:T(8,128)(2,1)} %w_out.1) | copy-start | bytes 786436
  19.9 7.5 %collective-permute-start.1 = (bf16[528,256]{1,0:T(8,128)(2,1)}, bf16[528,256]{1,0:T(8,128)(2,1)S(1)}, u32[]{:S(2)}, u32[]{:S(2)}) collective-permute-start(bf16[528,256]{1,0:T(8,128)(2,1)} %get-tuple-element.22.left_in), channel_id=1, source_target_pairs={{0,24},{4,28},{8,0},{12,4},{16,8},{20,12},{24,16},{28,20},{1,25},{... | collective-permute-start | bytes 811016 | tf_op jit(solution)/shard_map/ppermute | solution.py:280
  20.7 6.7 %collective-permute-start.4 = (bf16[528,256]{1,0:T(8,128)(2,1)S(1)}, bf16[528,256]{1,0:T(8,128)(2,1)S(1)}, u32[]{:S(2)}, u32[]{:S(2)}) collective-permute-start(bf16[528,256]{1,0:T(8,128)(2,1)S(1)} %get-tuple-element.28.refs_4_), channel_id=1, source_target_pairs={{0,4},{4,0},{8,12},{12,8},{16,20},{20,16},{24,28},{28,24},{1,5},{5... | collective-permute-start | bytes 811016 | tf_op jit(solution)/shard_map/ppermute | solution.py:275
  23.1 4.4 %collective-permute-start.9 = (bf16[528,256]{1,0:T(8,128)(2,1)S(1)}, bf16[528,256]{1,0:T(8,128)(2,1)S(1)}, u32[]{:S(2)}, u32[]{:S(2)}) collective-permute-start(bf16[528,256]{1,0:T(8,128)(2,1)S(1)} %collective-permute-done.8.refs_10_), channel_id=1, source_target_pairs={{0,4},{4,0},{8,12},{12,8},{16,20},{20,16},{24,28},{28,24},{1,5},{5... | collective-permute-start | bytes 811016 | tf_op jit(solution)/shard_map/ppermute | solution.py:275
  23.2 4.3 %collective-permute-start.6 = (bf16[528,256]{1,0:T(8,128)(2,1)S(1)}, bf16[528,256]{1,0:T(8,128)(2,1)S(1)}, u32[]{:S(2)}, u32[]{:S(2)}) collective-permute-start(bf16[528,256]{1,0:T(8,128)(2,1)S(1)} %collective-permute-done.5.refs_6_), channel_id=1, source_target_pairs={{0,4},{4,0},{8,12},{12,8},{16,20},{20,16},{24,28},{28,24},{1,5},{5... | collective-permute-start | bytes 811016 | tf_op jit(solution)/shard_map/ppermute | solution.py:275
  25.5 3.0 %collective-permute-start.7 = (bf16[528,256]{1,0:T(8,128)(2,1)S(1)}, bf16[528,256]{1,0:T(8,128)(2,1)S(1)}, u32[]{:S(2)}, u32[]{:S(2)}) collective-permute-start(bf16[528,256]{1,0:T(8,128)(2,1)S(1)} %collective-permute-done.refs_8_), channel_id=1, source_target_pairs={{0,4},{4,0},{8,12},{12,8},{16,20},{20,16},{24,28},{28,24},{1,5},{5... | collective-permute-start | bytes 811016 | tf_op jit(solution)/shard_map/ppermute | solution.py:275
  31.5 14.4 %collective-permute-start.10 = (bf16[2080,128]{1,0:T(8,128)(2,1)}, bf16[2080,128]{1,0:T(8,128)(2,1)S(1)}, u32[]{:S(2)}, u32[]{:S(2)}) collective-permute-start(bf16[2080,128]{1,0:T(8,128)(2,1)} %get-tuple-element.34), channel_id=1, source_target_pairs={{0,2},{1,3},{2,0},{3,1},{4,6},{5,7},{6,4},{7,5},{8,10},{9,11},{10,... | collective-permute-start | bytes 1597448 | tf_op jit(solution)/shard_map/ppermute | solution.py:290
  40.1 18.5 %collective-permute-start.11 = (bf16[2080,128]{1,0:T(8,128)(2,1)}, bf16[2080,128]{1,0:T(8,128)(2,1)S(1)}, u32[]{:S(2)}, u32[]{:S(2)}) collective-permute-start(bf16[2080,128]{1,0:T(8,128)(2,1)} %get-tuple-element.37), channel_id=1, source_target_pairs={{0,1},{1,2},{2,3},{3,0},{4,5},{5,6},{6,7},{7,4},{8,9},{9,10},{10,1... | collective-permute-start | bytes 1597448 | tf_op jit(solution)/shard_map/ppermute | solution.py:292
  40.5 18.1 %collective-permute-start.12 = (bf16[2080,128]{1,0:T(8,128)(2,1)S(1)}, bf16[2080,128]{1,0:T(8,128)(2,1)S(1)}, u32[]{:S(2)}, u32[]{:S(2)}) collective-permute-start(bf16[2080,128]{1,0:T(8,128)(2,1)S(1)} %get-tuple-element.38), channel_id=1, source_target_pairs={{0,3},{1,0},{2,1},{3,2},{4,7},{5,4},{6,5},{7,6},{8,11},{9,8},{10,9... | collective-permute-start | bytes 1597448 | tf_op jit(solution)/shard_map/ppermute | solution.py:293
  69.8 3.1 %collective-permute-start.13 = (bf16[2,16,32,128]{3,2,1,0:T(8,128)(2,1)S(1)}, bf16[2,16,32,128]{3,2,1,0:T(8,128)(2,1)S(1)}, u32[]{:S(2)}, u32[]{:S(2)}) collective-permute-start(bf16[2,16,32,128]{3,2,1,0:T(8,128)(2,1)S(1)} %get-tuple-element.39), channel_id=1, source_target_pairs={{0,4},{4,0},{8,12},{12,8},{16,20},{20,16},{24,28},{28,24},{1,5},{5... | collective-permute-start | bytes 786440 | tf_op jit(solution)/shard_map/ppermute | solution.py:275

commit v4 on v3

--- a/solution.py
+++ b/solution.py
@@ -107,6 +107,28 @@
         compiler_params=pltpu.CompilerParams(vmem_limit_bytes=8 * 2**20),
         name="order",
     )(w_out, left, right)
+
+
+def choose_kernel(which, a, b, out):
+    @pl.when(which[0] == 0)
+    def _():
+        out[...] = a[...]
+
+    @pl.when(which[0] != 0)
+    def _():
+        out[...] = b[...]
+
+
+def choose(which, a, b):
+    vmem = pl.BlockSpec(memory_space=pltpu.VMEM)
+    return pl.pallas_call(
+        choose_kernel,
+        in_specs=[pl.BlockSpec(memory_space=pltpu.SMEM)] + [vmem] * 2,
+        out_specs=vmem,
+        out_shape=jax.ShapeDtypeStruct(a.shape, a.dtype),
+        compiler_params=pltpu.CompilerParams(vmem_limit_bytes=4 * 2**20),
+        name="choose",
+    )(which, a, b)
 
 
 def pair_kernel(first, place, *refs):
@@ -275,13 +297,29 @@
     flip = lambda v: lax.ppermute(v, "col", [(s, s ^ 1) for s in range(8)])
     rights = {0: right}
     lefts = {0: left}
-    for t in (2, 1, 3):
+    for t in (1, 3):
         rights[t] = lax.ppermute(right, "row", shift_pairs(4, -t))
         lefts[t] = lax.ppermute(left, "col", shift_pairs(8, -2 * t))
-    mix, lefts[0], rights[0], rights[2] = lax.optimization_barrier((*order(w_out, left, right), rights[2]))
+    def relay(near, axis):
+        pairs = []
+        for sy in range(4):
+            for sz in range(4):
+                for sc in range(2):
+                    step = 2 * sc - 1
+                    dy, dz = ((sy + step) % 4, sz) if axis == "row" else (sy, (sz + step) % 4)
+                    pairs.append((8 * sy + 2 * sz + sc, 8 * dy + 2 * dz + sc))
+        return lax.ppermute(near, ("row", "col"), pairs)
+
+    which = core.astype(jnp.int32).reshape(1)
+    rights[2] = relay(choose(which, rights[1], rights[3]), "row")
+    passed = choose(which, lefts[1], lefts[3])
+    own, rights[1], rights[3], passed = lax.optimization_barrier((right, rights[1], rights[3], passed))
+    lefts[2] = relay(passed, "col")
+    late_left, late_right, rights[2] = lax.optimization_barrier((left, right, rights[2]))
+    mix, lefts[0], rights[0] = order(w_out, late_left, late_right)
     columns = []
     for t in range(4):
-        columns += [rights[t], flip(rights[t])]
+        columns += [rights[t], flip(rights[t] if t else own)]
     rows = [lefts[t] for t in range(4)]
 
     quarter = lambda *ks: jnp.stack([(x + k - z) & 3 for k in ks]).astype(jnp.int32)

time: 73.9 us -> 72.6 us (0.982)
  starting transfers between devices: 24.3 us -> 21.2 us
  blocking collectives: 9.96 us -> 12.1 us
  Pallas kernels: 17.6 us -> 16.5 us
    ppermute x3 -> x2, starting transfers between devices: 6.42 us -> 3.64 us  [per_device(): rights[t] = lax.ppermute(right, 'row', shift_pairs(4, -t))]
    ppermute x3 -> x2, waiting for transfers between devices: 0.01 us -> 2.43 us  [per_device(): rights[t] = lax.ppermute(right, 'row', shift_pairs(4, -t))]
    all_to_all x1, blocking collectives: 9.96 us -> 12.1 us  [per_device(): lax.all_to_all(pieces, 'col', 0, 0, axis_index_groups=[[0, 2, 4, 6], [5,...]
    ppermute x3 -> x2, starting transfers between devices: 5.74 us -> 3.76 us  [per_device(): lefts[t] = lax.ppermute(left, 'col', shift_pairs(8, -2 * t))]
    ppermute x0 -> x2, starting transfers between devices: none -> 1.36 us  [relay(): return lax.ppermute(near, ('row', 'col'), pairs)]
    ppermute x5, waiting for transfers between devices: 2.24 us -> 1.17 us  [per_device(): flip = lambda v: lax.ppermute(v, 'col', [(s, s ^ 1) for s in range(8)])]
    pallas_call x1, Pallas kernels: 1.38 us -> 0.4 us  [order(): pl.pallas_call(order_kernel, in_specs=[vmem] * 3, out_specs=[vmem] * 3, o...]
    ppermute x1, waiting for transfers between devices: 2.89 us -> 1.92 us  [per_device(): got[2] = lax.ppermute(part, 'depth', shift_pairs(4, 2))]
where the time goes in v4:
time: 72.6 us; the launch traced here: 72.4 us
  starting transfers between devices  21.2 us (29%)
  waiting for transfers between devices  20.3 us (28%)
  Pallas kernels  16.5 us (23%)
  blocking collectives  12.1 us (17%)
  local copies, waits for them, and re-layouts  2.03 us (3%)
    ppermute x1, waiting for transfers between devices, per_device(): got[1] = lax.ppermute(ahead, 'depth', shift_pairs(4, 1))  12.2 us
    all_to_all x1, blocking collectives, per_device(): lax.all_to_all(pieces, 'col', 0, 0, axis_index_groups=[[0, 2, 4, 6], [5,...  12.1 us
    pallas_call x2, Pallas kernels, pair(): pl.pallas_call(functools.partial(pair_kernel, first), in_specs=[pl.BlockS...  8.71 us
    ppermute x5, starting transfers between devices, per_device(): flip = lambda v: lax.ppermute(v, 'col', [(s, s ^ 1) for s in range(8)])  6.81 us
    pallas_call x1, Pallas kernels, project(): pl.pallas_call(project_kernel, grid=(steps,), in_specs=[pl.BlockSpec((hal...  5.3 us
    ppermute x2, starting transfers between devices, per_device(): lefts[t] = lax.ppermute(left, 'col', shift_pairs(8, -2 * t))  3.76 us
    ppermute x2, starting transfers between devices, per_device(): rights[t] = lax.ppermute(right, 'row', shift_pairs(4, -t))  3.64 us
    ppermute x1, starting transfers between devices, per_device(): got[2] = lax.ppermute(part, 'depth', shift_pairs(4, 2))  3.01 us
  transfers between devices with their start and end apart: 14, of which 5 were waited for; matrix products, arithmetic and copies ran while one was open for 0% of the time, Pallas kernels for 10%

profile of v4, /device:TPU:1, one launch (start us, length us, event | category | flops | bytes accessed | tf_op | source)
XLA Modules:
  0.0 72.4 jit_solution(8623443013874807623)
XLA Ops:
  0.0 0.0 copy-start.2
  0.0 5.3 %project.1 = (bf16[528,256]{1,0:T(8,128)(2,1)}, bf16[528,256]{1,0:T(8,128)(2,1)}) custom-call(bf16[256,16,256]{2,1,0:T(8,128)(2,1)} %sig.1, bf16[16,256]{1,0:T(8,128)(2,1)} %bitcast.23, f32[1,256]{1,0:T(1,128)} %bitcast.24, f32[1,256]{1,0:T(1,128)} %bitcast.25, bf16[32,256]{1,0:T(8,128)(2,1)} %bitcast.21, f32[1,32]{1,0:T(1,128)} %bitcast.26, ...), custom_call_target="tpu_custom_call" | custom-call | tf_op jit(solution)/shard_map/project/pallas_call | solution.py:64
  5.3 2.1 %collective-permute-start.1 = (bf16[528,256]{1,0:T(8,128)(2,1)}, bf16[528,256]{1,0:T(8,128)(2,1)S(1)}, u32[]{:S(2)}, u32[]{:S(2)}) collective-permute-start(bf16[528,256]{1,0:T(8,128)(2,1)} %get-tuple-element.32.right_in), channel_id=1, source_target_pairs={{0,32},{32,64},{64,96},{96,0},{1,33},{33,65},{65,97},{97,1},{2,34}... | collective-permute-start | bytes 811016 | tf_op jit(solution)/shard_map/ppermute | solution.py:301
  7.4 1.5 %collective-permute-start = (bf16[528,256]{1,0:T(8,128)(2,1)}, bf16[528,256]{1,0:T(8,128)(2,1)S(1)}, u32[]{:S(2)}, u32[]{:S(2)}) collective-permute-start(bf16[528,256]{1,0:T(8,128)(2,1)} %get-tuple-element.32.right_in), channel_id=1, source_target_pairs={{0,96},{32,0},{64,32},{96,64},{1,97},{33,1},{65,33},{97,65},{2,98}... | collective-permute-start | bytes 811016 | tf_op jit(solution)/shard_map/ppermute | solution.py:301
  8.9 1.6 %collective-permute-start.4 = (bf16[528,256]{1,0:T(8,128)(2,1)}, bf16[528,256]{1,0:T(8,128)(2,1)S(1)}, u32[]{:S(2)}, u32[]{:S(2)}) collective-permute-start(bf16[528,256]{1,0:T(8,128)(2,1)} %get-tuple-element.27.left_in), channel_id=1, source_target_pairs={{0,8},{4,12},{8,16},{12,20},{16,24},{20,28},{24,0},{28,4},{1,9},{5... | collective-permute-start | bytes 811016 | tf_op jit(solution)/shard_map/ppermute | solution.py:302
  10.6 2.1 %collective-permute-start.3 = (bf16[528,256]{1,0:T(8,128)(2,1)}, bf16[528,256]{1,0:T(8,128)(2,1)S(1)}, u32[]{:S(2)}, u32[]{:S(2)}) collective-permute-start(bf16[528,256]{1,0:T(8,128)(2,1)} %get-tuple-element.27.left_in), channel_id=1, source_target_pairs={{0,24},{4,28},{8,0},{12,4},{16,8},{20,12},{24,16},{28,20},{1,25},{... | collective-permute-start | bytes 811016 | tf_op jit(solution)/shard_map/ppermute | solution.py:302
  12.7 2.4 %collective-permute-done.1.b.refs_10_ = bf16[528,256]{1,0:T(8,128)(2,1)S(1)} collective-permute-done((bf16[528,256]{1,0:T(8,128)(2,1)}, bf16[528,256]{1,0:T(8,128)(2,1)S(1)}, u32[]{:S(2)}, u32[]{:S(2)}) %collective-permute-start.1) | collective-permute-done | bytes 270368 | tf_op jit(solution)/shard_map/ppermute | solution.py:301
  15.1 0.0 collective-permute-done.a.refs_6_
  15.2 0.9 %collective-permute-start.2 = (bf16[528,256]{1,0:T(8,128)(2,1)S(1)}, bf16[528,256]{1,0:T(8,128)(2,1)S(1)}, u32[]{:S(2)}, u32[]{:S(2)}) collective-permute-start(bf16[528,256]{1,0:T(8,128)(2,1)S(1)} %choose.2), channel_id=1, source_target_pairs={{0,96},{4,36},{8,104},{12,44},{16,112},{20,52},{24,120},{28,60},{3... | collective-permute-start | bytes 811016 | tf_op jit(solution)/shard_map/ppermute | solution.py:311
  16.1 2.6 %collective-permute-done.4.b.refs_3_ = bf16[528,256]{1,0:T(8,128)(2,1)S(1)} collective-permute-done((bf16[528,256]{1,0:T(8,128)(2,1)}, bf16[528,256]{1,0:T(8,128)(2,1)S(1)}, u32[]{:S(2)}, u32[]{:S(2)}) %collective-permute-start.4) | collective-permute-done | bytes 270368 | tf_op jit(solution)/shard_map/ppermute | solution.py:302
  18.6 0.0 collective-permute-done.3.a.refs_1_
  18.7 0.5 collective-permute-start.5
  19.1 4.7 %collective-permute-start.6 = (bf16[528,256]{1,0:T(8,128)(2,1)}, bf16[528,256]{1,0:T(8,128)(2,1)S(1)}, u32[]{:S(2)}, u32[]{:S(2)}) collective-permute-start(bf16[528,256]{1,0:T(8,128)(2,1)} %get-tuple-element.32.right_in), channel_id=1, source_target_pairs={{0,4},{4,0},{8,12},{12,8},{16,20},{20,16},{24,28},{28,24},{1,5},{5... | collective-permute-start | bytes 811016 | tf_op jit(solution)/shard_map/ppermute | solution.py:297
  23.8 0.0 collective-permute-start.7
  23.8 0.5 collective-permute-start.9
  24.3 0.0 collective-permute-done.2.refs_8_
  24.3 0.0 collective-permute-start.8
  24.3 0.1 pad_add_fusion.place
  24.4 0.0 copy-done.2
  24.4 0.0 copy-start
  24.4 1.0 %copy-done = bf16[528,256]{1,0:T(8,128)(2,1)S(1)} copy-done((bf16[528,256]{1,0:T(8,128)(2,1)S(1)}, bf16[528,256]{1,0:T(8,128)(2,1)}, u32[]{:S(2)}) %copy-start) | copy-done | bytes 270360
  25.3 0.0 copy-start.1
  25.3 1.0 %copy-done.1 = bf16[528,256]{1,0:T(8,128)(2,1)S(1)} copy-done((bf16[528,256]{1,0:T(8,128)(2,1)S(1)}, bf16[528,256]{1,0:T(8,128)(2,1)}, u32[]{:S(2)}) %copy-start.1) | copy-done | bytes 270360
  26.3 0.4 order.1
  26.7 0.0 collective-permute-done.5.refs_2_
  26.7 0.0 collective-permute-done.6.refs_5_
  26.7 0.0 collective-permute-done.7.refs_7_
  26.7 0.0 collective-permute-done.9.refs_11_
  26.7 0.0 collective-permute-done.8.refs_9_
  26.7 2.1 %pair_first.1 = (bf16[2080,128]{1,0:T(8,128)(2,1)S(1)}, bf16[12,528,256]{2,1,0:T(8,128)(2,1)S(1)}) custom-call(s32[1]{0:T(128)} %bitcast.12.place, bf16[528,256]{1,0:T(8,128)(2,1)S(1)} %get-tuple-element.29.refs_0_, bf16[528,256]{1,0:T(8,128)(2,1)S(1)} %collective-permute-done.3.a.refs_1_, bf16[528,256]{1,0:T(8,128)(2,1)S(1)} %collective-permute-done.5.refs_2_, ...), custom_call_target="tpu_custom_call" | custom-call | flops 268435456 | bytes 65536 | tf_op jit(solution)/shard_map/pair_first/pallas_call | solution.py:194
  28.9 3.0 %collective-permute-start.10 = (bf16[2080,128]{1,0:T(8,128)(2,1)S(1)}, bf16[2080,128]{1,0:T(8,128)(2,1)S(1)}, u32[]{:S(2)}, u32[]{:S(2)}) collective-permute-start(bf16[2080,128]{1,0:T(8,128)(2,1)S(1)} %get-tuple-element.40), channel_id=1, source_target_pairs={{0,2},{1,3},{2,0},{3,1},{4,6},{5,7},{6,4},{7,5},{8,10},{9,11},{10,... | collective-permute-start | bytes 1597448 | tf_op jit(solution)/shard_map/ppermute | solution.py:328
  31.9 6.6 %pair_rest.1 = (bf16[2080,128]{1,0:T(8,128)(2,1)}, bf16[2080,128]{1,0:T(8,128)(2,1)}, f32[2048,128]{1,0:T(8,128)S(1)}, f32[16,128]{1,0:T(8,128)S(1)}) custom-call(s32[3]{0:T(128)S(1)} %pad_add_fusion.place, bf16[12,528,256]{2,1,0:T(8,128)(2,1)S(1)} %get-tuple-element.37.refs_0_, bf16[128,1024]{1,0:T(8,128)(2,1)S(1)} %get-tuple-element.36.refs_12_.refs_1_), custom_call_target="tpu_custom_call" | custom-call | flops 268435456 | bytes 65536 | tf_op jit(solution)/shard_map/pair_rest/pallas_call | solution.py:194
  38.5 0.3 collective-permute-start.11
  38.8 2.4 %collective-permute-start.12 = (bf16[2080,128]{1,0:T(8,128)(2,1)}, bf16[2080,128]{1,0:T(8,128)(2,1)S(1)}, u32[]{:S(2)}, u32[]{:S(2)}) collective-permute-start(bf16[2080,128]{1,0:T(8,128)(2,1)} %get-tuple-element.44), channel_id=1, source_target_pairs={{0,3},{1,0},{2,1},{3,2},{4,7},{5,4},{6,5},{7,6},{8,11},{9,8},{10,9... | collective-permute-start | bytes 1597448 | tf_op jit(solution)/shard_map/ppermute | solution.py:331
  41.2 0.1 stack.50.place
  41.2 1.9 %collective-permute-done.10.part = bf16[2080,128]{1,0:T(8,128)(2,1)S(1)} collective-permute-done((bf16[2080,128]{1,0:T(8,128)(2,1)S(1)}, bf16[2080,128]{1,0:T(8,128)(2,1)S(1)}, u32[]{:S(2)}, u32[]{:S(2)}) %collective-permute-start.10) | collective-permute-done | bytes 532512 | tf_op jit(solution)/shard_map/ppermute | solution.py:328
  43.2 0.1 fold.1
  43.3 12.2 %collective-permute-done.11.a = bf16[2080,128]{1,0:T(8,128)(2,1)S(1)} collective-permute-done((bf16[2080,128]{1,0:T(8,128)(2,1)}, bf16[2080,128]{1,0:T(8,128)(2,1)S(1)}, u32[]{:S(2)}, u32[]{:S(2)}) %collective-permute-start.11) | collective-permute-done | bytes 532512 | tf_op jit(solution)/shard_map/ppermute | solution.py:330
  55.5 0.0 collective-permute-done.12.b
  55.5 1.2 %settle.1 = bf16[4,16,32,128]{3,2,1,0:T(8,128)(2,1)S(1)} custom-call(s32[8]{0:T(128)S(1)} %stack.50.place, f32[2048,128]{1,0:T(8,128)S(1)} %get-tuple-element.41.mine, f32[16,128]{1,0:T(8,128)S(1)} %get-tuple-element.42.count, bf16[2080,128]{1,0:T(8,128)(2,1)S(1)} %collective-permute-done.11.a, bf16[2080,128]{1,0:T(8,128)(2,1)S(1)} %collective-permute-done.12.b), custom_call_target="tpu_custom_call" | custom-call | tf_op jit(solution)/shard_map/settle/pallas_call | solution.py:244
  56.6 12.1 %all_to_all.5 = bf16[4,16,32,128]{3,2,1,0:T(8,128)(2,1)S(1)} all-to-all(bf16[4,16,32,128]{3,2,1,0:T(8,128)(2,1)S(1)} %settle.1), channel_id=1, replica_groups={{0,8,16,24},{20,28,4,12},{1,9,17,25},{21,29,5,13},{2,10,18,26},{22,30,6..., dimensions={0} | all-to-all | bytes 1048576 | tf_op jit(solution)/shard_map/all_to_all | solution.py:340
  68.8 1.6 %collective-permute-start.13 = (bf16[2,16,32,128]{3,2,1,0:T(8,128)(2,1)S(1)}, bf16[2,16,32,128]{3,2,1,0:T(8,128)(2,1)S(1)}, u32[]{:S(2)}, u32[]{:S(2)}) collective-permute-start(bf16[2,16,32,128]{3,2,1,0:T(8,128)(2,1)S(1)} %get-tuple-element.45), channel_id=1, source_target_pairs={{0,4},{4,0},{8,12},{12,8},{16,20},{20,16},{24,28},{28,24},{1,5},{5... | collective-permute-start | bytes 786440 | tf_op jit(solution)/shard_map/ppermute | solution.py:297
  70.4 1.2 %collective-permute-done.13.given = bf16[2,16,32,128]{3,2,1,0:T(8,128)(2,1)S(1)} collective-permute-done((bf16[2,16,32,128]{3,2,1,0:T(8,128)(2,1)S(1)}, bf16[2,16,32,128]{3,2,1,0:T(8,128)(2,1)S(1)}, u32[]{:S(2)}, u32[]{:S(2)}) %collective-permute-start.13) | collective-permute-done | bytes 262176 | tf_op jit(solution)/shard_map/ppermute | solution.py:297
  71.6 0.8 %lay.1 = bf16[32,64,128]{2,1,0:T(8,128)(2,1)} custom-call(s32[1]{0:T(128)} %bitcast.place, bf16[2,16,32,128]{3,2,1,0:T(8,128)(2,1)S(1)} %get-tuple-element.46.kept, bf16[2,16,32,128]{3,2,1,0:T(8,128)(2,1)S(1)} %collective-permute-done.13.given), custom_call_target="tpu_custom_call" | custom-call | tf_op jit(solution)/shard_map/lay/pallas_call | solution.py:266
  (3 shorter events, 0.1 us)
Async XLA Ops:
  0.0 24.4 %copy-start.2 = (bf16[1024,128]{1,0:T(8,128)(2,1)S(1)}, bf16[1024,128]{1,0:T(8,128)(2,1)}, u32[]{:S(2)}) copy-start(bf16[1024,128]{1,0:T(8,128)(2,1)} %w_out.1) | copy-start | bytes 786436
  5.3 9.8 %collective-permute-start.1 = (bf16[528,256]{1,0:T(8,128)(2,1)}, bf16[528,256]{1,0:T(8,128)(2,1)S(1)}, u32[]{:S(2)}, u32[]{:S(2)}) collective-permute-start(bf16[528,256]{1,0:T(8,128)(2,1)} %get-tuple-element.32.right_in), channel_id=1, source_target_pairs={{0,32},{32,64},{64,96},{96,0},{1,33},{33,65},{65,97},{97,1},{2,34}... | collective-permute-start | bytes 811016 | tf_op jit(solution)/shard_map/ppermute | solution.py:301
  7.4 7.7 %collective-permute-start = (bf16[528,256]{1,0:T(8,128)(2,1)}, bf16[528,256]{1,0:T(8,128)(2,1)S(1)}, u32[]{:S(2)}, u32[]{:S(2)}) collective-permute-start(bf16[528,256]{1,0:T(8,128)(2,1)} %get-tuple-element.32.right_in), channel_id=1, source_target_pairs={{0,96},{32,0},{64,32},{96,64},{1,97},{33,1},{65,33},{97,65},{2,98}... | collective-permute-start | bytes 811016 | tf_op jit(solution)/shard_map/ppermute | solution.py:301
  8.9 9.7 %collective-permute-start.4 = (bf16[528,256]{1,0:T(8,128)(2,1)}, bf16[528,256]{1,0:T(8,128)(2,1)S(1)}, u32[]{:S(2)}, u32[]{:S(2)}) collective-permute-start(bf16[528,256]{1,0:T(8,128)(2,1)} %get-tuple-element.27.left_in), channel_id=1, source_target_pairs={{0,8},{4,12},{8,16},{12,20},{16,24},{20,28},{24,0},{28,4},{1,9},{5... | collective-permute-start | bytes 811016 | tf_op jit(solution)/shard_map/ppermute | solution.py:302
  10.6 8.1 %collective-permute-start.3 = (bf16[528,256]{1,0:T(8,128)(2,1)}, bf16[528,256]{1,0:T(8,128)(2,1)S(1)}, u32[]{:S(2)}, u32[]{:S(2)}) collective-permute-start(bf16[528,256]{1,0:T(8,128)(2,1)} %get-tuple-element.27.left_in), channel_id=1, source_target_pairs={{0,24},{4,28},{8,0},{12,4},{16,8},{20,12},{24,16},{28,20},{1,25},{... | collective-permute-start | bytes 811016 | tf_op jit(solution)/shard_map/ppermute | solution.py:302
  15.2 9.1 %collective-permute-start.2 = (bf16[528,256]{1,0:T(8,128)(2,1)S(1)}, bf16[528,256]{1,0:T(8,128)(2,1)S(1)}, u32[]{:S(2)}, u32[]{:S(2)}) collective-permute-start(bf16[528,256]{1,0:T(8,128)(2,1)S(1)} %choose.2), channel_id=1, source_target_pairs={{0,96},{4,36},{8,104},{12,44},{16,112},{20,52},{24,120},{28,60},{3... | collective-permute-start | bytes 811016 | tf_op jit(solution)/shard_map/ppermute | solution.py:311
  18.7 8.0 %collective-permute-start.5 = (bf16[528,256]{1,0:T(8,128)(2,1)S(1)}, bf16[528,256]{1,0:T(8,128)(2,1)S(1)}, u32[]{:S(2)}, u32[]{:S(2)}) collective-permute-start(bf16[528,256]{1,0:T(8,128)(2,1)S(1)} %choose.3), channel_id=1, source_target_pairs={{0,24},{4,12},{8,0},{12,20},{16,8},{20,28},{24,16},{28,4},{32,56},... | collective-permute-start | bytes 811016 | tf_op jit(solution)/shard_map/ppermute | solution.py:311
  19.1 7.6 %collective-permute-start.6 = (bf16[528,256]{1,0:T(8,128)(2,1)}, bf16[528,256]{1,0:T(8,128)(2,1)S(1)}, u32[]{:S(2)}, u32[]{:S(2)}) collective-permute-start(bf16[528,256]{1,0:T(8,128)(2,1)} %get-tuple-element.32.right_in), channel_id=1, source_target_pairs={{0,4},{4,0},{8,12},{12,8},{16,20},{20,16},{24,28},{28,24},{1,5},{5... | collective-permute-start | bytes 811016 | tf_op jit(solution)/shard_map/ppermute | solution.py:297
  23.8 2.9 %collective-permute-start.7 = (bf16[528,256]{1,0:T(8,128)(2,1)S(1)}, bf16[528,256]{1,0:T(8,128)(2,1)S(1)}, u32[]{:S(2)}, u32[]{:S(2)}) collective-permute-start(bf16[528,256]{1,0:T(8,128)(2,1)S(1)} %collective-permute-done.a.refs_6_), channel_id=1, source_target_pairs={{0,4},{4,0},{8,12},{12,8},{16,20},{20,16},{24,28},{28,24},{1,5},{5... | collective-permute-start | bytes 811016 | tf_op jit(solution)/shard_map/ppermute | solution.py:297
  23.8 2.9 %collective-permute-start.9 = (bf16[528,256]{1,0:T(8,128)(2,1)S(1)}, bf16[528,256]{1,0:T(8,128)(2,1)S(1)}, u32[]{:S(2)}, u32[]{:S(2)}) collective-permute-start(bf16[528,256]{1,0:T(8,128)(2,1)S(1)} %collective-permute-done.1.b.refs_10_), channel_id=1, source_target_pairs={{0,4},{4,0},{8,12},{12,8},{16,20},{20,16},{24,28},{28,24},{1,5},{5... | collective-permute-start | bytes 811016 | tf_op jit(solution)/shard_map/ppermute | solution.py:297
  24.3 2.4 %collective-permute-start.8 = (bf16[528,256]{1,0:T(8,128)(2,1)S(1)}, bf16[528,256]{1,0:T(8,128)(2,1)S(1)}, u32[]{:S(2)}, u32[]{:S(2)}) collective-permute-start(bf16[528,256]{1,0:T(8,128)(2,1)S(1)} %collective-permute-done.2.refs_8_), channel_id=1, source_target_pairs={{0,4},{4,0},{8,12},{12,8},{16,20},{20,16},{24,28},{28,24},{1,5},{5... | collective-permute-start | bytes 811016 | tf_op jit(solution)/shard_map/ppermute | solution.py:297
  24.4 1.0 %copy-start = (bf16[528,256]{1,0:T(8,128)(2,1)S(1)}, bf16[528,256]{1,0:T(8,128)(2,1)}, u32[]{:S(2)}) copy-start(bf16[528,256]{1,0:T(8,128)(2,1)} %get-tuple-element.32.right_in) | copy-start | bytes 811012
  25.3 1.0 %copy-start.1 = (bf16[528,256]{1,0:T(8,128)(2,1)S(1)}, bf16[528,256]{1,0:T(8,128)(2,1)}, u32[]{:S(2)}) copy-start(bf16[528,256]{1,0:T(8,128)(2,1)} %get-tuple-element.27.left_in) | copy-start | bytes 811012
  28.9 14.3 %collective-permute-start.10 = (bf16[2080,128]{1,0:T(8,128)(2,1)S(1)}, bf16[2080,128]{1,0:T(8,128)(2,1)S(1)}, u32[]{:S(2)}, u32[]{:S(2)}) collective-permute-start(bf16[2080,128]{1,0:T(8,128)(2,1)S(1)} %get-tuple-element.40), channel_id=1, source_target_pairs={{0,2},{1,3},{2,0},{3,1},{4,6},{5,7},{6,4},{7,5},{8,10},{9,11},{10,... | collective-permute-start | bytes 1597448 | tf_op jit(solution)/shard_map/ppermute | solution.py:328
  38.5 17.0 %collective-permute-start.11 = (bf16[2080,128]{1,0:T(8,128)(2,1)}, bf16[2080,128]{1,0:T(8,128)(2,1)S(1)}, u32[]{:S(2)}, u32[]{:S(2)}) collective-permute-start(bf16[2080,128]{1,0:T(8,128)(2,1)} %get-tuple-element.43), channel_id=1, source_target_pairs={{0,1},{1,2},{2,3},{3,0},{4,5},{5,6},{6,7},{7,4},{8,9},{9,10},{10,1... | collective-permute-start | bytes 1597448 | tf_op jit(solution)/shard_map/ppermute | solution.py:330
  38.8 16.7 %collective-permute-start.12 = (bf16[2080,128]{1,0:T(8,128)(2,1)}, bf16[2080,128]{1,0:T(8,128)(2,1)S(1)}, u32[]{:S(2)}, u32[]{:S(2)}) collective-permute-start(bf16[2080,128]{1,0:T(8,128)(2,1)} %get-tuple-element.44), channel_id=1, source_target_pairs={{0,3},{1,0},{2,1},{3,2},{4,7},{5,4},{6,5},{7,6},{8,11},{9,8},{10,9... | collective-permute-start | bytes 1597448 | tf_op jit(solution)/shard_map/ppermute | solution.py:331
  68.8 2.8 %collective-permute-start.13 = (bf16[2,16,32,128]{3,2,1,0:T(8,128)(2,1)S(1)}, bf16[2,16,32,128]{3,2,1,0:T(8,128)(2,1)S(1)}, u32[]{:S(2)}, u32[]{:S(2)}) collective-permute-start(bf16[2,16,32,128]{3,2,1,0:T(8,128)(2,1)S(1)} %get-tuple-element.45), channel_id=1, source_target_pairs={{0,4},{4,0},{8,12},{12,8},{16,20},{20,16},{24,28},{28,24},{1,5},{5... | collective-permute-start | bytes 786440 | tf_op jit(solution)/shard_map/ppermute | solution.py:297

commit v5 on v4

--- a/solution.py
+++ b/solution.py
@@ -37,20 +37,24 @@
     flat = sig[...].astype(F32).reshape(half * RES, 256)
     wide[0] = flat[:, 0:128]
     wide[1] = flat[:, 128:256]
-    for r in range(RES):
-        low = wide[0, pl.ds(r, half, stride=RES), :]
-        high = wide[1, pl.ds(r, half, stride=RES), :]
-        mean = jnp.sum(low + high, axis=1, keepdims=True) * (1.0 / 256)
-        low = low - mean
-        high = high - mean
-        spread = jnp.sum(low * low + high * high, axis=1, keepdims=True) * (1.0 / 256)
-        scale = lax.rsqrt(spread + 1e-5)
-        low = low * scale * gain[:, 0:128] + shift[:, 0:128]
-        high = high * scale * gain[:, 128:256] + shift[:, 128:256]
-        normed = jnp.concatenate([low.astype(BF16), high.astype(BF16)], axis=1)
-        both = (dot(weights, normed, NT) + bias) * presence[r : r + 1, :]
-        left[r * HID : (r + 1) * HID, :] = both[0:HID].astype(BF16)
-        cols[r * HID : (r + 1) * HID, :] = both[HID : 2 * HID]
+    for first in range(0, RES, 4):
+        normed = []
+        for r in range(first, first + 4):
+            low = wide[0, pl.ds(r, half, stride=RES), :]
+            high = wide[1, pl.ds(r, half, stride=RES), :]
+            mean = jnp.sum(low + high, axis=1, keepdims=True) * (1.0 / 256)
+            low = low - mean
+            high = high - mean
+            spread = jnp.sum(low * low + high * high, axis=1, keepdims=True) * (1.0 / 256)
+            scale = lax.rsqrt(spread + 1e-5)
+            low = low * scale * gain[:, 0:128] + shift[:, 0:128]
+            high = high * scale * gain[:, 128:256] + shift[:, 128:256]
+            normed.append(jnp.concatenate([low.astype(BF16), high.astype(BF16)], axis=1))
+        four = dot(weights, jnp.concatenate(normed, axis=0), NT)
+        for r in range(first, first + 4):
+            both = (four[:, (r - first) * half : (r - first + 1) * half] + bias) * presence[r : r + 1, :]
+            left[r * HID : (r + 1) * HID, :] = both[0:HID].astype(BF16)
+            cols[r * HID : (r + 1) * HID, :] = both[HID : 2 * HID]
     for d in range(HID):
         right[d * RES : (d + 1) * RES, :] = cols[pl.ds(d, RES, stride=HID), :].astype(BF16)
     left[SHARD:ROWS, :] = mask[...]
@@ -298,8 +302,8 @@
     rights = {0: right}
     lefts = {0: left}
     for t in (1, 3):
+        lefts[t] = lax.ppermute(left, "col", shift_pairs(8, -2 * t))
         rights[t] = lax.ppermute(right, "row", shift_pairs(4, -t))
-        lefts[t] = lax.ppermute(left, "col", shift_pairs(8, -2 * t))
     def relay(near, axis):
         pairs = []
         for sy in range(4):

time: 72.6 us -> 72.4 us (level)
  no operation moved by 1% of the time
where the time goes in v5:
time: 72.4 us; the launch traced here: 72.1 us
  starting transfers between devices  21.2 us (29%)
  waiting for transfers between devices  20.3 us (28%)
  Pallas kernels  16.3 us (23%)
  blocking collectives  12.2 us (17%)
  local copies, waits for them, and re-layouts  2.03 us (3%)
    ppermute x1, waiting for transfers between devices, per_device(): got[1] = lax.ppermute(ahead, 'depth', shift_pairs(4, 1))  12.2 us
    all_to_all x1, blocking collectives, per_device(): lax.all_to_all(pieces, 'col', 0, 0, axis_index_groups=[[0, 2, 4, 6], [5,...  12.2 us
    pallas_call x2, Pallas kernels, pair(): pl.pallas_call(functools.partial(pair_kernel, first), in_specs=[pl.BlockS...  8.7 us
    ppermute x5, starting transfers between devices, per_device(): flip = lambda v: lax.ppermute(v, 'col', [(s, s ^ 1) for s in range(8)])  6.77 us
    pallas_call x1, Pallas kernels, project(): pl.pallas_call(project_kernel, grid=(steps,), in_specs=[pl.BlockSpec((hal...  5.04 us
    ppermute x2, starting transfers between devices, per_device(): lefts[t] = lax.ppermute(left, 'col', shift_pairs(8, -2 * t))  3.76 us
    ppermute x2, starting transfers between devices, per_device(): rights[t] = lax.ppermute(right, 'row', shift_pairs(4, -t))  3.64 us
    ppermute x1, starting transfers between devices, per_device(): got[2] = lax.ppermute(part, 'depth', shift_pairs(4, 2))  3.01 us
  transfers between devices with their start and end apart: 14, of which 5 were waited for; matrix products, arithmetic and copies ran while one was open for 0% of the time, Pallas kernels for 10%

profile of v5, /device:TPU:1, one launch (start us, length us, event | category | flops | bytes accessed | tf_op | source)
XLA Modules:
  0.0 72.1 jit_solution(3025647424633064099)
XLA Ops:
  0.0 0.0 copy-start.2
  0.0 5.0 %project.1 = (bf16[528,256]{1,0:T(8,128)(2,1)}, bf16[528,256]{1,0:T(8,128)(2,1)}) custom-call(bf16[256,16,256]{2,1,0:T(8,128)(2,1)} %sig.1, bf16[16,256]{1,0:T(8,128)(2,1)} %bitcast.23, f32[1,256]{1,0:T(1,128)} %bitcast.24, f32[1,256]{1,0:T(1,128)} %bitcast.25, bf16[32,256]{1,0:T(8,128)(2,1)} %bitcast.21, f32[1,32]{1,0:T(1,128)} %bitcast.26, ...), custom_call_target="tpu_custom_call" | custom-call | tf_op jit(solution)/shard_map/project/pallas_call | solution.py:68
  5.0 2.1 %collective-permute-start.1 = (bf16[528,256]{1,0:T(8,128)(2,1)}, bf16[528,256]{1,0:T(8,128)(2,1)S(1)}, u32[]{:S(2)}, u32[]{:S(2)}) collective-permute-start(bf16[528,256]{1,0:T(8,128)(2,1)} %get-tuple-element.32.right_in), channel_id=1, source_target_pairs={{0,32},{32,64},{64,96},{96,0},{1,33},{33,65},{65,97},{97,1},{2,34}... | collective-permute-start | bytes 811016 | tf_op jit(solution)/shard_map/ppermute | solution.py:306
  7.2 1.5 %collective-permute-start = (bf16[528,256]{1,0:T(8,128)(2,1)}, bf16[528,256]{1,0:T(8,128)(2,1)S(1)}, u32[]{:S(2)}, u32[]{:S(2)}) collective-permute-start(bf16[528,256]{1,0:T(8,128)(2,1)} %get-tuple-element.32.right_in), channel_id=1, source_target_pairs={{0,96},{32,0},{64,32},{96,64},{1,97},{33,1},{65,33},{97,65},{2,98}... | collective-permute-start | bytes 811016 | tf_op jit(solution)/shard_map/ppermute | solution.py:306
  8.7 1.6 %collective-permute-start.4 = (bf16[528,256]{1,0:T(8,128)(2,1)}, bf16[528,256]{1,0:T(8,128)(2,1)S(1)}, u32[]{:S(2)}, u32[]{:S(2)}) collective-permute-start(bf16[528,256]{1,0:T(8,128)(2,1)} %get-tuple-element.27.left_in), channel_id=1, source_target_pairs={{0,8},{4,12},{8,16},{12,20},{16,24},{20,28},{24,0},{28,4},{1,9},{5... | collective-permute-start | bytes 811016 | tf_op jit(solution)/shard_map/ppermute | solution.py:305
  10.3 2.1 %collective-permute-start.3 = (bf16[528,256]{1,0:T(8,128)(2,1)}, bf16[528,256]{1,0:T(8,128)(2,1)S(1)}, u32[]{:S(2)}, u32[]{:S(2)}) collective-permute-start(bf16[528,256]{1,0:T(8,128)(2,1)} %get-tuple-element.27.left_in), channel_id=1, source_target_pairs={{0,24},{4,28},{8,0},{12,4},{16,8},{20,12},{24,16},{28,20},{1,25},{... | collective-permute-start | bytes 811016 | tf_op jit(solution)/shard_map/ppermute | solution.py:305
  12.4 2.4 %collective-permute-done.1.b.refs_10_ = bf16[528,256]{1,0:T(8,128)(2,1)S(1)} collective-permute-done((bf16[528,256]{1,0:T(8,128)(2,1)}, bf16[528,256]{1,0:T(8,128)(2,1)S(1)}, u32[]{:S(2)}, u32[]{:S(2)}) %collective-permute-start.1) | collective-permute-done | bytes 270368 | tf_op jit(solution)/shard_map/ppermute | solution.py:306
  14.9 0.0 collective-permute-done.a.refs_6_
  14.9 0.9 %collective-permute-start.2 = (bf16[528,256]{1,0:T(8,128)(2,1)S(1)}, bf16[528,256]{1,0:T(8,128)(2,1)S(1)}, u32[]{:S(2)}, u32[]{:S(2)}) collective-permute-start(bf16[528,256]{1,0:T(8,128)(2,1)S(1)} %choose.2), channel_id=1, source_target_pairs={{0,96},{4,36},{8,104},{12,44},{16,112},{20,52},{24,120},{28,60},{3... | collective-permute-start | bytes 811016 | tf_op jit(solution)/shard_map/ppermute | solution.py:315
  15.8 2.6 %collective-permute-done.4.b.refs_3_ = bf16[528,256]{1,0:T(8,128)(2,1)S(1)} collective-permute-done((bf16[528,256]{1,0:T(8,128)(2,1)}, bf16[528,256]{1,0:T(8,128)(2,1)S(1)}, u32[]{:S(2)}, u32[]{:S(2)}) %collective-permute-start.4) | collective-permute-done | bytes 270368 | tf_op jit(solution)/shard_map/ppermute | solution.py:305
  18.4 0.0 collective-permute-done.3.a.refs_1_
  18.4 0.5 collective-permute-start.5
  18.8 4.7 %collective-permute-start.6 = (bf16[528,256]{1,0:T(8,128)(2,1)}, bf16[528,256]{1,0:T(8,128)(2,1)S(1)}, u32[]{:S(2)}, u32[]{:S(2)}) collective-permute-start(bf16[528,256]{1,0:T(8,128)(2,1)} %get-tuple-element.32.right_in), channel_id=1, source_target_pairs={{0,4},{4,0},{8,12},{12,8},{16,20},{20,16},{24,28},{28,24},{1,5},{5... | collective-permute-start | bytes 811016 | tf_op jit(solution)/shard_map/ppermute | solution.py:301
  23.5 0.0 collective-permute-start.7
  23.5 0.5 collective-permute-start.9
  24.0 0.0 collective-permute-done.2.refs_8_
  24.0 0.0 collective-permute-start.8
  24.0 0.1 pad_add_fusion.place
  24.1 0.0 copy-done.2
  24.1 0.0 copy-start
  24.1 1.0 %copy-done = bf16[528,256]{1,0:T(8,128)(2,1)S(1)} copy-done((bf16[528,256]{1,0:T(8,128)(2,1)S(1)}, bf16[528,256]{1,0:T(8,128)(2,1)}, u32[]{:S(2)}) %copy-start) | copy-done | bytes 270360
  25.1 0.0 copy-start.1
  25.1 1.0 %copy-done.1 = bf16[528,256]{1,0:T(8,128)(2,1)S(1)} copy-done((bf16[528,256]{1,0:T(8,128)(2,1)S(1)}, bf16[528,256]{1,0:T(8,128)(2,1)}, u32[]{:S(2)}) %copy-start.1) | copy-done | bytes 270360
  26.0 0.4 order.1
  26.4 0.0 collective-permute-done.5.refs_2_
  26.4 0.0 collective-permute-done.6.refs_5_
  26.4 0.0 collective-permute-done.7.refs_7_
  26.5 0.0 collective-permute-done.9.refs_11_
  26.5 0.0 collective-permute-done.8.refs_9_
  26.5 2.1 %pair_first.1 = (bf16[2080,128]{1,0:T(8,128)(2,1)S(1)}, bf16[12,528,256]{2,1,0:T(8,128)(2,1)S(1)}) custom-call(s32[1]{0:T(128)} %bitcast.12.place, bf16[528,256]{1,0:T(8,128)(2,1)S(1)} %get-tuple-element.29.refs_0_, bf16[528,256]{1,0:T(8,128)(2,1)S(1)} %collective-permute-done.3.a.refs_1_, bf16[528,256]{1,0:T(8,128)(2,1)S(1)} %collective-permute-done.5.refs_2_, ...), custom_call_target="tpu_custom_call" | custom-call | flops 268435456 | bytes 65536 | tf_op jit(solution)/shard_map/pair_first/pallas_call | solution.py:198
  28.6 3.0 %collective-permute-start.10 = (bf16[2080,128]{1,0:T(8,128)(2,1)S(1)}, bf16[2080,128]{1,0:T(8,128)(2,1)S(1)}, u32[]{:S(2)}, u32[]{:S(2)}) collective-permute-start(bf16[2080,128]{1,0:T(8,128)(2,1)S(1)} %get-tuple-element.40), channel_id=1, source_target_pairs={{0,2},{1,3},{2,0},{3,1},{4,6},{5,7},{6,4},{7,5},{8,10},{9,11},{10,... | collective-permute-start | bytes 1597448 | tf_op jit(solution)/shard_map/ppermute | solution.py:332
  31.6 6.6 %pair_rest.1 = (bf16[2080,128]{1,0:T(8,128)(2,1)}, bf16[2080,128]{1,0:T(8,128)(2,1)}, f32[2048,128]{1,0:T(8,128)S(1)}, f32[16,128]{1,0:T(8,128)S(1)}) custom-call(s32[3]{0:T(128)S(1)} %pad_add_fusion.place, bf16[12,528,256]{2,1,0:T(8,128)(2,1)S(1)} %get-tuple-element.37.refs_0_, bf16[128,1024]{1,0:T(8,128)(2,1)S(1)} %get-tuple-element.36.refs_12_.refs_1_), custom_call_target="tpu_custom_call" | custom-call | flops 268435456 | bytes 65536 | tf_op jit(solution)/shard_map/pair_rest/pallas_call | solution.py:198
  38.2 0.3 collective-permute-start.11
  38.5 2.4 %collective-permute-start.12 = (bf16[2080,128]{1,0:T(8,128)(2,1)}, bf16[2080,128]{1,0:T(8,128)(2,1)S(1)}, u32[]{:S(2)}, u32[]{:S(2)}) collective-permute-start(bf16[2080,128]{1,0:T(8,128)(2,1)} %get-tuple-element.44), channel_id=1, source_target_pairs={{0,3},{1,0},{2,1},{3,2},{4,7},{5,4},{6,5},{7,6},{8,11},{9,8},{10,9... | collective-permute-start | bytes 1597448 | tf_op jit(solution)/shard_map/ppermute | solution.py:335
  40.9 0.1 stack.50.place
  41.0 1.9 %collective-permute-done.10.part = bf16[2080,128]{1,0:T(8,128)(2,1)S(1)} collective-permute-done((bf16[2080,128]{1,0:T(8,128)(2,1)S(1)}, bf16[2080,128]{1,0:T(8,128)(2,1)S(1)}, u32[]{:S(2)}, u32[]{:S(2)}) %collective-permute-start.10) | collective-permute-done | bytes 532512 | tf_op jit(solution)/shard_map/ppermute | solution.py:332
  42.9 0.1 fold.1
  43.0 12.2 %collective-permute-done.11.a = bf16[2080,128]{1,0:T(8,128)(2,1)S(1)} collective-permute-done((bf16[2080,128]{1,0:T(8,128)(2,1)}, bf16[2080,128]{1,0:T(8,128)(2,1)S(1)}, u32[]{:S(2)}, u32[]{:S(2)}) %collective-permute-start.11) | collective-permute-done | bytes 532512 | tf_op jit(solution)/shard_map/ppermute | solution.py:334
  55.2 0.0 collective-permute-done.12.b
  55.2 1.2 %settle.1 = bf16[4,16,32,128]{3,2,1,0:T(8,128)(2,1)S(1)} custom-call(s32[8]{0:T(128)S(1)} %stack.50.place, f32[2048,128]{1,0:T(8,128)S(1)} %get-tuple-element.41.mine, f32[16,128]{1,0:T(8,128)S(1)} %get-tuple-element.42.count, bf16[2080,128]{1,0:T(8,128)(2,1)S(1)} %collective-permute-done.11.a, bf16[2080,128]{1,0:T(8,128)(2,1)S(1)} %collective-permute-done.12.b), custom_call_target="tpu_custom_call" | custom-call | tf_op jit(solution)/shard_map/settle/pallas_call | solution.py:248
  56.4 12.2 %all_to_all.5 = bf16[4,16,32,128]{3,2,1,0:T(8,128)(2,1)S(1)} all-to-all(bf16[4,16,32,128]{3,2,1,0:T(8,128)(2,1)S(1)} %settle.1), channel_id=1, replica_groups={{0,8,16,24},{20,28,4,12},{1,9,17,25},{21,29,5,13},{2,10,18,26},{22,30,6..., dimensions={0} | all-to-all | bytes 1048576 | tf_op jit(solution)/shard_map/all_to_all | solution.py:344
  68.6 1.6 %collective-permute-start.13 = (bf16[2,16,32,128]{3,2,1,0:T(8,128)(2,1)S(1)}, bf16[2,16,32,128]{3,2,1,0:T(8,128)(2,1)S(1)}, u32[]{:S(2)}, u32[]{:S(2)}) collective-permute-start(bf16[2,16,32,128]{3,2,1,0:T(8,128)(2,1)S(1)} %get-tuple-element.45), channel_id=1, source_target_pairs={{0,4},{4,0},{8,12},{12,8},{16,20},{20,16},{24,28},{28,24},{1,5},{5... | collective-permute-start | bytes 786440 | tf_op jit(solution)/shard_map/ppermute | solution.py:301
  70.2 1.2 %collective-permute-done.13.given = bf16[2,16,32,128]{3,2,1,0:T(8,128)(2,1)S(1)} collective-permute-done((bf16[2,16,32,128]{3,2,1,0:T(8,128)(2,1)S(1)}, bf16[2,16,32,128]{3,2,1,0:T(8,128)(2,1)S(1)}, u32[]{:S(2)}, u32[]{:S(2)}) %collective-permute-start.13) | collective-permute-done | bytes 262176 | tf_op jit(solution)/shard_map/ppermute | solution.py:301
  71.3 0.8 %lay.1 = bf16[32,64,128]{2,1,0:T(8,128)(2,1)} custom-call(s32[1]{0:T(128)} %bitcast.place, bf16[2,16,32,128]{3,2,1,0:T(8,128)(2,1)S(1)} %get-tuple-element.46.kept, bf16[2,16,32,128]{3,2,1,0:T(8,128)(2,1)S(1)} %collective-permute-done.13.given), custom_call_target="tpu_custom_call" | custom-call | tf_op jit(solution)/shard_map/lay/pallas_call | solution.py:270
  (3 shorter events, 0.1 us)
Async XLA Ops:
  0.0 24.1 %copy-start.2 = (bf16[1024,128]{1,0:T(8,128)(2,1)S(1)}, bf16[1024,128]{1,0:T(8,128)(2,1)}, u32[]{:S(2)}) copy-start(bf16[1024,128]{1,0:T(8,128)(2,1)} %w_out.1) | copy-start | bytes 786436
  5.0 9.8 %collective-permute-start.1 = (bf16[528,256]{1,0:T(8,128)(2,1)}, bf16[528,256]{1,0:T(8,128)(2,1)S(1)}, u32[]{:S(2)}, u32[]{:S(2)}) collective-permute-start(bf16[528,256]{1,0:T(8,128)(2,1)} %get-tuple-element.32.right_in), channel_id=1, source_target_pairs={{0,32},{32,64},{64,96},{96,0},{1,33},{33,65},{65,97},{97,1},{2,34}... | collective-permute-start | bytes 811016 | tf_op jit(solution)/shard_map/ppermute | solution.py:306
  7.2 7.7 %collective-permute-start = (bf16[528,256]{1,0:T(8,128)(2,1)}, bf16[528,256]{1,0:T(8,128)(2,1)S(1)}, u32[]{:S(2)}, u32[]{:S(2)}) collective-permute-start(bf16[528,256]{1,0:T(8,128)(2,1)} %get-tuple-element.32.right_in), channel_id=1, source_target_pairs={{0,96},{32,0},{64,32},{96,64},{1,97},{33,1},{65,33},{97,65},{2,98}... | collective-permute-start | bytes 811016 | tf_op jit(solution)/shard_map/ppermute | solution.py:306
  8.7 9.7 %collective-permute-start.4 = (bf16[528,256]{1,0:T(8,128)(2,1)}, bf16[528,256]{1,0:T(8,128)(2,1)S(1)}, u32[]{:S(2)}, u32[]{:S(2)}) collective-permute-start(bf16[528,256]{1,0:T(8,128)(2,1)} %get-tuple-element.27.left_in), channel_id=1, source_target_pairs={{0,8},{4,12},{8,16},{12,20},{16,24},{20,28},{24,0},{28,4},{1,9},{5... | collective-permute-start | bytes 811016 | tf_op jit(solution)/shard_map/ppermute | solution.py:305
  10.3 8.0 %collective-permute-start.3 = (bf16[528,256]{1,0:T(8,128)(2,1)}, bf16[528,256]{1,0:T(8,128)(2,1)S(1)}, u32[]{:S(2)}, u32[]{:S(2)}) collective-permute-start(bf16[528,256]{1,0:T(8,128)(2,1)} %get-tuple-element.27.left_in), channel_id=1, source_target_pairs={{0,24},{4,28},{8,0},{12,4},{16,8},{20,12},{24,16},{28,20},{1,25},{... | collective-permute-start | bytes 811016 | tf_op jit(solution)/shard_map/ppermute | solution.py:305
  14.9 9.1 %collective-permute-start.2 = (bf16[528,256]{1,0:T(8,128)(2,1)S(1)}, bf16[528,256]{1,0:T(8,128)(2,1)S(1)}, u32[]{:S(2)}, u32[]{:S(2)}) collective-permute-start(bf16[528,256]{1,0:T(8,128)(2,1)S(1)} %choose.2), channel_id=1, source_target_pairs={{0,96},{4,36},{8,104},{12,44},{16,112},{20,52},{24,120},{28,60},{3... | collective-permute-start | bytes 811016 | tf_op jit(solution)/shard_map/ppermute | solution.py:315
  18.4 8.0 %collective-permute-start.5 = (bf16[528,256]{1,0:T(8,128)(2,1)S(1)}, bf16[528,256]{1,0:T(8,128)(2,1)S(1)}, u32[]{:S(2)}, u32[]{:S(2)}) collective-permute-start(bf16[528,256]{1,0:T(8,128)(2,1)S(1)} %choose.3), channel_id=1, source_target_pairs={{0,24},{4,12},{8,0},{12,20},{16,8},{20,28},{24,16},{28,4},{32,56},... | collective-permute-start | bytes 811016 | tf_op jit(solution)/shard_map/ppermute | solution.py:315
  18.8 7.6 %collective-permute-start.6 = (bf16[528,256]{1,0:T(8,128)(2,1)}, bf16[528,256]{1,0:T(8,128)(2,1)S(1)}, u32[]{:S(2)}, u32[]{:S(2)}) collective-permute-start(bf16[528,256]{1,0:T(8,128)(2,1)} %get-tuple-element.32.right_in), channel_id=1, source_target_pairs={{0,4},{4,0},{8,12},{12,8},{16,20},{20,16},{24,28},{28,24},{1,5},{5... | collective-permute-start | bytes 811016 | tf_op jit(solution)/shard_map/ppermute | solution.py:301
  23.5 2.9 %collective-permute-start.7 = (bf16[528,256]{1,0:T(8,128)(2,1)S(1)}, bf16[528,256]{1,0:T(8,128)(2,1)S(1)}, u32[]{:S(2)}, u32[]{:S(2)}) collective-permute-start(bf16[528,256]{1,0:T(8,128)(2,1)S(1)} %collective-permute-done.a.refs_6_), channel_id=1, source_target_pairs={{0,4},{4,0},{8,12},{12,8},{16,20},{20,16},{24,28},{28,24},{1,5},{5... | collective-permute-start | bytes 811016 | tf_op jit(solution)/shard_map/ppermute | solution.py:301
  23.5 2.9 %collective-permute-start.9 = (bf16[528,256]{1,0:T(8,128)(2,1)S(1)}, bf16[528,256]{1,0:T(8,128)(2,1)S(1)}, u32[]{:S(2)}, u32[]{:S(2)}) collective-permute-start(bf16[528,256]{1,0:T(8,128)(2,1)S(1)} %collective-permute-done.1.b.refs_10_), channel_id=1, source_target_pairs={{0,4},{4,0},{8,12},{12,8},{16,20},{20,16},{24,28},{28,24},{1,5},{5... | collective-permute-start | bytes 811016 | tf_op jit(solution)/shard_map/ppermute | solution.py:301
  24.0 2.4 %collective-permute-start.8 = (bf16[528,256]{1,0:T(8,128)(2,1)S(1)}, bf16[528,256]{1,0:T(8,128)(2,1)S(1)}, u32[]{:S(2)}, u32[]{:S(2)}) collective-permute-start(bf16[528,256]{1,0:T(8,128)(2,1)S(1)} %collective-permute-done.2.refs_8_), channel_id=1, source_target_pairs={{0,4},{4,0},{8,12},{12,8},{16,20},{20,16},{24,28},{28,24},{1,5},{5... | collective-permute-start | bytes 811016 | tf_op jit(solution)/shard_map/ppermute | solution.py:301
  24.1 1.0 %copy-start = (bf16[528,256]{1,0:T(8,128)(2,1)S(1)}, bf16[528,256]{1,0:T(8,128)(2,1)}, u32[]{:S(2)}) copy-start(bf16[528,256]{1,0:T(8,128)(2,1)} %get-tuple-element.32.right_in) | copy-start | bytes 811012
  25.1 1.0 %copy-start.1 = (bf16[528,256]{1,0:T(8,128)(2,1)S(1)}, bf16[528,256]{1,0:T(8,128)(2,1)}, u32[]{:S(2)}) copy-start(bf16[528,256]{1,0:T(8,128)(2,1)} %get-tuple-element.27.left_in) | copy-start | bytes 811012
  28.6 14.3 %collective-permute-start.10 = (bf16[2080,128]{1,0:T(8,128)(2,1)S(1)}, bf16[2080,128]{1,0:T(8,128)(2,1)S(1)}, u32[]{:S(2)}, u32[]{:S(2)}) collective-permute-start(bf16[2080,128]{1,0:T(8,128)(2,1)S(1)} %get-tuple-element.40), channel_id=1, source_target_pairs={{0,2},{1,3},{2,0},{3,1},{4,6},{5,7},{6,4},{7,5},{8,10},{9,11},{10,... | collective-permute-start | bytes 1597448 | tf_op jit(solution)/shard_map/ppermute | solution.py:332
  38.2 17.0 %collective-permute-start.11 = (bf16[2080,128]{1,0:T(8,128)(2,1)}, bf16[2080,128]{1,0:T(8,128)(2,1)S(1)}, u32[]{:S(2)}, u32[]{:S(2)}) collective-permute-start(bf16[2080,128]{1,0:T(8,128)(2,1)} %get-tuple-element.43), channel_id=1, source_target_pairs={{0,1},{1,2},{2,3},{3,0},{4,5},{5,6},{6,7},{7,4},{8,9},{9,10},{10,1... | collective-permute-start | bytes 1597448 | tf_op jit(solution)/shard_map/ppermute | solution.py:334
  38.5 16.7 %collective-permute-start.12 = (bf16[2080,128]{1,0:T(8,128)(2,1)}, bf16[2080,128]{1,0:T(8,128)(2,1)S(1)}, u32[]{:S(2)}, u32[]{:S(2)}) collective-permute-start(bf16[2080,128]{1,0:T(8,128)(2,1)} %get-tuple-element.44), channel_id=1, source_target_pairs={{0,3},{1,0},{2,1},{3,2},{4,7},{5,4},{6,5},{7,6},{8,11},{9,8},{10,9... | collective-permute-start | bytes 1597448 | tf_op jit(solution)/shard_map/ppermute | solution.py:335
  68.6 2.7 %collective-permute-start.13 = (bf16[2,16,32,128]{3,2,1,0:T(8,128)(2,1)S(1)}, bf16[2,16,32,128]{3,2,1,0:T(8,128)(2,1)S(1)}, u32[]{:S(2)}, u32[]{:S(2)}) collective-permute-start(bf16[2,16,32,128]{3,2,1,0:T(8,128)(2,1)S(1)} %get-tuple-element.45), channel_id=1, source_target_pairs={{0,4},{4,0},{8,12},{12,8},{16,20},{20,16},{24,28},{28,24},{1,5},{5... | collective-permute-start | bytes 786440 | tf_op jit(solution)/shard_map/ppermute | solution.py:301

commit v6 on v5

--- a/solution.py
+++ b/solution.py
@@ -18,7 +18,7 @@
 SHARD = RES * HID
 ROWS = SHARD + RES
 WIDE = 8 * RES
-BIG = 56 * 2**20
+BIG = 62 * 2**20
 
 
 def dot(a, b, dims):

time: 72.4 us -> 72.4 us (level)
  no operation moved by 1% of the time
where the time goes in v6:
time: 72.4 us; the launch traced here: 72.1 us
  starting transfers between devices  21.2 us (29%)
  waiting for transfers between devices  20.3 us (28%)
  Pallas kernels  16.3 us (23%)
  blocking collectives  12.2 us (17%)
  local copies, waits for them, and re-layouts  2.03 us (3%)
    ppermute x1, waiting for transfers between devices, per_device(): got[1] = lax.ppermute(ahead, 'depth', shift_pairs(4, 1))  12.2 us
    all_to_all x1, blocking collectives, per_device(): lax.all_to_all(pieces, 'col', 0, 0, axis_index_groups=[[0, 2, 4, 6], [5,...  12.2 us
    pallas_call x2, Pallas kernels, pair(): pl.pallas_call(functools.partial(pair_kernel, first), in_specs=[pl.BlockS...  8.7 us
    ppermute x5, starting transfers between devices, per_device(): flip = lambda v: lax.ppermute(v, 'col', [(s, s ^ 1) for s in range(8)])  6.77 us
    pallas_call x1, Pallas kernels, project(): pl.pallas_call(project_kernel, grid=(steps,), in_specs=[pl.BlockSpec((hal...  5.04 us
    ppermute x2, starting transfers between devices, per_device(): lefts[t] = lax.ppermute(left, 'col', shift_pairs(8, -2 * t))  3.76 us
    ppermute x2, starting transfers between devices, per_device(): rights[t] = lax.ppermute(right, 'row', shift_pairs(4, -t))  3.64 us
    ppermute x1, starting transfers between devices, per_device(): got[2] = lax.ppermute(part, 'depth', shift_pairs(4, 2))  3.01 us
  transfers between devices with their start and end apart: 14, of which 5 were waited for; matrix products, arithmetic and copies ran while one was open for 0% of the time, Pallas kernels for 10%

profile of v6, /device:TPU:1, one launch (start us, length us, event | category | flops | bytes accessed | tf_op | source)
XLA Modules:
  0.0 72.1 jit_solution(3025647424633064099)
XLA Ops:
  0.0 0.0 copy-start.2
  0.0 5.0 %project.1 = (bf16[528,256]{1,0:T(8,128)(2,1)}, bf16[528,256]{1,0:T(8,128)(2,1)}) custom-call(bf16[256,16,256]{2,1,0:T(8,128)(2,1)} %sig.1, bf16[16,256]{1,0:T(8,128)(2,1)} %bitcast.23, f32[1,256]{1,0:T(1,128)} %bitcast.24, f32[1,256]{1,0:T(1,128)} %bitcast.25, bf16[32,256]{1,0:T(8,128)(2,1)} %bitcast.21, f32[1,32]{1,0:T(1,128)} %bitcast.26, ...), custom_call_target="tpu_custom_call" | custom-call | tf_op jit(solution)/shard_map/project/pallas_call | solution.py:68
  5.0 2.1 %collective-permute-start.1 = (bf16[528,256]{1,0:T(8,128)(2,1)}, bf16[528,256]{1,0:T(8,128)(2,1)S(1)}, u32[]{:S(2)}, u32[]{:S(2)}) collective-permute-start(bf16[528,256]{1,0:T(8,128)(2,1)} %get-tuple-element.32.right_in), channel_id=1, source_target_pairs={{0,32},{32,64},{64,96},{96,0},{1,33},{33,65},{65,97},{97,1},{2,34}... | collective-permute-start | bytes 811016 | tf_op jit(solution)/shard_map/ppermute | solution.py:306
  7.2 1.5 %collective-permute-start = (bf16[528,256]{1,0:T(8,128)(2,1)}, bf16[528,256]{1,0:T(8,128)(2,1)S(1)}, u32[]{:S(2)}, u32[]{:S(2)}) collective-permute-start(bf16[528,256]{1,0:T(8,128)(2,1)} %get-tuple-element.32.right_in), channel_id=1, source_target_pairs={{0,96},{32,0},{64,32},{96,64},{1,97},{33,1},{65,33},{97,65},{2,98}... | collective-permute-start | bytes 811016 | tf_op jit(solution)/shard_map/ppermute | solution.py:306
  8.7 1.6 %collective-permute-start.4 = (bf16[528,256]{1,0:T(8,128)(2,1)}, bf16[528,256]{1,0:T(8,128)(2,1)S(1)}, u32[]{:S(2)}, u32[]{:S(2)}) collective-permute-start(bf16[528,256]{1,0:T(8,128)(2,1)} %get-tuple-element.27.left_in), channel_id=1, source_target_pairs={{0,8},{4,12},{8,16},{12,20},{16,24},{20,28},{24,0},{28,4},{1,9},{5... | collective-permute-start | bytes 811016 | tf_op jit(solution)/shard_map/ppermute | solution.py:305
  10.3 2.1 %collective-permute-start.3 = (bf16[528,256]{1,0:T(8,128)(2,1)}, bf16[528,256]{1,0:T(8,128)(2,1)S(1)}, u32[]{:S(2)}, u32[]{:S(2)}) collective-permute-start(bf16[528,256]{1,0:T(8,128)(2,1)} %get-tuple-element.27.left_in), channel_id=1, source_target_pairs={{0,24},{4,28},{8,0},{12,4},{16,8},{20,12},{24,16},{28,20},{1,25},{... | collective-permute-start | bytes 811016 | tf_op jit(solution)/shard_map/ppermute | solution.py:305
  12.4 2.4 %collective-permute-done.1.b.refs_10_ = bf16[528,256]{1,0:T(8,128)(2,1)S(1)} collective-permute-done((bf16[528,256]{1,0:T(8,128)(2,1)}, bf16[528,256]{1,0:T(8,128)(2,1)S(1)}, u32[]{:S(2)}, u32[]{:S(2)}) %collective-permute-start.1) | collective-permute-done | bytes 270368 | tf_op jit(solution)/shard_map/ppermute | solution.py:306
  14.9 0.0 collective-permute-done.a.refs_6_
  14.9 0.9 %collective-permute-start.2 = (bf16[528,256]{1,0:T(8,128)(2,1)S(1)}, bf16[528,256]{1,0:T(8,128)(2,1)S(1)}, u32[]{:S(2)}, u32[]{:S(2)}) collective-permute-start(bf16[528,256]{1,0:T(8,128)(2,1)S(1)} %choose.2), channel_id=1, source_target_pairs={{0,96},{4,36},{8,104},{12,44},{16,112},{20,52},{24,120},{28,60},{3... | collective-permute-start | bytes 811016 | tf_op jit(solution)/shard_map/ppermute | solution.py:315
  15.8 2.6 %collective-permute-done.4.b.refs_3_ = bf16[528,256]{1,0:T(8,128)(2,1)S(1)} collective-permute-done((bf16[528,256]{1,0:T(8,128)(2,1)}, bf16[528,256]{1,0:T(8,128)(2,1)S(1)}, u32[]{:S(2)}, u32[]{:S(2)}) %collective-permute-start.4) | collective-permute-done | bytes 270368 | tf_op jit(solution)/shard_map/ppermute | solution.py:305
  18.4 0.0 collective-permute-done.3.a.refs_1_
  18.4 0.5 collective-permute-start.5
  18.8 4.7 %collective-permute-start.6 = (bf16[528,256]{1,0:T(8,128)(2,1)}, bf16[528,256]{1,0:T(8,128)(2,1)S(1)}, u32[]{:S(2)}, u32[]{:S(2)}) collective-permute-start(bf16[528,256]{1,0:T(8,128)(2,1)} %get-tuple-element.32.right_in), channel_id=1, source_target_pairs={{0,4},{4,0},{8,12},{12,8},{16,20},{20,16},{24,28},{28,24},{1,5},{5... | collective-permute-start | bytes 811016 | tf_op jit(solution)/shard_map/ppermute | solution.py:301
  23.5 0.0 collective-permute-start.7
  23.5 0.5 collective-permute-start.9
  24.0 0.0 collective-permute-done.2.refs_8_
  24.0 0.0 collective-permute-start.8
  24.0 0.1 pad_add_fusion.place
  24.1 0.0 copy-done.2
  24.1 0.0 copy-start
  24.1 1.0 %copy-done = bf16[528,256]{1,0:T(8,128)(2,1)S(1)} copy-done((bf16[528,256]{1,0:T(8,128)(2,1)S(1)}, bf16[528,256]{1,0:T(8,128)(2,1)}, u32[]{:S(2)}) %copy-start) | copy-done | bytes 270360
  25.1 0.0 copy-start.1
  25.1 1.0 %copy-done.1 = bf16[528,256]{1,0:T(8,128)(2,1)S(1)} copy-done((bf16[528,256]{1,0:T(8,128)(2,1)S(1)}, bf16[528,256]{1,0:T(8,128)(2,1)}, u32[]{:S(2)}) %copy-start.1) | copy-done | bytes 270360
  26.0 0.4 order.1
  26.4 0.0 collective-permute-done.5.refs_2_
  26.4 0.0 collective-permute-done.6.refs_5_
  26.4 0.0 collective-permute-done.7.refs_7_
  26.5 0.0 collective-permute-done.9.refs_11_
  26.5 0.0 collective-permute-done.8.refs_9_
  26.5 2.1 %pair_first.1 = (bf16[2080,128]{1,0:T(8,128)(2,1)S(1)}, bf16[12,528,256]{2,1,0:T(8,128)(2,1)S(1)}) custom-call(s32[1]{0:T(128)} %bitcast.12.place, bf16[528,256]{1,0:T(8,128)(2,1)S(1)} %get-tuple-element.29.refs_0_, bf16[528,256]{1,0:T(8,128)(2,1)S(1)} %collective-permute-done.3.a.refs_1_, bf16[528,256]{1,0:T(8,128)(2,1)S(1)} %collective-permute-done.5.refs_2_, ...), custom_call_target="tpu_custom_call" | custom-call | flops 268435456 | bytes 65536 | tf_op jit(solution)/shard_map/pair_first/pallas_call | solution.py:198
  28.6 3.0 %collective-permute-start.10 = (bf16[2080,128]{1,0:T(8,128)(2,1)S(1)}, bf16[2080,128]{1,0:T(8,128)(2,1)S(1)}, u32[]{:S(2)}, u32[]{:S(2)}) collective-permute-start(bf16[2080,128]{1,0:T(8,128)(2,1)S(1)} %get-tuple-element.40), channel_id=1, source_target_pairs={{0,2},{1,3},{2,0},{3,1},{4,6},{5,7},{6,4},{7,5},{8,10},{9,11},{10,... | collective-permute-start | bytes 1597448 | tf_op jit(solution)/shard_map/ppermute | solution.py:332
  31.6 6.6 %pair_rest.1 = (bf16[2080,128]{1,0:T(8,128)(2,1)}, bf16[2080,128]{1,0:T(8,128)(2,1)}, f32[2048,128]{1,0:T(8,128)S(1)}, f32[16,128]{1,0:T(8,128)S(1)}) custom-call(s32[3]{0:T(128)S(1)} %pad_add_fusion.place, bf16[12,528,256]{2,1,0:T(8,128)(2,1)S(1)} %get-tuple-element.37.refs_0_, bf16[128,1024]{1,0:T(8,128)(2,1)S(1)} %get-tuple-element.36.refs_12_.refs_1_), custom_call_target="tpu_custom_call" | custom-call | flops 268435456 | bytes 65536 | tf_op jit(solution)/shard_map/pair_rest/pallas_call | solution.py:198
  38.2 0.3 collective-permute-start.11
  38.5 2.4 %collective-permute-start.12 = (bf16[2080,128]{1,0:T(8,128)(2,1)}, bf16[2080,128]{1,0:T(8,128)(2,1)S(1)}, u32[]{:S(2)}, u32[]{:S(2)}) collective-permute-start(bf16[2080,128]{1,0:T(8,128)(2,1)} %get-tuple-element.44), channel_id=1, source_target_pairs={{0,3},{1,0},{2,1},{3,2},{4,7},{5,4},{6,5},{7,6},{8,11},{9,8},{10,9... | collective-permute-start | bytes 1597448 | tf_op jit(solution)/shard_map/ppermute | solution.py:335
  40.9 0.1 stack.50.place
  41.0 1.9 %collective-permute-done.10.part = bf16[2080,128]{1,0:T(8,128)(2,1)S(1)} collective-permute-done((bf16[2080,128]{1,0:T(8,128)(2,1)S(1)}, bf16[2080,128]{1,0:T(8,128)(2,1)S(1)}, u32[]{:S(2)}, u32[]{:S(2)}) %collective-permute-start.10) | collective-permute-done | bytes 532512 | tf_op jit(solution)/shard_map/ppermute | solution.py:332
  42.9 0.1 fold.1
  43.0 12.2 %collective-permute-done.11.a = bf16[2080,128]{1,0:T(8,128)(2,1)S(1)} collective-permute-done((bf16[2080,128]{1,0:T(8,128)(2,1)}, bf16[2080,128]{1,0:T(8,128)(2,1)S(1)}, u32[]{:S(2)}, u32[]{:S(2)}) %collective-permute-start.11) | collective-permute-done | bytes 532512 | tf_op jit(solution)/shard_map/ppermute | solution.py:334
  55.2 0.0 collective-permute-done.12.b
  55.2 1.2 %settle.1 = bf16[4,16,32,128]{3,2,1,0:T(8,128)(2,1)S(1)} custom-call(s32[8]{0:T(128)S(1)} %stack.50.place, f32[2048,128]{1,0:T(8,128)S(1)} %get-tuple-element.41.mine, f32[16,128]{1,0:T(8,128)S(1)} %get-tuple-element.42.count, bf16[2080,128]{1,0:T(8,128)(2,1)S(1)} %collective-permute-done.11.a, bf16[2080,128]{1,0:T(8,128)(2,1)S(1)} %collective-permute-done.12.b), custom_call_target="tpu_custom_call" | custom-call | tf_op jit(solution)/shard_map/settle/pallas_call | solution.py:248
  56.4 12.2 %all_to_all.5 = bf16[4,16,32,128]{3,2,1,0:T(8,128)(2,1)S(1)} all-to-all(bf16[4,16,32,128]{3,2,1,0:T(8,128)(2,1)S(1)} %settle.1), channel_id=1, replica_groups={{0,8,16,24},{20,28,4,12},{1,9,17,25},{21,29,5,13},{2,10,18,26},{22,30,6..., dimensions={0} | all-to-all | bytes 1048576 | tf_op jit(solution)/shard_map/all_to_all | solution.py:344
  68.6 1.6 %collective-permute-start.13 = (bf16[2,16,32,128]{3,2,1,0:T(8,128)(2,1)S(1)}, bf16[2,16,32,128]{3,2,1,0:T(8,128)(2,1)S(1)}, u32[]{:S(2)}, u32[]{:S(2)}) collective-permute-start(bf16[2,16,32,128]{3,2,1,0:T(8,128)(2,1)S(1)} %get-tuple-element.45), channel_id=1, source_target_pairs={{0,4},{4,0},{8,12},{12,8},{16,20},{20,16},{24,28},{28,24},{1,5},{5... | collective-permute-start | bytes 786440 | tf_op jit(solution)/shard_map/ppermute | solution.py:301
  70.2 1.2 %collective-permute-done.13.given = bf16[2,16,32,128]{3,2,1,0:T(8,128)(2,1)S(1)} collective-permute-done((bf16[2,16,32,128]{3,2,1,0:T(8,128)(2,1)S(1)}, bf16[2,16,32,128]{3,2,1,0:T(8,128)(2,1)S(1)}, u32[]{:S(2)}, u32[]{:S(2)}) %collective-permute-start.13) | collective-permute-done | bytes 262176 | tf_op jit(solution)/shard_map/ppermute | solution.py:301
  71.3 0.8 %lay.1 = bf16[32,64,128]{2,1,0:T(8,128)(2,1)} custom-call(s32[1]{0:T(128)} %bitcast.place, bf16[2,16,32,128]{3,2,1,0:T(8,128)(2,1)S(1)} %get-tuple-element.46.kept, bf16[2,16,32,128]{3,2,1,0:T(8,128)(2,1)S(1)} %collective-permute-done.13.given), custom_call_target="tpu_custom_call" | custom-call | tf_op jit(solution)/shard_map/lay/pallas_call | solution.py:270
  (3 shorter events, 0.1 us)
Async XLA Ops:
  0.0 24.1 %copy-start.2 = (bf16[1024,128]{1,0:T(8,128)(2,1)S(1)}, bf16[1024,128]{1,0:T(8,128)(2,1)}, u32[]{:S(2)}) copy-start(bf16[1024,128]{1,0:T(8,128)(2,1)} %w_out.1) | copy-start | bytes 786436
  5.0 9.8 %collective-permute-start.1 = (bf16[528,256]{1,0:T(8,128)(2,1)}, bf16[528,256]{1,0:T(8,128)(2,1)S(1)}, u32[]{:S(2)}, u32[]{:S(2)}) collective-permute-start(bf16[528,256]{1,0:T(8,128)(2,1)} %get-tuple-element.32.right_in), channel_id=1, source_target_pairs={{0,32},{32,64},{64,96},{96,0},{1,33},{33,65},{65,97},{97,1},{2,34}... | collective-permute-start | bytes 811016 | tf_op jit(solution)/shard_map/ppermute | solution.py:306
  7.2 7.7 %collective-permute-start = (bf16[528,256]{1,0:T(8,128)(2,1)}, bf16[528,256]{1,0:T(8,128)(2,1)S(1)}, u32[]{:S(2)}, u32[]{:S(2)}) collective-permute-start(bf16[528,256]{1,0:T(8,128)(2,1)} %get-tuple-element.32.right_in), channel_id=1, source_target_pairs={{0,96},{32,0},{64,32},{96,64},{1,97},{33,1},{65,33},{97,65},{2,98}... | collective-permute-start | bytes 811016 | tf_op jit(solution)/shard_map/ppermute | solution.py:306
  8.7 9.7 %collective-permute-start.4 = (bf16[528,256]{1,0:T(8,128)(2,1)}, bf16[528,256]{1,0:T(8,128)(2,1)S(1)}, u32[]{:S(2)}, u32[]{:S(2)}) collective-permute-start(bf16[528,256]{1,0:T(8,128)(2,1)} %get-tuple-element.27.left_in), channel_id=1, source_target_pairs={{0,8},{4,12},{8,16},{12,20},{16,24},{20,28},{24,0},{28,4},{1,9},{5... | collective-permute-start | bytes 811016 | tf_op jit(solution)/shard_map/ppermute | solution.py:305
  10.3 8.0 %collective-permute-start.3 = (bf16[528,256]{1,0:T(8,128)(2,1)}, bf16[528,256]{1,0:T(8,128)(2,1)S(1)}, u32[]{:S(2)}, u32[]{:S(2)}) collective-permute-start(bf16[528,256]{1,0:T(8,128)(2,1)} %get-tuple-element.27.left_in), channel_id=1, source_target_pairs={{0,24},{4,28},{8,0},{12,4},{16,8},{20,12},{24,16},{28,20},{1,25},{... | collective-permute-start | bytes 811016 | tf_op jit(solution)/shard_map/ppermute | solution.py:305
  14.9 9.1 %collective-permute-start.2 = (bf16[528,256]{1,0:T(8,128)(2,1)S(1)}, bf16[528,256]{1,0:T(8,128)(2,1)S(1)}, u32[]{:S(2)}, u32[]{:S(2)}) collective-permute-start(bf16[528,256]{1,0:T(8,128)(2,1)S(1)} %choose.2), channel_id=1, source_target_pairs={{0,96},{4,36},{8,104},{12,44},{16,112},{20,52},{24,120},{28,60},{3... | collective-permute-start | bytes 811016 | tf_op jit(solution)/shard_map/ppermute | solution.py:315
  18.4 8.0 %collective-permute-start.5 = (bf16[528,256]{1,0:T(8,128)(2,1)S(1)}, bf16[528,256]{1,0:T(8,128)(2,1)S(1)}, u32[]{:S(2)}, u32[]{:S(2)}) collective-permute-start(bf16[528,256]{1,0:T(8,128)(2,1)S(1)} %choose.3), channel_id=1, source_target_pairs={{0,24},{4,12},{8,0},{12,20},{16,8},{20,28},{24,16},{28,4},{32,56},... | collective-permute-start | bytes 811016 | tf_op jit(solution)/shard_map/ppermute | solution.py:315
  18.8 7.6 %collective-permute-start.6 = (bf16[528,256]{1,0:T(8,128)(2,1)}, bf16[528,256]{1,0:T(8,128)(2,1)S(1)}, u32[]{:S(2)}, u32[]{:S(2)}) collective-permute-start(bf16[528,256]{1,0:T(8,128)(2,1)} %get-tuple-element.32.right_in), channel_id=1, source_target_pairs={{0,4},{4,0},{8,12},{12,8},{16,20},{20,16},{24,28},{28,24},{1,5},{5... | collective-permute-start | bytes 811016 | tf_op jit(solution)/shard_map/ppermute | solution.py:301
  23.5 2.9 %collective-permute-start.7 = (bf16[528,256]{1,0:T(8,128)(2,1)S(1)}, bf16[528,256]{1,0:T(8,128)(2,1)S(1)}, u32[]{:S(2)}, u32[]{:S(2)}) collective-permute-start(bf16[528,256]{1,0:T(8,128)(2,1)S(1)} %collective-permute-done.a.refs_6_), channel_id=1, source_target_pairs={{0,4},{4,0},{8,12},{12,8},{16,20},{20,16},{24,28},{28,24},{1,5},{5... | collective-permute-start | bytes 811016 | tf_op jit(solution)/shard_map/ppermute | solution.py:301
  23.5 2.9 %collective-permute-start.9 = (bf16[528,256]{1,0:T(8,128)(2,1)S(1)}, bf16[528,256]{1,0:T(8,128)(2,1)S(1)}, u32[]{:S(2)}, u32[]{:S(2)}) collective-permute-start(bf16[528,256]{1,0:T(8,128)(2,1)S(1)} %collective-permute-done.1.b.refs_10_), channel_id=1, source_target_pairs={{0,4},{4,0},{8,12},{12,8},{16,20},{20,16},{24,28},{28,24},{1,5},{5... | collective-permute-start | bytes 811016 | tf_op jit(solution)/shard_map/ppermute | solution.py:301
  24.0 2.4 %collective-permute-start.8 = (bf16[528,256]{1,0:T(8,128)(2,1)S(1)}, bf16[528,256]{1,0:T(8,128)(2,1)S(1)}, u32[]{:S(2)}, u32[]{:S(2)}) collective-permute-start(bf16[528,256]{1,0:T(8,128)(2,1)S(1)} %collective-permute-done.2.refs_8_), channel_id=1, source_target_pairs={{0,4},{4,0},{8,12},{12,8},{16,20},{20,16},{24,28},{28,24},{1,5},{5... | collective-permute-start | bytes 811016 | tf_op jit(solution)/shard_map/ppermute | solution.py:301
  24.1 1.0 %copy-start = (bf16[528,256]{1,0:T(8,128)(2,1)S(1)}, bf16[528,256]{1,0:T(8,128)(2,1)}, u32[]{:S(2)}) copy-start(bf16[528,256]{1,0:T(8,128)(2,1)} %get-tuple-element.32.right_in) | copy-start | bytes 811012
  25.1 1.0 %copy-start.1 = (bf16[528,256]{1,0:T(8,128)(2,1)S(1)}, bf16[528,256]{1,0:T(8,128)(2,1)}, u32[]{:S(2)}) copy-start(bf16[528,256]{1,0:T(8,128)(2,1)} %get-tuple-element.27.left_in) | copy-start | bytes 811012
  28.6 14.3 %collective-permute-start.10 = (bf16[2080,128]{1,0:T(8,128)(2,1)S(1)}, bf16[2080,128]{1,0:T(8,128)(2,1)S(1)}, u32[]{:S(2)}, u32[]{:S(2)}) collective-permute-start(bf16[2080,128]{1,0:T(8,128)(2,1)S(1)} %get-tuple-element.40), channel_id=1, source_target_pairs={{0,2},{1,3},{2,0},{3,1},{4,6},{5,7},{6,4},{7,5},{8,10},{9,11},{10,... | collective-permute-start | bytes 1597448 | tf_op jit(solution)/shard_map/ppermute | solution.py:332
  38.2 17.0 %collective-permute-start.11 = (bf16[2080,128]{1,0:T(8,128)(2,1)}, bf16[2080,128]{1,0:T(8,128)(2,1)S(1)}, u32[]{:S(2)}, u32[]{:S(2)}) collective-permute-start(bf16[2080,128]{1,0:T(8,128)(2,1)} %get-tuple-element.43), channel_id=1, source_target_pairs={{0,1},{1,2},{2,3},{3,0},{4,5},{5,6},{6,7},{7,4},{8,9},{9,10},{10,1... | collective-permute-start | bytes 1597448 | tf_op jit(solution)/shard_map/ppermute | solution.py:334
  38.5 16.7 %collective-permute-start.12 = (bf16[2080,128]{1,0:T(8,128)(2,1)}, bf16[2080,128]{1,0:T(8,128)(2,1)S(1)}, u32[]{:S(2)}, u32[]{:S(2)}) collective-permute-start(bf16[2080,128]{1,0:T(8,128)(2,1)} %get-tuple-element.44), channel_id=1, source_target_pairs={{0,3},{1,0},{2,1},{3,2},{4,7},{5,4},{6,5},{7,6},{8,11},{9,8},{10,9... | collective-permute-start | bytes 1597448 | tf_op jit(solution)/shard_map/ppermute | solution.py:335
  68.6 2.7 %collective-permute-start.13 = (bf16[2,16,32,128]{3,2,1,0:T(8,128)(2,1)S(1)}, bf16[2,16,32,128]{3,2,1,0:T(8,128)(2,1)S(1)}, u32[]{:S(2)}, u32[]{:S(2)}) collective-permute-start(bf16[2,16,32,128]{3,2,1,0:T(8,128)(2,1)S(1)} %get-tuple-element.45), channel_id=1, source_target_pairs={{0,4},{4,0},{8,12},{12,8},{16,20},{20,16},{24,28},{28,24},{1,5},{5... | collective-permute-start | bytes 786440 | tf_op jit(solution)/shard_map/ppermute | solution.py:301

commit v7 on v6

--- a/solution.py
+++ b/solution.py
@@ -317,7 +317,7 @@
     which = core.astype(jnp.int32).reshape(1)
     rights[2] = relay(choose(which, rights[1], rights[3]), "row")
     passed = choose(which, lefts[1], lefts[3])
-    own, rights[1], rights[3], passed = lax.optimization_barrier((right, rights[1], rights[3], passed))
+    own, passed = lax.optimization_barrier((right, passed))
     lefts[2] = relay(passed, "col")
     late_left, late_right, rights[2] = lax.optimization_barrier((left, right, rights[2]))
     mix, lefts[0], rights[0] = order(w_out, late_left, late_right)

time: 72.4 us -> 72.4 us (level)
  no operation moved by 1% of the time
where the time goes in v7:
time: 72.4 us; the launch traced here: 72.2 us
  starting transfers between devices  21.2 us (29%)
  waiting for transfers between devices  20.3 us (28%)
  Pallas kernels  16.3 us (23%)
  blocking collectives  12.1 us (17%)
  local copies, waits for them, and re-layouts  2.03 us (3%)
    ppermute x1, waiting for transfers between devices, per_device(): got[1] = lax.ppermute(ahead, 'depth', shift_pairs(4, 1))  12.2 us
    all_to_all x1, blocking collectives, per_device(): lax.all_to_all(pieces, 'col', 0, 0, axis_index_groups=[[0, 2, 4, 6], [5,...  12.1 us
    pallas_call x2, Pallas kernels, pair(): pl.pallas_call(functools.partial(pair_kernel, first), in_specs=[pl.BlockS...  8.72 us
    ppermute x5, starting transfers between devices, per_device(): flip = lambda v: lax.ppermute(v, 'col', [(s, s ^ 1) for s in range(8)])  6.8 us
    pallas_call x1, Pallas kernels, project(): pl.pallas_call(project_kernel, grid=(steps,), in_specs=[pl.BlockSpec((hal...  5.04 us
    ppermute x2, starting transfers between devices, per_device(): lefts[t] = lax.ppermute(left, 'col', shift_pairs(8, -2 * t))  3.76 us
    ppermute x2, starting transfers between devices, per_device(): rights[t] = lax.ppermute(right, 'row', shift_pairs(4, -t))  3.64 us
    ppermute x1, starting transfers between devices, per_device(): got[2] = lax.ppermute(part, 'depth', shift_pairs(4, 2))  3 us
  transfers between devices with their start and end apart: 14, of which 5 were waited for; matrix products, arithmetic and copies ran while one was open for 0% of the time, Pallas kernels for 10%

profile of v7, /device:TPU:1, one launch (start us, length us, event | category | flops | bytes accessed | tf_op | source)
XLA Modules:
  0.0 72.2 jit_solution(3338987658661469136)
XLA Ops:
  0.0 0.0 copy-start.2
  0.0 5.0 %project.1 = (bf16[528,256]{1,0:T(8,128)(2,1)}, bf16[528,256]{1,0:T(8,128)(2,1)}) custom-call(bf16[256,16,256]{2,1,0:T(8,128)(2,1)} %sig.1, bf16[16,256]{1,0:T(8,128)(2,1)} %bitcast.23, f32[1,256]{1,0:T(1,128)} %bitcast.24, f32[1,256]{1,0:T(1,128)} %bitcast.25, bf16[32,256]{1,0:T(8,128)(2,1)} %bitcast.21, f32[1,32]{1,0:T(1,128)} %bitcast.26, ...), custom_call_target="tpu_custom_call" | custom-call | tf_op jit(solution)/shard_map/project/pallas_call | solution.py:68
  5.0 2.1 %collective-permute-start.1 = (bf16[528,256]{1,0:T(8,128)(2,1)}, bf16[528,256]{1,0:T(8,128)(2,1)S(1)}, u32[]{:S(2)}, u32[]{:S(2)}) collective-permute-start(bf16[528,256]{1,0:T(8,128)(2,1)} %get-tuple-element.30.right_in), channel_id=1, source_target_pairs={{0,32},{32,64},{64,96},{96,0},{1,33},{33,65},{65,97},{97,1},{2,34}... | collective-permute-start | bytes 811016 | tf_op jit(solution)/shard_map/ppermute | solution.py:306
  7.2 1.5 %collective-permute-start = (bf16[528,256]{1,0:T(8,128)(2,1)}, bf16[528,256]{1,0:T(8,128)(2,1)S(1)}, u32[]{:S(2)}, u32[]{:S(2)}) collective-permute-start(bf16[528,256]{1,0:T(8,128)(2,1)} %get-tuple-element.30.right_in), channel_id=1, source_target_pairs={{0,96},{32,0},{64,32},{96,64},{1,97},{33,1},{65,33},{97,65},{2,98}... | collective-permute-start | bytes 811016 | tf_op jit(solution)/shard_map/ppermute | solution.py:306
  8.7 1.6 %collective-permute-start.4 = (bf16[528,256]{1,0:T(8,128)(2,1)}, bf16[528,256]{1,0:T(8,128)(2,1)S(1)}, u32[]{:S(2)}, u32[]{:S(2)}) collective-permute-start(bf16[528,256]{1,0:T(8,128)(2,1)} %get-tuple-element.25.left_in), channel_id=1, source_target_pairs={{0,8},{4,12},{8,16},{12,20},{16,24},{20,28},{24,0},{28,4},{1,9},{5... | collective-permute-start | bytes 811016 | tf_op jit(solution)/shard_map/ppermute | solution.py:305
  10.3 2.1 %collective-permute-start.3 = (bf16[528,256]{1,0:T(8,128)(2,1)}, bf16[528,256]{1,0:T(8,128)(2,1)S(1)}, u32[]{:S(2)}, u32[]{:S(2)}) collective-permute-start(bf16[528,256]{1,0:T(8,128)(2,1)} %get-tuple-element.25.left_in), channel_id=1, source_target_pairs={{0,24},{4,28},{8,0},{12,4},{16,8},{20,12},{24,16},{28,20},{1,25},{... | collective-permute-start | bytes 811016 | tf_op jit(solution)/shard_map/ppermute | solution.py:305
  12.4 2.4 %collective-permute-done.1.b.refs_10_ = bf16[528,256]{1,0:T(8,128)(2,1)S(1)} collective-permute-done((bf16[528,256]{1,0:T(8,128)(2,1)}, bf16[528,256]{1,0:T(8,128)(2,1)S(1)}, u32[]{:S(2)}, u32[]{:S(2)}) %collective-permute-start.1) | collective-permute-done | bytes 270368 | tf_op jit(solution)/shard_map/ppermute | solution.py:306
  14.9 0.0 collective-permute-done.a.refs_6_
  14.9 0.9 %collective-permute-start.2 = (bf16[528,256]{1,0:T(8,128)(2,1)S(1)}, bf16[528,256]{1,0:T(8,128)(2,1)S(1)}, u32[]{:S(2)}, u32[]{:S(2)}) collective-permute-start(bf16[528,256]{1,0:T(8,128)(2,1)S(1)} %choose.2), channel_id=1, source_target_pairs={{0,96},{4,36},{8,104},{12,44},{16,112},{20,52},{24,120},{28,60},{3... | collective-permute-start | bytes 811016 | tf_op jit(solution)/shard_map/ppermute | solution.py:315
  15.8 2.6 %collective-permute-done.4.b.refs_3_ = bf16[528,256]{1,0:T(8,128)(2,1)S(1)} collective-permute-done((bf16[528,256]{1,0:T(8,128)(2,1)}, bf16[528,256]{1,0:T(8,128)(2,1)S(1)}, u32[]{:S(2)}, u32[]{:S(2)}) %collective-permute-start.4) | collective-permute-done | bytes 270368 | tf_op jit(solution)/shard_map/ppermute | solution.py:305
  18.4 0.0 collective-permute-done.3.a.refs_1_
  18.4 0.5 collective-permute-start.5
  18.8 4.7 %collective-permute-start.6 = (bf16[528,256]{1,0:T(8,128)(2,1)}, bf16[528,256]{1,0:T(8,128)(2,1)S(1)}, u32[]{:S(2)}, u32[]{:S(2)}) collective-permute-start(bf16[528,256]{1,0:T(8,128)(2,1)} %get-tuple-element.30.right_in), channel_id=1, source_target_pairs={{0,4},{4,0},{8,12},{12,8},{16,20},{20,16},{24,28},{28,24},{1,5},{5... | collective-permute-start | bytes 811016 | tf_op jit(solution)/shard_map/ppermute | solution.py:301
  23.5 0.0 collective-permute-start.9
  23.5 0.5 collective-permute-start.7
  24.0 0.0 collective-permute-done.2.refs_8_
  24.0 0.0 collective-permute-start.8
  24.0 0.1 pad_add_fusion.place
  24.1 0.0 copy-done.2
  24.1 0.0 copy-start
  24.1 1.0 %copy-done = bf16[528,256]{1,0:T(8,128)(2,1)S(1)} copy-done((bf16[528,256]{1,0:T(8,128)(2,1)S(1)}, bf16[528,256]{1,0:T(8,128)(2,1)}, u32[]{:S(2)}) %copy-start) | copy-done | bytes 270360
  25.1 0.0 copy-start.1
  25.1 1.0 %copy-done.1 = bf16[528,256]{1,0:T(8,128)(2,1)S(1)} copy-done((bf16[528,256]{1,0:T(8,128)(2,1)S(1)}, bf16[528,256]{1,0:T(8,128)(2,1)}, u32[]{:S(2)}) %copy-start.1) | copy-done | bytes 270360
  26.0 0.4 order.1
  26.4 0.0 collective-permute-done.5.refs_2_
  26.4 0.0 collective-permute-done.6.refs_5_
  26.4 0.0 collective-permute-done.9.refs_11_
  26.5 0.0 collective-permute-done.7.refs_7_
  26.5 0.0 collective-permute-done.8.refs_9_
  26.5 2.1 %pair_first.1 = (bf16[2080,128]{1,0:T(8,128)(2,1)S(1)}, bf16[12,528,256]{2,1,0:T(8,128)(2,1)S(1)}) custom-call(s32[1]{0:T(128)} %bitcast.12.place, bf16[528,256]{1,0:T(8,128)(2,1)S(1)} %get-tuple-element.27.refs_0_, bf16[528,256]{1,0:T(8,128)(2,1)S(1)} %collective-permute-done.3.a.refs_1_, bf16[528,256]{1,0:T(8,128)(2,1)S(1)} %collective-permute-done.5.refs_2_, ...), custom_call_target="tpu_custom_call" | custom-call | flops 268435456 | bytes 65536 | tf_op jit(solution)/shard_map/pair_first/pallas_call | solution.py:198
  28.6 3.0 %collective-permute-start.10 = (bf16[2080,128]{1,0:T(8,128)(2,1)S(1)}, bf16[2080,128]{1,0:T(8,128)(2,1)S(1)}, u32[]{:S(2)}, u32[]{:S(2)}) collective-permute-start(bf16[2080,128]{1,0:T(8,128)(2,1)S(1)} %get-tuple-element.36), channel_id=1, source_target_pairs={{0,2},{1,3},{2,0},{3,1},{4,6},{5,7},{6,4},{7,5},{8,10},{9,11},{10,... | collective-permute-start | bytes 1597448 | tf_op jit(solution)/shard_map/ppermute | solution.py:332
  31.6 6.6 %pair_rest.1 = (bf16[2080,128]{1,0:T(8,128)(2,1)}, bf16[2080,128]{1,0:T(8,128)(2,1)}, f32[2048,128]{1,0:T(8,128)S(1)}, f32[16,128]{1,0:T(8,128)S(1)}) custom-call(s32[3]{0:T(128)S(1)} %pad_add_fusion.place, bf16[12,528,256]{2,1,0:T(8,128)(2,1)S(1)} %get-tuple-element.33.refs_0_, bf16[128,1024]{1,0:T(8,128)(2,1)S(1)} %get-tuple-element.32.refs_12_.refs_1_), custom_call_target="tpu_custom_call" | custom-call | flops 268435456 | bytes 65536 | tf_op jit(solution)/shard_map/pair_rest/pallas_call | solution.py:198
  38.2 0.3 collective-permute-start.11
  38.5 2.3 %collective-permute-start.12 = (bf16[2080,128]{1,0:T(8,128)(2,1)}, bf16[2080,128]{1,0:T(8,128)(2,1)S(1)}, u32[]{:S(2)}, u32[]{:S(2)}) collective-permute-start(bf16[2080,128]{1,0:T(8,128)(2,1)} %get-tuple-element.40), channel_id=1, source_target_pairs={{0,3},{1,0},{2,1},{3,2},{4,7},{5,4},{6,5},{7,6},{8,11},{9,8},{10,9... | collective-permute-start | bytes 1597448 | tf_op jit(solution)/shard_map/ppermute | solution.py:335
  40.9 0.1 stack.50.place
  41.0 1.9 %collective-permute-done.10.part = bf16[2080,128]{1,0:T(8,128)(2,1)S(1)} collective-permute-done((bf16[2080,128]{1,0:T(8,128)(2,1)S(1)}, bf16[2080,128]{1,0:T(8,128)(2,1)S(1)}, u32[]{:S(2)}, u32[]{:S(2)}) %collective-permute-start.10) | collective-permute-done | bytes 532512 | tf_op jit(solution)/shard_map/ppermute | solution.py:332
  42.9 0.1 fold.1
  43.0 12.2 %collective-permute-done.11.a = bf16[2080,128]{1,0:T(8,128)(2,1)S(1)} collective-permute-done((bf16[2080,128]{1,0:T(8,128)(2,1)}, bf16[2080,128]{1,0:T(8,128)(2,1)S(1)}, u32[]{:S(2)}, u32[]{:S(2)}) %collective-permute-start.11) | collective-permute-done | bytes 532512 | tf_op jit(solution)/shard_map/ppermute | solution.py:334
  55.2 0.0 collective-permute-done.12.b
  55.2 1.2 %settle.1 = bf16[4,16,32,128]{3,2,1,0:T(8,128)(2,1)S(1)} custom-call(s32[8]{0:T(128)S(1)} %stack.50.place, f32[2048,128]{1,0:T(8,128)S(1)} %get-tuple-element.37.mine, f32[16,128]{1,0:T(8,128)S(1)} %get-tuple-element.38.count, bf16[2080,128]{1,0:T(8,128)(2,1)S(1)} %collective-permute-done.11.a, bf16[2080,128]{1,0:T(8,128)(2,1)S(1)} %collective-permute-done.12.b), custom_call_target="tpu_custom_call" | custom-call | tf_op jit(solution)/shard_map/settle/pallas_call | solution.py:248
  56.4 12.1 %all_to_all.5 = bf16[4,16,32,128]{3,2,1,0:T(8,128)(2,1)S(1)} all-to-all(bf16[4,16,32,128]{3,2,1,0:T(8,128)(2,1)S(1)} %settle.1), channel_id=1, replica_groups={{0,8,16,24},{20,28,4,12},{1,9,17,25},{21,29,5,13},{2,10,18,26},{22,30,6..., dimensions={0} | all-to-all | bytes 1048576 | tf_op jit(solution)/shard_map/all_to_all | solution.py:344
  68.5 1.6 %collective-permute-start.13 = (bf16[2,16,32,128]{3,2,1,0:T(8,128)(2,1)S(1)}, bf16[2,16,32,128]{3,2,1,0:T(8,128)(2,1)S(1)}, u32[]{:S(2)}, u32[]{:S(2)}) collective-permute-start(bf16[2,16,32,128]{3,2,1,0:T(8,128)(2,1)S(1)} %get-tuple-element.41), channel_id=1, source_target_pairs={{0,4},{4,0},{8,12},{12,8},{16,20},{20,16},{24,28},{28,24},{1,5},{5... | collective-permute-start | bytes 786440 | tf_op jit(solution)/shard_map/ppermute | solution.py:301
  70.2 1.2 %collective-permute-done.13.given = bf16[2,16,32,128]{3,2,1,0:T(8,128)(2,1)S(1)} collective-permute-done((bf16[2,16,32,128]{3,2,1,0:T(8,128)(2,1)S(1)}, bf16[2,16,32,128]{3,2,1,0:T(8,128)(2,1)S(1)}, u32[]{:S(2)}, u32[]{:S(2)}) %collective-permute-start.13) | collective-permute-done | bytes 262176 | tf_op jit(solution)/shard_map/ppermute | solution.py:301
  71.3 0.8 %lay.1 = bf16[32,64,128]{2,1,0:T(8,128)(2,1)} custom-call(s32[1]{0:T(128)} %bitcast.place, bf16[2,16,32,128]{3,2,1,0:T(8,128)(2,1)S(1)} %get-tuple-element.42.kept, bf16[2,16,32,128]{3,2,1,0:T(8,128)(2,1)S(1)} %collective-permute-done.13.given), custom_call_target="tpu_custom_call" | custom-call | tf_op jit(solution)/shard_map/lay/pallas_call | solution.py:270
  (3 shorter events, 0.1 us)
Async XLA Ops:
  0.0 24.1 %copy-start.2 = (bf16[1024,128]{1,0:T(8,128)(2,1)S(1)}, bf16[1024,128]{1,0:T(8,128)(2,1)}, u32[]{:S(2)}) copy-start(bf16[1024,128]{1,0:T(8,128)(2,1)} %w_out.1) | copy-start | bytes 786436
  5.0 9.8 %collective-permute-start.1 = (bf16[528,256]{1,0:T(8,128)(2,1)}, bf16[528,256]{1,0:T(8,128)(2,1)S(1)}, u32[]{:S(2)}, u32[]{:S(2)}) collective-permute-start(bf16[528,256]{1,0:T(8,128)(2,1)} %get-tuple-element.30.right_in), channel_id=1, source_target_pairs={{0,32},{32,64},{64,96},{96,0},{1,33},{33,65},{65,97},{97,1},{2,34}... | collective-permute-start | bytes 811016 | tf_op jit(solution)/shard_map/ppermute | solution.py:306
  7.2 7.7 %collective-permute-start = (bf16[528,256]{1,0:T(8,128)(2,1)}, bf16[528,256]{1,0:T(8,128)(2,1)S(1)}, u32[]{:S(2)}, u32[]{:S(2)}) collective-permute-start(bf16[528,256]{1,0:T(8,128)(2,1)} %get-tuple-element.30.right_in), channel_id=1, source_target_pairs={{0,96},{32,0},{64,32},{96,64},{1,97},{33,1},{65,33},{97,65},{2,98}... | collective-permute-start | bytes 811016 | tf_op jit(solution)/shard_map/ppermute | solution.py:306
  8.7 9.7 %collective-permute-start.4 = (bf16[528,256]{1,0:T(8,128)(2,1)}, bf16[528,256]{1,0:T(8,128)(2,1)S(1)}, u32[]{:S(2)}, u32[]{:S(2)}) collective-permute-start(bf16[528,256]{1,0:T(8,128)(2,1)} %get-tuple-element.25.left_in), channel_id=1, source_target_pairs={{0,8},{4,12},{8,16},{12,20},{16,24},{20,28},{24,0},{28,4},{1,9},{5... | collective-permute-start | bytes 811016 | tf_op jit(solution)/shard_map/ppermute | solution.py:305
  10.3 8.0 %collective-permute-start.3 = (bf16[528,256]{1,0:T(8,128)(2,1)}, bf16[528,256]{1,0:T(8,128)(2,1)S(1)}, u32[]{:S(2)}, u32[]{:S(2)}) collective-permute-start(bf16[528,256]{1,0:T(8,128)(2,1)} %get-tuple-element.25.left_in), channel_id=1, source_target_pairs={{0,24},{4,28},{8,0},{12,4},{16,8},{20,12},{24,16},{28,20},{1,25},{... | collective-permute-start | bytes 811016 | tf_op jit(solution)/shard_map/ppermute | solution.py:305
  14.9 9.1 %collective-permute-start.2 = (bf16[528,256]{1,0:T(8,128)(2,1)S(1)}, bf16[528,256]{1,0:T(8,128)(2,1)S(1)}, u32[]{:S(2)}, u32[]{:S(2)}) collective-permute-start(bf16[528,256]{1,0:T(8,128)(2,1)S(1)} %choose.2), channel_id=1, source_target_pairs={{0,96},{4,36},{8,104},{12,44},{16,112},{20,52},{24,120},{28,60},{3... | collective-permute-start | bytes 811016 | tf_op jit(solution)/shard_map/ppermute | solution.py:315
  18.4 8.0 %collective-permute-start.5 = (bf16[528,256]{1,0:T(8,128)(2,1)S(1)}, bf16[528,256]{1,0:T(8,128)(2,1)S(1)}, u32[]{:S(2)}, u32[]{:S(2)}) collective-permute-start(bf16[528,256]{1,0:T(8,128)(2,1)S(1)} %choose.3), channel_id=1, source_target_pairs={{0,24},{4,12},{8,0},{12,20},{16,8},{20,28},{24,16},{28,4},{32,56},... | collective-permute-start | bytes 811016 | tf_op jit(solution)/shard_map/ppermute | solution.py:315
  18.8 7.6 %collective-permute-start.6 = (bf16[528,256]{1,0:T(8,128)(2,1)}, bf16[528,256]{1,0:T(8,128)(2,1)S(1)}, u32[]{:S(2)}, u32[]{:S(2)}) collective-permute-start(bf16[528,256]{1,0:T(8,128)(2,1)} %get-tuple-element.30.right_in), channel_id=1, source_target_pairs={{0,4},{4,0},{8,12},{12,8},{16,20},{20,16},{24,28},{28,24},{1,5},{5... | collective-permute-start | bytes 811016 | tf_op jit(solution)/shard_map/ppermute | solution.py:301
  23.5 2.9 %collective-permute-start.9 = (bf16[528,256]{1,0:T(8,128)(2,1)S(1)}, bf16[528,256]{1,0:T(8,128)(2,1)S(1)}, u32[]{:S(2)}, u32[]{:S(2)}) collective-permute-start(bf16[528,256]{1,0:T(8,128)(2,1)S(1)} %collective-permute-done.1.b.refs_10_), channel_id=1, source_target_pairs={{0,4},{4,0},{8,12},{12,8},{16,20},{20,16},{24,28},{28,24},{1,5},{5... | collective-permute-start | bytes 811016 | tf_op jit(solution)/shard_map/ppermute | solution.py:301
  23.5 2.9 %collective-permute-start.7 = (bf16[528,256]{1,0:T(8,128)(2,1)S(1)}, bf16[528,256]{1,0:T(8,128)(2,1)S(1)}, u32[]{:S(2)}, u32[]{:S(2)}) collective-permute-start(bf16[528,256]{1,0:T(8,128)(2,1)S(1)} %collective-permute-done.a.refs_6_), channel_id=1, source_target_pairs={{0,4},{4,0},{8,12},{12,8},{16,20},{20,16},{24,28},{28,24},{1,5},{5... | collective-permute-start | bytes 811016 | tf_op jit(solution)/shard_map/ppermute | solution.py:301
  24.0 2.4 %collective-permute-start.8 = (bf16[528,256]{1,0:T(8,128)(2,1)S(1)}, bf16[528,256]{1,0:T(8,128)(2,1)S(1)}, u32[]{:S(2)}, u32[]{:S(2)}) collective-permute-start(bf16[528,256]{1,0:T(8,128)(2,1)S(1)} %collective-permute-done.2.refs_8_), channel_id=1, source_target_pairs={{0,4},{4,0},{8,12},{12,8},{16,20},{20,16},{24,28},{28,24},{1,5},{5... | collective-permute-start | bytes 811016 | tf_op jit(solution)/shard_map/ppermute | solution.py:301
  24.1 1.0 %copy-start = (bf16[528,256]{1,0:T(8,128)(2,1)S(1)}, bf16[528,256]{1,0:T(8,128)(2,1)}, u32[]{:S(2)}) copy-start(bf16[528,256]{1,0:T(8,128)(2,1)} %get-tuple-element.30.right_in) | copy-start | bytes 811012
  25.1 1.0 %copy-start.1 = (bf16[528,256]{1,0:T(8,128)(2,1)S(1)}, bf16[528,256]{1,0:T(8,128)(2,1)}, u32[]{:S(2)}) copy-start(bf16[528,256]{1,0:T(8,128)(2,1)} %get-tuple-element.25.left_in) | copy-start | bytes 811012
  28.6 14.3 %collective-permute-start.10 = (bf16[2080,128]{1,0:T(8,128)(2,1)S(1)}, bf16[2080,128]{1,0:T(8,128)(2,1)S(1)}, u32[]{:S(2)}, u32[]{:S(2)}) collective-permute-start(bf16[2080,128]{1,0:T(8,128)(2,1)S(1)} %get-tuple-element.36), channel_id=1, source_target_pairs={{0,2},{1,3},{2,0},{3,1},{4,6},{5,7},{6,4},{7,5},{8,10},{9,11},{10,... | collective-permute-start | bytes 1597448 | tf_op jit(solution)/shard_map/ppermute | solution.py:332
  38.2 17.0 %collective-permute-start.11 = (bf16[2080,128]{1,0:T(8,128)(2,1)}, bf16[2080,128]{1,0:T(8,128)(2,1)S(1)}, u32[]{:S(2)}, u32[]{:S(2)}) collective-permute-start(bf16[2080,128]{1,0:T(8,128)(2,1)} %get-tuple-element.39), channel_id=1, source_target_pairs={{0,1},{1,2},{2,3},{3,0},{4,5},{5,6},{6,7},{7,4},{8,9},{9,10},{10,1... | collective-permute-start | bytes 1597448 | tf_op jit(solution)/shard_map/ppermute | solution.py:334
  38.5 16.7 %collective-permute-start.12 = (bf16[2080,128]{1,0:T(8,128)(2,1)}, bf16[2080,128]{1,0:T(8,128)(2,1)S(1)}, u32[]{:S(2)}, u32[]{:S(2)}) collective-permute-start(bf16[2080,128]{1,0:T(8,128)(2,1)} %get-tuple-element.40), channel_id=1, source_target_pairs={{0,3},{1,0},{2,1},{3,2},{4,7},{5,4},{6,5},{7,6},{8,11},{9,8},{10,9... | collective-permute-start | bytes 1597448 | tf_op jit(solution)/shard_map/ppermute | solution.py:335
  68.5 2.8 %collective-permute-start.13 = (bf16[2,16,32,128]{3,2,1,0:T(8,128)(2,1)S(1)}, bf16[2,16,32,128]{3,2,1,0:T(8,128)(2,1)S(1)}, u32[]{:S(2)}, u32[]{:S(2)}) collective-permute-start(bf16[2,16,32,128]{3,2,1,0:T(8,128)(2,1)S(1)} %get-tuple-element.41), channel_id=1, source_target_pairs={{0,4},{4,0},{8,12},{12,8},{16,20},{20,16},{24,28},{28,24},{1,5},{5... | collective-permute-start | bytes 786440 | tf_op jit(solution)/shard_map/ppermute | solution.py:301
